TPU v7x, 32 devices: a whole 2x2x4 slice. The times are simulated.
32 devices in a mesh: label: 16 (over z, y, x), query: 2 (over core).
Axes of the slice: x: 2, y: 2, z: 4, core: 2. Of those that a mesh axis runs over, the one named last changes fastest.
Arguments:
- queries: bfloat16 [384, 768], P('query'), may hold values from -6 to 6
- label_ids: int32 [384, 10], P('query'), may hold values from 0 to 1023, as said below
- label_text: bfloat16 [1024, 32, 768], P('label'), may hold values from -6 to 6
- up_weight: bfloat16 [768, 3072], P(None, 'query'), may hold values from -0.21875 to 0.21875
- down_weight: bfloat16 [768, 3072], P(None, 'query'), may hold values from -0.109375 to 0.109375
- free_vectors: float32 [1024, 768], P('label'), may hold values from -4 to 4
- moments: float32 [1024, 768], P('label'), may hold values from -0.06 to 0.06
- seconds: float32 [1024, 768], P('label'), may hold values from 1e-05 to 0.001
Outputs:
- free_new: float32 [1024, 768], P('label')
- moments_new: float32 [1024, 768], P('label')
- seconds_new: float32 [1024, 768], P('label')
- query_grad: float32 [384, 768], P('query')
- up_grad: float32 [768, 3072], P('label', 'query')
- down_grad: float32 [768, 3072], P('label', 'query')
Inputs may be any that keep to these rules, and one draw needn't show every extreme that they name: `label_ids`: the 10 ids of one query are distinct.
All inputs are finite; a program needn't handle non-finite values.
Results may differ from a plain program's by a relative error of at most 0.023.
Values sent between devices are 32-bit elements; how exact they have to be, the bound alone decides.
No kernel may reach another device: no remote copies, remote signals or barrier semaphores. Data moves between devices by JAX's collectives and lax.ppermute only.
A program may use at most 64 MiB of HBM per device.

v0:
```python
import jax
import jax.numpy as jnp
from jax import lax
from jax.sharding import PartitionSpec as P

beta_one = 0.9
beta_two = 0.999
adam_eps = 1e-08
learn_rate = 0.05
first_fix = 1.0 - 0.9**10
second_fix = 1.0 - 0.999**10


def gelu_tanh(values):
    return jax.nn.gelu(values, approximate=True)


def body(queries, label_ids, label_text, up_weight, down_weight, free_vectors, moments, seconds):
    label_rows, text_len, model_width = label_text.shape
    unit_cols = up_weight.shape[1]
    temper = 1.0 / jnp.sqrt(jnp.float32(model_width))
    text_rows = label_text.reshape(label_rows * text_len, model_width)
    preact = jnp.dot(text_rows, up_weight, preferred_element_type=jnp.float32)
    hidden = gelu_tanh(preact).astype(jnp.bfloat16)
    pooled_hidden = jnp.mean(
        hidden.reshape(label_rows, text_len, unit_cols), axis=1, dtype=jnp.float32
    )
    pooled_text = jnp.mean(label_text, axis=1, dtype=jnp.float32)
    encoded_part = jnp.einsum(
        "lf,df->ld", pooled_hidden, down_weight.astype(jnp.float32), precision=lax.Precision.HIGHEST
    )
    encoded = lax.psum(encoded_part, "query")
    label_vec = pooled_text + encoded + free_vectors
    label_bf = label_vec.astype(jnp.bfloat16)
    first_label = lax.axis_index("label") * label_rows
    local_ids = label_ids - first_label
    owners = (
        local_ids[:, :, None] == jnp.arange(label_rows, dtype=jnp.int32)[None, None, :]
    ).astype(jnp.float32)
    similar = jnp.einsum("id,jd->ij", queries, label_bf, preferred_element_type=jnp.float32)
    partial_value = jnp.einsum("ikj,ij->ik", owners, similar, precision=lax.Precision.HIGHEST)
    scores = lax.psum(partial_value, "label") * temper
    likely = jax.nn.softmax(scores, axis=-1)
    target = jnp.where(jnp.arange(scores.shape[1]) < 2, 0.5, 0.0).astype(jnp.float32)
    pair_coef = ((likely - target[None, :]) * temper).astype(jnp.bfloat16)
    spread = jnp.einsum(
        "ik,ikj->ij", pair_coef.astype(jnp.float32), owners, precision=lax.Precision.HIGHEST
    ).astype(jnp.bfloat16)
    query_terms = jnp.dot(spread, label_bf, preferred_element_type=jnp.float32)
    query_grad = lax.psum(query_terms, "label")
    grad_part = jnp.einsum("ij,id->jd", spread, queries, preferred_element_type=jnp.float32)
    count_part = jnp.sum(owners, axis=(0, 1))
    label_grad, counts = lax.psum((grad_part, count_part), "query")
    out_grad = label_grad.astype(jnp.bfloat16)
    hidden_grad = jnp.dot(out_grad, down_weight, preferred_element_type=jnp.float32) / text_len
    token_grad = jnp.broadcast_to(
        hidden_grad[:, None, :], (label_rows, text_len, unit_cols)
    ).reshape(label_rows * text_len, unit_cols)
    preact_grad = jax.vjp(gelu_tanh, preact)[1](token_grad)[0].astype(jnp.bfloat16)
    joined = lax.psum_scatter(
        jnp.concatenate(
            (
                lax.dot_general(
                    text_rows,
                    preact_grad,
                    (((0,), (0,)), ((), ())),
                    preferred_element_type=jnp.float32,
                ),
                jnp.einsum(
                    "ld,lf->df",
                    out_grad.astype(jnp.float32),
                    pooled_hidden,
                    precision=lax.Precision.HIGHEST,
                ),
            ),
            axis=1,
        ),
        "label",
        scatter_dimension=0,
        tiled=True,
    )
    up_part = joined[:, :unit_cols]
    down_part = joined[:, unit_cols:]
    touched = (counts > 0.5)[:, None]
    moment_step = beta_one * moments + (1.0 - beta_one) * label_grad
    second_step = beta_two * seconds + (1.0 - beta_two) * label_grad * label_grad
    update = (
        learn_rate * (moment_step / first_fix) / (jnp.sqrt(second_step / second_fix) + adam_eps)
    )
    free_new = jnp.where(touched, free_vectors - update, free_vectors)
    moments_new = jnp.where(touched, moment_step, moments)
    seconds_new = jnp.where(touched, second_step, seconds)
    return (free_new, moments_new, seconds_new, query_grad, up_part, down_part)


def solution(mesh):
    placed = (
        P("query", None),
        P("query", None),
        P("label", None, None),
        P(None, "query"),
        P(None, "query"),
        P("label", None),
        P("label", None),
        P("label", None),
    )
    return jax.shard_map(
        body,
        mesh=mesh,
        in_specs=placed,
        out_specs=(
            P("label", None),
            P("label", None),
            P("label", None),
            P("query", None),
            P("label", "query"),
            P("label", "query"),
        ),
        check_vma=False,
    )
```

profile of v0, /device:TPU:0, one launch (start us, length us, event | category | flops | bytes accessed | tf_op | source)
XLA Modules:
  0.0 473.7 jit_solution(6487693377887045940)
XLA Ops:
  7.2 0.0 copy-start
  7.2 0.0 all-reduce.4.cloned.1.call-start
  7.2 1.6 copy-done
  8.8 0.0 copy-start.1
  8.8 0.0 copy-start.10
  8.8 0.0 copy-start.5
  8.8 0.0 copy-start.4
  8.8 12.9 %convert_reduce_fusion = (f32[64,1536]{1,0:T(8,128)S(1)}, f32[2048,1536]{1,0:T(8,128)}) fusion(bf16[2048,768]{1,0:T(8,128)(2,1)} %bitcast.38, bf16[768,1536]{1,0:T(8,128)(2,1)S(1)} %copy-done), kind=kOutput, calls=%fused_computation.14 | convolution fusion | flops 4866342912 | bytes 18481152 | tf_op jit(solution)/shard_map/dot_general | solution.py:23
  21.7 0.0 copy-done.1
  21.7 2.9 fusion.13
  24.7 0.0 all-reduce.4.cloned.1.call-update
  24.7 0.0 all-reduce.6.cloned.1.call-start
  24.7 2.9 convert_reduce_fusion.1
  27.6 0.5 compare_select_fusion
  28.1 0.0 copy-done.10
  28.1 17.5 %all-reduce.4.cloned.1.call-done = f32[64,768]{1,0:T(8,128)} async-done(((f32[64,768]{1,0:T(8,128)}), f32[64,768]{1,0:T(8,128)}) %all-reduce.4.cloned.1.call-update) | async-done | bytes 196624 | tf_op jit(solution)/shard_map/psum | solution.py:32
  45.6 0.0 copy-done.5
  45.6 1.0 add_convert_fusion
  46.6 0.0 copy-done.4
  46.6 0.2 convolution_bitcast_fusion.1
  46.8 0.1 select_reduce_fusion.1
  46.9 77.0 %psum.37 = f32[192,10]{0,1:T(8,128)S(1)} all-reduce(f32[192,10]{0,1:T(8,128)S(1)} %select_reduce_fusion.1), channel_id=1, replica_groups=mesh['label'=16,'query'=2] {'label'}, use_global_device_ids=true, to_apply=%region_5.0 | all-reduce | flops 1920 | bytes 15360 | tf_op jit(solution)/shard_map/psum | solution.py:42
  124.0 0.7 fusion.27
  124.7 0.7 convert_reduce_fusion.2
  125.4 0.1 copy.34
  125.5 0.0 copy-start.6
  125.5 0.9 fusion.32
  126.4 0.0 all-reduce.6.cloned.1.call-update
  126.5 0.2 reduce-scatter.4.cloned.1.call-start
  126.7 13.9 %all-reduce.6.cloned.1.call-done = f32[64,768]{1,0:T(8,128)} async-done(((f32[64,768]{1,0:T(8,128)}), f32[64,768]{1,0:T(8,128)}) %all-reduce.6.cloned.1.call-update) | async-done | bytes 196624 | tf_op jit(solution)/shard_map/psum | solution.py:53
  140.6 0.0 copy-start.2
  140.6 2.4 convolution_multiply_fusion
  143.0 0.0 copy-done.6
  143.0 10.5 %fusion.6 = bf16[2048,1536]{1,0:T(8,128)(2,1)S(1)} fusion(f32[2048,1536]{1,0:T(8,128)} %get-tuple-element.32, f32[64,1536]{1,0:T(8,128)S(1)} %convolution_multiply_fusion), kind=kLoop, calls=%fused_computation.10 | loop fusion | flops 62914560 | bytes 19267584 | tf_op jit(solution)/shard_map/convert_element_type | solution.py:59
  153.5 0.0 copy-done.2
  153.5 0.0 copy-start.3
  153.5 6.8 %convolution_bitcast_fusion = f32[768,1536]{0,1:T(8,128)} fusion(bf16[2048,1536]{1,0:T(8,128)(2,1)S(1)} %fusion.6, bf16[2048,768]{1,0:T(8,128)(2,1)S(1)} %bitcast.39), kind=kOutput, calls=%fused_computation.18 | convolution fusion | flops 4831838208 | bytes 14155776 | tf_op jit(solution)/shard_map/dot_general | solution.py:63
  160.3 0.0 copy-done.3
  160.3 2.1 fusion.11
  162.4 6.6 %pad_maximum_fusion = f32[768,3072]{0,1:T(8,128)} fusion(f32[768,1536]{0,1:T(8,128)S(1)} %fusion.11, f32[768,1536]{0,1:T(8,128)} %convolution_bitcast_fusion), kind=kLoop, calls=%fused_computation.16 | loop fusion | flops 2359296 | bytes 18874368 | tf_op jit(solution)/shard_map/concatenate | solution.py:61
  169.0 0.0 copy-start.11
  169.0 0.0 copy-start.7
  169.0 0.0 copy-start.8
  169.0 0.0 copy-start.9
  169.0 9.7 %copy.36 = f32[768,3072]{1,0:T(8,128)} copy(f32[768,3072]{0,1:T(8,128)} %pad_maximum_fusion) | data formatting | bytes 18874368
  178.7 0.0 reduce-scatter.4.cloned.1.call-update
  178.7 0.0 all-reduce.8.cloned.1.call-start
  178.8 0.0 copy-done.11
  178.8 2.5 psum.35
  181.3 0.0 copy-done.7
  181.3 1.0 fusion.31
  182.3 0.0 all-reduce.8.cloned.1.call-update
  182.3 0.0 copy-done.8
  182.3 0.0 copy-done.9
  182.3 1.0 fusion.19
  183.3 166.9 %reduce-scatter.4.cloned.1.call-done = f32[48,3072]{1,0:T(8,128)} async-done(((f32[768,3072]{1,0:T(8,128)}), f32[48,3072]{1,0:T(8,128)}) %reduce-scatter.4.cloned.1.call-update) | async-done | bytes 589840
  350.2 1.9 fusion.30
  352.1 113.1 %all-reduce.8.cloned.1.call-done = f32[192,768]{1,0:T(8,128)} async-done(((f32[192,768]{1,0:T(8,128)}), f32[192,768]{1,0:T(8,128)}) %all-reduce.8.cloned.1.call-update) | async-done | bytes 589840 | tf_op jit(solution)/shard_map/psum | solution.py:50
  465.3 1.9 copy.46
  (4 shorter events, 0.1 us)
Async XLA Ops:
  7.2 1.7 copy-start
  7.2 38.4 %all-reduce.4.cloned.1.call-start = ((), (), s32[]{:S(2)}) async-start(), calls=%async_computation.1 | async-start | bytes 393216 | tf_op jit(solution)/shard_map/psum | solution.py:32
  8.8 12.9 %copy-start.1 = (bf16[768,1536]{1,0:T(8,128)(2,1)S(1)}, bf16[768,1536]{1,0:T(8,128)(2,1)}, u32[]{:S(2)}) copy-start(bf16[768,1536]{1,0:T(8,128)(2,1)} %param.12) | copy-start | bytes 7077892
  8.8 19.3 %copy-start.10 = (s32[192,10]{0,1:T(8,128)S(1)}, s32[192,10]{0,1:T(8,128)}, u32[]{:S(2)}) copy-start(s32[192,10]{0,1:T(8,128)} %param.9) | copy-start | bytes 23044
  8.8 36.8 %copy-start.5 = (f32[64,768]{1,0:T(8,128)S(1)}, f32[64,768]{1,0:T(8,128)}, u32[]{:S(2)}) copy-start(f32[64,768]{1,0:T(8,128)} %param.13) | copy-start | bytes 589828
  8.8 37.7 %copy-start.4 = (bf16[192,768]{1,0:T(8,128)(2,1)S(1)}, bf16[192,768]{1,0:T(8,128)(2,1)}, u32[]{:S(2)}) copy-start(bf16[192,768]{1,0:T(8,128)(2,1)} %param.8) | copy-start | bytes 884740
  24.7 115.9 %all-reduce.6.cloned.1.call-start = ((), (), s32[]{:S(2)}) async-start(), calls=%async_computation.2 | async-start | bytes 393216 | tf_op jit(solution)/shard_map/psum | solution.py:53
  125.5 17.5 %copy-start.6 = (bf16[192,64]{1,0:T(8,128)(2,1)}, bf16[192,64]{1,0:T(8,128)(2,1)S(1)}, u32[]{:S(2)}) copy-start(bf16[192,64]{1,0:T(8,128)(2,1)S(1)} %copy.34) | copy-start | bytes 73732
  126.5 223.8 %reduce-scatter.4.cloned.1.call-start = ((), (), s32[]{:S(2)}) async-start(), calls=%async_computation.4 | async-start | bytes 10027008
  140.6 12.9 %copy-start.2 = (bf16[64,32,768]{2,1,0:T(8,128)(2,1)S(1)}, bf16[64,32,768]{2,1,0:T(8,128)(2,1)}, u32[]{:S(2)}) copy-start(bf16[64,32,768]{2,1,0:T(8,128)(2,1)} %param.10) | copy-start | bytes 9437188
  153.5 6.8 %copy-start.3 = (f32[64,768]{1,0:T(8,128)S(1)}, f32[64,768]{1,0:T(8,128)}, u32[]{:S(2)}) copy-start(f32[64,768]{1,0:T(8,128)} %all-reduce.6.cloned.1.call-done) | copy-start | bytes 589828
  169.0 9.8 %copy-start.11 = (f32[64]{0:T(128)S(1)}, f32[64]{0:T(128)}, u32[]{:S(2)}) copy-start(f32[64]{0:T(128)} %get-tuple-element.24) | copy-start | bytes 772
  169.0 12.3 %copy-start.7 = (bf16[192,64]{1,0:T(8,128)(2,1)S(1)}, bf16[192,64]{1,0:T(8,128)(2,1)}, u32[]{:S(2)}) copy-start(bf16[192,64]{1,0:T(8,128)(2,1)} %copy-done.6) | copy-start | bytes 73732
  169.0 13.3 %copy-start.8 = (f32[64,768]{1,0:T(8,128)S(1)}, f32[64,768]{1,0:T(8,128)}, u32[]{:S(2)}) copy-start(f32[64,768]{1,0:T(8,128)} %param.15) | copy-start | bytes 589828
  169.0 13.3 %copy-start.9 = (f32[64,768]{1,0:T(8,128)S(1)}, f32[64,768]{1,0:T(8,128)}, u32[]{:S(2)}) copy-start(f32[64,768]{1,0:T(8,128)} %param.14) | copy-start | bytes 589828
  178.7 286.6 %all-reduce.8.cloned.1.call-start = ((), (), s32[]{:S(2)}) async-start(), calls=%async_computation.3 | async-start | bytes 1179648 | tf_op jit(solution)/shard_map/psum | solution.py:50
Sparse Core Ops, SparseCore 0:
  24.8 20.7 all-reduce.3
  126.6 13.9 all-reduce.5
  178.8 171.3 reduce-scatter.3
  356.9 108.3 all-reduce.7
where the time goes:
time: 474 us
  waiting for transfers between devices  311 us (66%)
  blocking collectives  79.5 us (17%)
  matrix products  29.3 us (6%)
  other arithmetic  24 us (5%)
  local copies, waits for them, and re-layouts  15.3 us (3%)
  between operations  13.9 us (3%)
    unnamed x5, waiting for transfers between devices  167 us
    psum x1, waiting for transfers between devices, body(): query_grad = lax.psum(query_terms, 'label')  113 us
    psum x1, blocking collectives, body(): scores = lax.psum(partial_value, 'label') * temper  77 us
    psum x1, waiting for transfers between devices, body(): encoded = lax.psum(encoded_part, 'query')  17.5 us
    psum x1, waiting for transfers between devices, body(): label_grad, counts = lax.psum((grad_part, count_part), 'query')  13.9 us
    unnamed x26, local copies, waits for them, and re-layouts  13.3 us
    dot_general x1, matrix products, body(): preact = jnp.dot(text_rows, up_weight, preferred_element_type=jnp.float32)  12.9 us
    convert_element_type x1, other arithmetic, body(): jax.vjp(gelu_tanh, preact)[1](token_grad)[0].astype(jnp.bfloat16)  10.5 us
  transfers between devices with their start and end apart: 4, of which 4 were waited for; matrix products, arithmetic and copies ran while one was open for 2% of the time, Pallas kernels for 0%

commit v1 on v0

v1 whole, which is shorter than its diff:
```python
import functools

import jax
import jax.numpy as jnp
from jax import lax
from jax.experimental import pallas as pl
from jax.sharding import PartitionSpec as P

beta_one = 0.9
beta_two = 0.999
adam_eps = 1e-08
learn_rate = 0.05
first_fix = 1.0 - 0.9**10
second_fix = 1.0 - 0.999**10

PLANE = 4
CHUNKS = 3


def gelu_tanh(values):
    return jax.nn.gelu(values, approximate=True)


def pair_swap(values, axis, count, bits):
    return lax.ppermute(values, axis, [(s, s ^ bits) for s in range(count)])


def query_gather(values, query_count):
    if query_count != 2:
        return lax.all_gather(values, "query")
    other = pair_swap(values, "query", 2, 1)
    first = lax.axis_index("query") == 0
    return jnp.stack((jnp.where(first, values, other), jnp.where(first, other, values)))


def query_sum(values, query_count):
    if query_count != 2:
        return lax.psum(values, "query")
    return values + pair_swap(values, "query", 2, 1)


def label_sum(values, label_count):
    values = values + sum(pair_swap(values, "label", label_count, b) for b in range(1, PLANE))
    return values + sum(
        pair_swap(values, "label", label_count, b) for b in range(PLANE, label_count, PLANE)
    )


def rounded(values):
    def kernel(wide_ref, narrow_ref):
        narrow_ref[...] = wide_ref[...].astype(jnp.bfloat16)

    return pl.pallas_call(
        kernel, out_shape=jax.ShapeDtypeStruct(values.shape, jnp.bfloat16)
    )(values)


def split_bf16(values):
    high = values.astype(jnp.bfloat16)
    low = (values - high.astype(jnp.float32)).astype(jnp.bfloat16)
    return high, low


def half_exchange(blocks, axis, bit, label_count):
    mine = (lax.axis_index("label") // bit) % 2
    keep = lax.dynamic_index_in_dim(blocks, mine, axis, keepdims=False)
    give = lax.dynamic_index_in_dim(blocks, 1 - mine, axis, keepdims=False)
    return keep + pair_swap(give, "label", label_count, bit)


def scatter_sum(partial, label_count):
    rows, cols = partial.shape
    planes = label_count // PLANE
    own = rows // label_count
    half = cols // 2
    blocks = partial.reshape(planes, 2, 2, own, cols)
    left = half_exchange(blocks[..., :half], 2, 1, label_count)
    right = half_exchange(blocks[..., half:], 1, 2, label_count)
    left = half_exchange(left, 1, 2, label_count)
    right = half_exchange(right, 1, 1, label_count)
    joined = jnp.concatenate((left, right), axis=-1)
    plane = lax.axis_index("label") // PLANE
    total = lax.dynamic_index_in_dim(joined, plane, 0, keepdims=False)
    for other in range(1, planes):
        give = lax.dynamic_index_in_dim(joined, plane ^ other, 0, keepdims=False)
        total = total + pair_swap(give, "label", label_count, other * PLANE)
    return total


def gather_labels(values, label_count):
    planes = label_count // PLANE
    rows, cols = values.shape
    whole = jnp.stack(
        [values] + [pair_swap(values, "label", label_count, b * PLANE) for b in range(1, planes)]
    )
    half = cols // 2
    left, right = whole[..., :half], whole[..., half:]
    left = jnp.stack((left, pair_swap(left, "label", label_count, 2)), axis=1)
    right = jnp.stack((right, pair_swap(right, "label", label_count, 1)), axis=1)
    left = jnp.stack((left, pair_swap(left, "label", label_count, 1)), axis=2)
    right = jnp.stack((right, pair_swap(right, "label", label_count, 2)), axis=1)
    return jnp.concatenate((left, right), axis=-1).reshape(label_count, rows, cols)


def body(
    label_count,
    query_count,
    queries,
    label_ids,
    label_text,
    up_weight,
    down_weight,
    free_vectors,
    moments,
    seconds,
):
    label_rows, text_len, model_width = label_text.shape
    query_rows = queries.shape[0]
    unit_cols = up_weight.shape[1]
    labels = label_count * label_rows
    temper = 1.0 / jnp.sqrt(jnp.float32(model_width))
    shard = lax.axis_index("label")
    core = lax.axis_index("query")

    every_query = query_gather(queries.astype(jnp.float32), query_count)
    every_query = rounded(every_query.reshape(query_count * query_rows, model_width))
    ids = query_gather(label_ids.T, query_count)
    ids = jnp.moveaxis(ids, 0, 1).reshape(ids.shape[1], query_count * query_rows)

    text_rows = label_text.reshape(label_rows * text_len, model_width)
    preact = jnp.dot(text_rows, up_weight, preferred_element_type=jnp.float32)
    hidden = gelu_tanh(preact).astype(jnp.bfloat16)
    pooled_hidden = jnp.mean(
        hidden.reshape(label_rows, text_len, unit_cols), axis=1, dtype=jnp.float32
    )
    pooled_text = jnp.mean(label_text, axis=1, dtype=jnp.float32)
    pooled_high, pooled_low = split_bf16(pooled_hidden)
    encoded_two = lax.dot_general(
        jnp.concatenate((pooled_high, pooled_low)),
        down_weight,
        (((1,), (1,)), ((), ())),
        preferred_element_type=jnp.float32,
    )
    encoded = query_sum(encoded_two[:label_rows] + encoded_two[label_rows:], query_count)
    label_vec = pooled_text + encoded + free_vectors
    label_bf = label_vec.astype(jnp.bfloat16)

    local = ids - shard * label_rows
    owned = local[:, None, :] == jnp.arange(label_rows, dtype=jnp.int32)[None, :, None]
    similar = lax.dot_general(
        label_bf, every_query, (((1,), (1,)), ((), ())), preferred_element_type=jnp.float32
    )
    partial = jnp.sum(jnp.where(owned, similar[None], 0.0), axis=1)
    scores = label_sum(partial, label_count) * temper
    likely = jax.nn.softmax(scores, axis=0)
    target = jnp.where(jnp.arange(scores.shape[0]) < 2, 0.5, 0.0).astype(jnp.float32)
    pair_coef = ((likely - target[:, None]) * temper).astype(jnp.bfloat16)
    coef = pair_coef.astype(jnp.float32)

    spread = jnp.sum(jnp.where(owned, coef[:, None, :], 0.0), axis=0).astype(jnp.bfloat16)
    touched = jnp.any(owned, axis=(0, 2))[:, None]
    label_grad = jnp.dot(spread, every_query, preferred_element_type=jnp.float32)
    out_grad = label_grad.astype(jnp.bfloat16)
    hidden_grad = jnp.dot(out_grad, down_weight, preferred_element_type=jnp.float32) / text_len

    up_parts = []
    chunk = unit_cols // CHUNKS
    for part in range(CHUNKS):
        cols = slice(part * chunk, (part + 1) * chunk)
        preact = jnp.dot(text_rows, up_weight[:, cols], preferred_element_type=jnp.float32)
        token_grad = jnp.broadcast_to(
            hidden_grad[:, None, cols], (label_rows, text_len, chunk)
        ).reshape(label_rows * text_len, chunk)
        preact_grad = jax.vjp(gelu_tanh, preact)[1](token_grad)[0].astype(jnp.bfloat16)
        up_part = lax.dot_general(
            text_rows, preact_grad, (((0,), (0,)), ((), ())), preferred_element_type=jnp.float32
        )
        up_parts.append(scatter_sum(up_part, label_count))
    up_grad = jnp.concatenate(up_parts, axis=1)

    share = label_rows // query_count
    own_share = lax.dynamic_slice_in_dim(label_bf.astype(jnp.float32), core * share, share)
    gathered = gather_labels(own_share, label_count).reshape(label_count * share, model_width)
    position = ids // label_rows ^ shard
    within = ids % label_rows - core * share
    place = jnp.where((within >= 0) & (within < share), position * share + within, -1)
    spread_share = jnp.sum(
        jnp.where(
            place[:, None, :] == jnp.arange(label_count * share, dtype=jnp.int32)[None, :, None],
            coef[:, None, :],
            0.0,
        ),
        axis=0,
    ).astype(jnp.bfloat16)
    query_terms = lax.dot_general(
        spread_share,
        rounded(gathered),
        (((0,), (0,)), ((), ())),
        preferred_element_type=jnp.float32,
    ).reshape(query_count, query_rows, model_width)
    if query_count == 2:
        query_grad = lax.dynamic_index_in_dim(query_terms, core, keepdims=False) + pair_swap(
            lax.dynamic_index_in_dim(query_terms, 1 - core, keepdims=False), "query", 2, 1
        )
    else:
        query_grad = lax.dynamic_index_in_dim(
            lax.psum(query_terms, "query"), core, keepdims=False
        )

    unit_share = unit_cols // label_count
    pooled_all = lax.all_to_all(
        pooled_hidden.reshape(label_rows, label_count, unit_share).swapaxes(0, 1), "label", 0, 0
    ).reshape(labels, unit_share)
    spread_all = jnp.sum(
        jnp.where(
            ids[:, None, :] == jnp.arange(labels, dtype=jnp.int32)[None, :, None],
            coef[:, None, :],
            0.0,
        ),
        axis=0,
    ).astype(jnp.bfloat16)
    out_grad_all = jnp.dot(spread_all, every_query, preferred_element_type=jnp.float32).astype(
        jnp.bfloat16
    )
    all_high, all_low = split_bf16(pooled_all)
    down_two = lax.dot_general(
        out_grad_all,
        jnp.concatenate((all_high, all_low), axis=1),
        (((0,), (0,)), ((), ())),
        preferred_element_type=jnp.float32,
    )
    down_cols = down_two[:, :unit_share] + down_two[:, unit_share:]
    down_grad = lax.all_to_all(
        down_cols.reshape(label_count, model_width // label_count, unit_share), "label", 0, 0
    )
    down_grad = down_grad.swapaxes(0, 1).reshape(model_width // label_count, unit_cols)

    moment_step = beta_one * moments + (1.0 - beta_one) * label_grad
    second_step = beta_two * seconds + (1.0 - beta_two) * label_grad * label_grad
    update = (
        learn_rate * (moment_step / first_fix) / (jnp.sqrt(second_step / second_fix) + adam_eps)
    )
    free_new = jnp.where(touched, free_vectors - update, free_vectors)
    moments_new = jnp.where(touched, moment_step, moments)
    seconds_new = jnp.where(touched, second_step, seconds)
    return (free_new, moments_new, seconds_new, query_grad, up_grad, down_grad)


def solution(mesh):
    placed = (
        P("query", None),
        P("query", None),
        P("label", None, None),
        P(None, "query"),
        P(None, "query"),
        P("label", None),
        P("label", None),
        P("label", None),
    )
    return jax.shard_map(
        functools.partial(body, mesh.shape["label"], mesh.shape["query"]),
        mesh=mesh,
        in_specs=placed,
        out_specs=(
            P("label", None),
            P("label", None),
            P("label", None),
            P("query", None),
            P("label", "query"),
            P("label", "query"),
        ),
        check_vma=False,
    )
```

time: 474 us -> 193 us (0.41)
  waiting for transfers between devices: 311 us -> 21 us
  blocking collectives: 79.5 us -> 0 us
  starting transfers between devices: 0.34 us -> 58.9 us
  matrix products: 29.3 us -> 46 us
  between operations: 13.9 us -> 1.4 us
  local copies, waits for them, and re-layouts: 15.3 us -> 27 us
  other arithmetic: 24 us -> 32.5 us
    unnamed x5 -> x0, waiting for transfers between devices: 167 us -> none
    psum x3 -> x0, waiting for transfers between devices: 144 us -> none  [the longest x1 113 us: body(): query_grad = lax.psum(query_terms, 'label')]
    psum x2 -> x0, blocking collectives: 79.5 us -> none  [the longest x1 77 us: body(): scores = lax.psum(partial_value, 'label') * temper]
    ppermute x0 -> x38, starting transfers between devices: none -> 46.5 us  [pair_swap(): return lax.ppermute(values, axis, [(s, s ^ bits) for s in range(count)])]
    ppermute x0 -> x38, waiting for transfers between devices: none -> 21 us  [pair_swap(): return lax.ppermute(values, axis, [(s, s ^ bits) for s in range(count)])]
    dot_general x5 -> x8, matrix products: 7.16 us -> 27.5 us  [the longest x3 16.5 us: body(): jnp.dot(text_rows, up_weight[:, cols], preferred_element_type=jnp.float32)]
    all_to_all x0 -> x2, starting transfers between devices: none -> 12.4 us  [the longest x1 7.95 us: body(): lax.all_to_all(pooled_hidden.reshape(label_rows, label_count, unit_share)...]
    add x0 -> x19, other arithmetic: none -> 12.1 us  [the longest x12 5.58 us: half_exchange(): return keep + pair_swap(give, 'label', label_count, bit)]
  transfers between devices with their start and end apart: 4 -> 40, of which waited for: 4 -> 8; matrix products, arithmetic and copies ran while one was open for 2% -> 53% of each run, Pallas kernels for 0% -> 2%
where the time goes in v1:
time: 193 us; the launch traced here: 191 us
  starting transfers between devices  58.9 us (31%)
  matrix products  46 us (24%)
  other arithmetic  32.5 us (17%)
  local copies, waits for them, and re-layouts  27 us (14%)
  waiting for transfers between devices  21 us (11%)
  Pallas kernels  4.64 us (2%)
    ppermute x38, starting transfers between devices, pair_swap(): return lax.ppermute(values, axis, [(s, s ^ bits) for s in range(count)])  46.5 us
    ppermute x38, waiting for transfers between devices, pair_swap(): return lax.ppermute(values, axis, [(s, s ^ bits) for s in range(count)])  21 us
    dot_general x3, matrix products, body(): jnp.dot(text_rows, up_weight[:, cols], preferred_element_type=jnp.float32)  16.5 us
    dot_general x1, matrix products, body(): preact = jnp.dot(text_rows, up_weight, preferred_element_type=jnp.float32)  10 us
    dot_general x3, matrix products, body(): lax.dot_general(text_rows, preact_grad, (((0,), (0,)), ((), ())), preferr...  7.95 us
    all_to_all x1, starting transfers between devices, body(): lax.all_to_all(pooled_hidden.reshape(label_rows, label_count, unit_share)...  7.95 us
    dot_general x3, local copies, waits for them, and re-layouts, body(): lax.dot_general(text_rows, preact_grad, (((0,), (0,)), ((), ())), preferr...  6.55 us
    add x12, other arithmetic, half_exchange(): return keep + pair_swap(give, 'label', label_count, bit)  5.58 us
  transfers between devices with their start and end apart: 40, of which 8 were waited for; matrix products, arithmetic and copies ran while one was open for 53% of the time, Pallas kernels for 2%

profile of v1, /device:TPU:0, one launch (start us, length us, event | category | flops | bytes accessed | tf_op | source)
XLA Modules:
  0.0 191.4 jit_solution(15288454770133880084)
XLA Ops:
  1.2 10.0 %convert_reduce_fusion = f32[64,1536]{1,0:T(8,128)S(1)} fusion(bf16[2048,768]{1,0:T(8,128)(2,1)} %bitcast.214, bf16[768,1536]{1,0:T(8,128)(2,1)} %param.11), kind=kOutput, calls=%fused_computation.11 | convolution fusion | flops 4866342912 | bytes 5898240 | tf_op jit(solution)/shard_map/dot_general | solution.py:131
  13.1 7.9 %all-to-all-start = ((f32[16,64,96]{2,1,0:T(8,128)}), f32[16,64,96]{2,1,0:T(8,128)}, u32[]{:S(2)}, u32[]{:S(2)}) async-start(f32[16,64,96]{2,1,0:T(8,128)} %bitcast.213), calls=%async_computation | async-start | bytes 1048576 | tf_op jit(solution)/shard_map/all_to_all | solution.py:211
  21.1 1.9 %fusion.52 = f32[128,768]{1,0:T(8,128)S(1)} fusion(bf16[768,1536]{1,0:T(8,128)(2,1)S(1)} %copy-done, bf16[64,1536]{1,0:T(8,128)(2,1)} %get-tuple-element.23, bf16[64,1536]{1,0:T(8,128)(2,1)S(1)} %get-tuple-element.22), kind=kOutput, calls=%fused_computation.111 | convolution fusion | flops 302776320 | bytes 3145728 | tf_op jit(solution)/shard_map/dot_general | solution.py:138
  27.0 1.1 add_convert_fusion
  28.1 1.9 %collective-permute-start.9 = (f32[32,768]{1,0:T(8,128)S(1)}, f32[32,768]{1,0:T(8,128)S(1)}, u32[]{:S(2)}, u32[]{:S(2)}) collective-permute-start(f32[32,768]{1,0:T(8,128)S(1)} %get-tuple-element.45), channel_id=1, source_target_pairs={{0,8},{2,10},{4,12},{6,14},{8,0},{10,2},{12,4},{14,6},{16,24},{18,... | collective-permute-start | bytes 294920 | tf_op jit(solution)/shard_map/ppermute | solution.py:25
  30.0 2.4 %collective-permute-start.10 = (f32[32,768]{1,0:T(8,128)S(1)}, f32[32,768]{1,0:T(8,128)S(1)}, u32[]{:S(2)}, u32[]{:S(2)}) collective-permute-start(f32[32,768]{1,0:T(8,128)S(1)} %get-tuple-element.45), channel_id=1, source_target_pairs={{0,16},{2,18},{4,20},{6,22},{8,24},{10,26},{12,28},{14,30},{16,0},... | collective-permute-start | bytes 294920 | tf_op jit(solution)/shard_map/ppermute | solution.py:25
  32.8 1.4 collective-permute-done.9
  34.2 8.9 %collective-permute-done.10 = f32[32,768]{1,0:T(8,128)S(1)} collective-permute-done((f32[32,768]{1,0:T(8,128)S(1)}, f32[32,768]{1,0:T(8,128)S(1)}, u32[]{:S(2)}, u32[]{:S(2)}) %collective-permute-start.10) | collective-permute-done | bytes 98336 | tf_op jit(solution)/shard_map/ppermute | solution.py:25
  43.9 1.5 collective-permute-start.14
  45.4 1.5 collective-permute-start.12
  46.8 1.1 select_bitcast_fusion.1
  48.0 1.1 pad_maximum_fusion
  49.1 2.2 %shard_map.127 = bf16[384,768]{1,0:T(8,128)(2,1)} custom-call(f32[384,768]{1,0:T(8,128)} %bitcast.225), custom_call_target="tpu_custom_call" | custom-call | tf_op jit(solution)/shard_map/pallas_call | solution.py:53
  51.3 1.4 fusion.117
  53.5 1.5 collective-permute-start.4
  54.9 1.5 collective-permute-start.3
  56.4 1.8 fusion.110
  58.8 1.4 collective-permute-start.8
  60.2 1.9 collective-permute-start.7
  62.1 1.1 collective-permute-start.6
  63.2 1.9 fusion.111
  65.1 1.5 collective-permute-start.13
  66.9 2.1 %fusion.60 = (f32[64,768]{1,0:T(8,128)}, f32[64,768]{1,0:T(8,128)}, f32[64,768]{1,0:T(8,128)}, bf16[64,768]{1,0:T(8,128)(2,1)S(1)}) fusion(f32[64,768]{1,0:T(8,128)} %param.15, pred[64]{0:T(512)(128)(4,1)S(1)} %fusion.39, f32[64,768]{1,0:T(8,128)S(1)} %copy-done.30, f32[64,768]{1,0:T(8,128)} %param.14, bf16[64,384]{1,0:T(8,128)(2,1)S(1)} %select_reduce_fusion.2, ...), kind=kOutput, calls=%fused_computation.155 | convolution fusion | flops 38535168 | bytes 1916992 | tf_op jit(solution)/shard_map/dot_general | solution.py:162
  70.3 5.4 %fusion.14 = bf16[2048,512]{1,0:T(8,128)(2,1)S(1)} fusion(f32[64,512]{1,0:T(8,128)S(1)} %get-tuple-element.27, bf16[2048,768]{1,0:T(8,128)(2,1)S(1)} %bitcast.215, bf16[768,1536]{1,0:T(8,128)(2,1)} %param.11), kind=kOutput, calls=%fused_computation.33 | convolution fusion | flops 1631584256 | bytes 6160384 | tf_op jit(solution)/shard_map/dot_general | solution.py:170
  75.7 1.9 convolution_bitcast_fusion.2
  77.6 1.6 copy.49
  79.2 1.6 fusion.113
  83.4 1.2 collective-permute-start.19
  84.6 5.7 %fusion.28 = bf16[2048,512]{1,0:T(8,128)(2,1)S(1)} fusion(f32[64,512]{1,0:T(8,128)S(1)} %copy-done.25, bf16[2048,768]{1,0:T(8,128)(2,1)S(1)} %bitcast.217, bf16[768,1536]{1,0:T(8,128)(2,1)} %param.11), kind=kOutput, calls=%fused_computation.47 | convolution fusion | flops 1631584256 | bytes 6160384 | tf_op jit(solution)/shard_map/dot_general | solution.py:170
  90.3 3.0 %convolution_bitcast_fusion = f32[768,512]{0,1:T(8,128)} fusion(bf16[2048,512]{1,0:T(8,128)(2,1)S(1)} %fusion.28, bf16[2048,768]{1,0:T(8,128)(2,1)S(1)} %bitcast.218), kind=kOutput, calls=%fused_computation.61 | convolution fusion | flops 1610612736 | bytes 6815744 | tf_op jit(solution)/shard_map/dot_general | solution.py:175
  93.3 3.0 %copy.51 = f32[768,512]{1,0:T(8,128)} copy(f32[768,512]{0,1:T(8,128)} %convolution_bitcast_fusion) | data formatting | bytes 3145728 | tf_op jit(solution)/shard_map/dot_general | solution.py:175
  96.4 1.5 fusion.115
  101.2 5.4 %fusion.21 = bf16[2048,512]{1,0:T(8,128)(2,1)S(1)} fusion(f32[64,512]{1,0:T(8,128)S(1)} %copy-done.24, bf16[2048,768]{1,0:T(8,128)(2,1)S(1)} %bitcast.219, bf16[768,1536]{1,0:T(8,128)(2,1)} %param.11), kind=kOutput, calls=%fused_computation.40 | convolution fusion | flops 1631584256 | bytes 6160384 | tf_op jit(solution)/shard_map/dot_general | solution.py:170
  106.6 3.0 %convolution_bitcast_fusion.1 = f32[768,512]{0,1:T(8,128)} fusion(bf16[2048,512]{1,0:T(8,128)(2,1)S(1)} %fusion.21, bf16[2048,768]{1,0:T(8,128)(2,1)S(1)} %bitcast.220), kind=kOutput, calls=%fused_computation.62 | convolution fusion | flops 1610612736 | bytes 6815744 | tf_op jit(solution)/shard_map/dot_general | solution.py:175
  109.7 1.9 copy.50
  114.7 3.2 %select_reduce_fusion = bf16[1024,384]{1,0:T(8,128)(2,1)} fusion(f32[10,384]{1,0:T(8,128)S(1)} %copy-done.27, s32[10,384]{1,0:T(8,128)S(1)} %copy-done.29), kind=kLoop, calls=%fused_computation.1 | loop fusion | flops 11403264 | bytes 817152 | tf_op jit(solution)/shard_map/reduce_sum | solution.py:214
  117.8 1.1 fusion.51
  118.9 3.7 %fusion.38 = f32[768,192]{0,1:T(8,128)} fusion(bf16[384,768]{1,0:T(8,128)(2,1)S(1)} %copy-done.15, bf16[1024,384]{1,0:T(8,128)(2,1)} %select_reduce_fusion, bf16[1024,96]{1,0:T(8,128)(2,1)S(1)} %get-tuple-element.6, bf16[1024,96]{1,0:T(8,128)(2,1)S(1)} %get-tuple-element.7), kind=kOutput, calls=%fused_computation.60 | convolution fusion | flops 907542528 | bytes 2359296 | tf_op jit(solution)/shard_map/dot_general | solution.py:226
  122.6 1.1 slice_add_fusion
  124.7 4.5 %all-to-all-start.1 = ((f32[16,48,96]{2,1,0:T(8,128)}), f32[16,48,96]{2,1,0:T(8,128)}, u32[]{:S(2)}, u32[]{:S(2)}) async-start(f32[16,48,96]{2,1,0:T(8,128)} %bitcast.73), calls=%async_computation.1 | async-start | bytes 786432 | tf_op jit(solution)/shard_map/all_to_all | solution.py:233
  129.2 1.6 collective-permute-start.33
  130.7 1.5 collective-permute-start.24
  132.2 1.2 maximum_maximum_fusion
  133.5 1.4 copy.48
  134.8 2.5 %shard_map.128 = bf16[512,768]{1,0:T(8,128)(2,1)} custom-call(f32[512,768]{1,0:T(8,128)} %bitcast.224), custom_call_target="tpu_custom_call" | custom-call | tf_op jit(solution)/shard_map/pallas_call | solution.py:53
  137.3 1.7 fusion.118
  140.4 1.2 bitcast_add_fusion.6
  141.7 1.1 bitcast_add_fusion.5
  142.8 1.5 collective-permute-start.18
  148.8 1.6 collective-permute-done.26
  150.5 1.2 collective-permute-start.34
  151.8 2.9 %collective-permute-done.18 = f32[4,48,256]{2,1,0:T(8,128)S(1)} collective-permute-done((f32[4,48,256]{2,1,0:T(8,128)S(1)}, f32[4,48,256]{2,1,0:T(8,128)S(1)}, u32[]{:S(2)}, u32[]{:S(2)}) %collective-permute-start.18) | collective-permute-done | bytes 196640 | tf_op jit(solution)/shard_map/ppermute | solution.py:25
  155.0 2.5 %collective-permute-start.27 = (f32[4,48,256]{2,1,0:T(8,128)S(1)}, f32[4,48,256]{2,1,0:T(8,128)S(1)}, u32[]{:S(2)}, u32[]{:S(2)}) collective-permute-start(f32[4,48,256]{2,1,0:T(8,128)S(1)} %dynamic-slice_bitcast_fusion.9), channel_id=1, source_target_pairs={{0,2},{2,0},{4,6},{6,4},{8,10},{10,8},{12,14},{14,12},{16,18},{18,... | collective-permute-start | bytes 589832 | tf_op jit(solution)/shard_map/ppermute | solution.py:25
  158.8 1.1 collective-permute-start.21
  159.9 2.4 %collective-permute-start.22 = (f32[48,512]{1,0:T(8,128)}, f32[48,512]{1,0:T(8,128)}, u32[]{:S(2)}, u32[]{:S(2)}) collective-permute-start(f32[48,512]{1,0:T(8,128)} %get-tuple-element.25), channel_id=1, source_target_pairs={{0,16},{2,18},{4,20},{6,22},{8,24},{10,26},{12,28},{14,30},{16,0},... | collective-permute-start | bytes 294920 | tf_op jit(solution)/shard_map/ppermute | solution.py:25
  166.2 2.0 %copy.54 = f32[48,16,96]{2,1,0:T(8,128)} copy(f32[48,16,96]{2,0,1:T(8,128)} %bitcast.74) | data formatting | bytes 589824 | tf_op jit(solution)/shard_map/transpose | solution.py:236
  168.2 1.9 reshape.145
  170.1 2.9 %collective-permute-start.36 = (f32[48,512]{1,0:T(8,128)}, f32[48,512]{1,0:T(8,128)S(1)}, u32[]{:S(2)}, u32[]{:S(2)}) collective-permute-start(f32[48,512]{1,0:T(8,128)} %get-tuple-element.34), channel_id=1, source_target_pairs={{0,16},{2,18},{4,20},{6,22},{8,24},{10,26},{12,28},{14,30},{16,0},... | collective-permute-start | bytes 294920 | tf_op jit(solution)/shard_map/ppermute | solution.py:25
  175.0 3.5 %collective-permute-start.29 = (f32[48,512]{1,0:T(8,128)}, f32[48,512]{1,0:T(8,128)S(1)}, u32[]{:S(2)}, u32[]{:S(2)}) collective-permute-start(f32[48,512]{1,0:T(8,128)} %get-tuple-element.31), channel_id=1, source_target_pairs={{0,16},{2,18},{4,20},{6,22},{8,24},{10,26},{12,28},{14,30},{16,0},... | collective-permute-start | bytes 294920 | tf_op jit(solution)/shard_map/ppermute | solution.py:25
  178.5 2.6 %collective-permute-done.36 = f32[48,512]{1,0:T(8,128)S(1)} collective-permute-done((f32[48,512]{1,0:T(8,128)}, f32[48,512]{1,0:T(8,128)S(1)}, u32[]{:S(2)}, u32[]{:S(2)}) %collective-permute-start.36) | collective-permute-done | bytes 98336 | tf_op jit(solution)/shard_map/ppermute | solution.py:25
  181.1 2.9 %collective-permute-start.30 = (f32[48,512]{1,0:T(8,128)}, f32[48,512]{1,0:T(8,128)S(1)}, u32[]{:S(2)}, u32[]{:S(2)}) collective-permute-start(f32[48,512]{1,0:T(8,128)} %get-tuple-element.32), channel_id=1, source_target_pairs={{0,24},{2,26},{4,28},{6,30},{8,16},{10,18},{12,20},{14,22},{16,8},... | collective-permute-start | bytes 294920 | tf_op jit(solution)/shard_map/ppermute | solution.py:25
  184.9 1.4 collective-permute-done.29
  186.3 1.6 collective-permute-done.30
  189.4 1.9 %bitcast_add_fusion = f32[192,768]{1,0:T(8,128)} fusion(f32[192,768]{1,0:T(8,128)} %collective-permute-done.16, f32[2,192,768]{2,1,0:T(8,128)S(1)} %bitcast.227, s32[]{:T(128)S(6)} %select_n.219), kind=kLoop, calls=%fused_computation.100 | loop fusion | flops 147456 | bytes 1769476 | tf_op jit(solution)/shard_map/add | solution.py:202
  (173 shorter events, 36.1 us)
Async XLA Ops:
  0.6 20.4 %copy-start = (bf16[768,1536]{1,0:T(8,128)(2,1)S(1)}, bf16[768,1536]{1,0:T(8,128)(2,1)}, u32[]{:S(2)}) copy-start(bf16[768,1536]{1,0:T(8,128)(2,1)} %param.12) | copy-start | bytes 7077892
  0.6 25.6 %collective-permute-start = (s32[10,192]{1,0:T(8,128)}, s32[10,192]{1,0:T(8,128)S(1)}, u32[]{:S(2)}, u32[]{:S(2)}) collective-permute-start(s32[10,192]{1,0:T(8,128)} %bitcast.231), channel_id=1, source_target_pairs={{0,1},{1,0},{2,3},{3,2},{4,5},{5,4},{6,7},{7,6},{8,9},{9,8},{10,11... | collective-permute-start | bytes 23048 | tf_op jit(solution)/shard_map/ppermute | solution.py:25
  12.1 11.7 %copy-start.23 = (bf16[192,768]{1,0:T(8,128)(2,1)S(1)}, bf16[192,768]{1,0:T(8,128)(2,1)}, u32[]{:S(2)}) copy-start(bf16[192,768]{1,0:T(8,128)(2,1)} %param.8) | copy-start | bytes 884740
  13.1 104.7 %all-to-all-start = ((f32[16,64,96]{2,1,0:T(8,128)}), f32[16,64,96]{2,1,0:T(8,128)}, u32[]{:S(2)}, u32[]{:S(2)}) async-start(f32[16,64,96]{2,1,0:T(8,128)} %bitcast.213), calls=%async_computation | async-start | bytes 1048576 | tf_op jit(solution)/shard_map/all_to_all | solution.py:211
  21.1 4.1 %copy-start.2 = (bf16[64,32,768]{2,1,0:T(8,128)(2,1)S(1)}, bf16[64,32,768]{2,1,0:T(8,128)(2,1)}, u32[]{:S(2)}) copy-start(bf16[64,32,768]{2,1,0:T(8,128)(2,1)} %param.10) | copy-start | bytes 9437188
  23.0 3.2 %copy-start.32 = (s32[192,10]{0,1:T(8,128)S(1)}, s32[192,10]{0,1:T(8,128)}, u32[]{:S(2)}) copy-start(s32[192,10]{0,1:T(8,128)} %param.9) | copy-start | bytes 23044
  23.7 3.3 %collective-permute-start.1 = (f32[64,768]{1,0:T(8,128)}, f32[64,768]{1,0:T(8,128)}, u32[]{:S(2)}, u32[]{:S(2)}) collective-permute-start(f32[64,768]{1,0:T(8,128)} %slice_add_fusion.1), channel_id=1, source_target_pairs={{0,1},{1,0},{2,3},{3,2},{4,5},{5,4},{6,7},{7,6},{8,9},{9,8},{10,11... | collective-permute-start | bytes 589832 | tf_op jit(solution)/shard_map/ppermute | solution.py:25
  24.7 22.2 %collective-permute-start.2 = (f32[192,768]{1,0:T(8,128)}, f32[192,768]{1,0:T(8,128)}, u32[]{:S(2)}, u32[]{:S(2)}) collective-permute-start(f32[192,768]{1,0:T(8,128)} %convert_element_type.77), channel_id=1, source_target_pairs={{0,1},{1,0},{2,3},{3,2},{4,5},{5,4},{6,7},{7,6},{8,9},{9,8},{10,11... | collective-permute-start | bytes 1769480 | tf_op jit(solution)/shard_map/ppermute | solution.py:25
  28.1 6.1 %collective-permute-start.9 = (f32[32,768]{1,0:T(8,128)S(1)}, f32[32,768]{1,0:T(8,128)S(1)}, u32[]{:S(2)}, u32[]{:S(2)}) collective-permute-start(f32[32,768]{1,0:T(8,128)S(1)} %get-tuple-element.45), channel_id=1, source_target_pairs={{0,8},{2,10},{4,12},{6,14},{8,0},{10,2},{12,4},{14,6},{16,24},{18,... | collective-permute-start | bytes 294920 | tf_op jit(solution)/shard_map/ppermute | solution.py:25
  30.0 13.0 %collective-permute-start.10 = (f32[32,768]{1,0:T(8,128)S(1)}, f32[32,768]{1,0:T(8,128)S(1)}, u32[]{:S(2)}, u32[]{:S(2)}) collective-permute-start(f32[32,768]{1,0:T(8,128)S(1)} %get-tuple-element.45), channel_id=1, source_target_pairs={{0,16},{2,18},{4,20},{6,22},{8,24},{10,26},{12,28},{14,30},{16,0},... | collective-permute-start | bytes 294920 | tf_op jit(solution)/shard_map/ppermute | solution.py:25
  32.4 10.7 %collective-permute-start.11 = (f32[32,768]{1,0:T(8,128)S(1)}, f32[32,768]{1,0:T(8,128)S(1)}, u32[]{:S(2)}, u32[]{:S(2)}) collective-permute-start(f32[32,768]{1,0:T(8,128)S(1)} %get-tuple-element.45), channel_id=1, source_target_pairs={{0,24},{2,26},{4,28},{6,30},{8,16},{10,18},{12,20},{14,22},{16,8},... | collective-permute-start | bytes 294920 | tf_op jit(solution)/shard_map/ppermute | solution.py:25
  43.9 12.5 %collective-permute-start.14 = (f32[4,32,384]{2,1,0:T(8,128)S(1)}, f32[4,32,384]{2,1,0:T(8,128)}, u32[]{:S(2)}, u32[]{:S(2)}) collective-permute-start(f32[4,32,384]{2,1,0:T(8,128)S(1)} %get-tuple-element.40), channel_id=1, source_target_pairs={{0,2},{2,0},{4,6},{6,4},{8,10},{10,8},{12,14},{14,12},{16,18},{18,... | collective-permute-start | bytes 589832 | tf_op jit(solution)/shard_map/ppermute | solution.py:25
  45.4 17.9 %collective-permute-start.12 = (f32[4,32,384]{2,1,0:T(8,128)}, f32[4,32,384]{2,1,0:T(8,128)}, u32[]{:S(2)}, u32[]{:S(2)}) collective-permute-start(f32[4,32,384]{2,1,0:T(8,128)} %get-tuple-element.41), channel_id=1, source_target_pairs={{0,4},{2,6},{4,0},{6,2},{8,12},{10,14},{12,8},{14,10},{16,20},{18,... | collective-permute-start | bytes 589832 | tf_op jit(solution)/shard_map/ppermute | solution.py:25
  49.1 17.8 %copy-start.30 = (f32[64,768]{1,0:T(8,128)S(1)}, f32[64,768]{1,0:T(8,128)}, u32[]{:S(2)}) copy-start(f32[64,768]{1,0:T(8,128)} %param.13) | copy-start | bytes 589828
  51.3 15.6 %copy-start.14 = (bf16[384,768]{1,0:T(8,128)(2,1)S(1)}, bf16[384,768]{1,0:T(8,128)(2,1)}, u32[]{:S(2)}) copy-start(bf16[384,768]{1,0:T(8,128)(2,1)} %shard_map.127) | copy-start | bytes 1769476
  52.8 5.9 %collective-permute-start.5 = (f32[10,384]{1,0:T(8,128)S(1)}, f32[10,384]{1,0:T(8,128)S(1)}, u32[]{:S(2)}, u32[]{:S(2)}) collective-permute-start(f32[10,384]{1,0:T(8,128)S(1)} %select_reduce_fusion.3), channel_id=1, source_target_pairs={{0,6},{2,4},{4,2},{6,0},{8,14},{10,12},{12,10},{14,8},{16,22},{18,... | collective-permute-start | bytes 46088 | tf_op jit(solution)/shard_map/ppermute | solution.py:25
  53.5 5.3 %collective-permute-start.4 = (f32[10,384]{1,0:T(8,128)S(1)}, f32[10,384]{1,0:T(8,128)S(1)}, u32[]{:S(2)}, u32[]{:S(2)}) collective-permute-start(f32[10,384]{1,0:T(8,128)S(1)} %select_reduce_fusion.3), channel_id=1, source_target_pairs={{0,4},{2,6},{4,0},{6,2},{8,12},{10,14},{12,8},{14,10},{16,20},{18,... | collective-permute-start | bytes 46088 | tf_op jit(solution)/shard_map/ppermute | solution.py:25
  54.9 3.8 %collective-permute-start.3 = (f32[10,384]{1,0:T(8,128)S(1)}, f32[10,384]{1,0:T(8,128)S(1)}, u32[]{:S(2)}, u32[]{:S(2)}) collective-permute-start(f32[10,384]{1,0:T(8,128)S(1)} %select_reduce_fusion.3), channel_id=1, source_target_pairs={{0,2},{2,0},{4,6},{6,4},{8,10},{10,8},{12,14},{14,12},{16,18},{18,... | collective-permute-start | bytes 46088 | tf_op jit(solution)/shard_map/ppermute | solution.py:25
  58.2 71.0 %collective-permute-start.15 = (f32[4,2,32,384]{3,2,0,1:T(8,128)}, f32[4,2,32,384]{3,2,0,1:T(8,128)}, u32[]{:S(2)}, u32[]{:S(2)}) collective-permute-start(f32[4,2,32,384]{3,2,0,1:T(8,128)} %get-tuple-element.43), channel_id=1, source_target_pairs={{0,4},{2,6},{4,0},{6,2},{8,12},{10,14},{12,8},{14,10},{16,20},{18,... | collective-permute-start | bytes 1179656 | tf_op jit(solution)/shard_map/ppermute | solution.py:25
  58.8 7.8 %collective-permute-start.8 = (f32[10,384]{1,0:T(8,128)S(1)}, f32[10,384]{1,0:T(8,128)S(1)}, u32[]{:S(2)}, u32[]{:S(2)}) collective-permute-start(f32[10,384]{1,0:T(8,128)S(1)} %add_add_fusion), channel_id=1, source_target_pairs={{0,24},{2,26},{4,28},{6,30},{8,16},{10,18},{12,20},{14,22},{16,8},... | collective-permute-start | bytes 46088 | tf_op jit(solution)/shard_map/ppermute | solution.py:25
  60.2 6.4 %collective-permute-start.7 = (f32[10,384]{1,0:T(8,128)S(1)}, f32[10,384]{1,0:T(8,128)S(1)}, u32[]{:S(2)}, u32[]{:S(2)}) collective-permute-start(f32[10,384]{1,0:T(8,128)S(1)} %add_add_fusion), channel_id=1, source_target_pairs={{0,16},{2,18},{4,20},{6,22},{8,24},{10,26},{12,28},{14,30},{16,0},... | collective-permute-start | bytes 46088 | tf_op jit(solution)/shard_map/ppermute | solution.py:25
  62.1 4.5 %collective-permute-start.6 = (f32[10,384]{1,0:T(8,128)S(1)}, f32[10,384]{1,0:T(8,128)S(1)}, u32[]{:S(2)}, u32[]{:S(2)}) collective-permute-start(f32[10,384]{1,0:T(8,128)S(1)} %add_add_fusion), channel_id=1, source_target_pairs={{0,8},{2,10},{4,12},{6,14},{8,0},{10,2},{12,4},{14,6},{16,24},{18,... | collective-permute-start | bytes 46088 | tf_op jit(solution)/shard_map/ppermute | solution.py:25
  65.1 5.1 %copy-start.3 = (bf16[64,32,768]{2,1,0:T(8,128)(2,1)S(1)}, bf16[64,32,768]{2,1,0:T(8,128)(2,1)}, u32[]{:S(2)}) copy-start(bf16[64,32,768]{2,1,0:T(8,128)(2,1)} %param.10) | copy-start | bytes 9437188
  65.1 65.6 %collective-permute-start.13 = (f32[4,2,32,384]{3,2,0,1:T(8,128)}, f32[4,2,32,384]{3,2,0,1:T(8,128)}, u32[]{:S(2)}, u32[]{:S(2)}) collective-permute-start(f32[4,2,32,384]{3,2,0,1:T(8,128)} %get-tuple-element.37), channel_id=1, source_target_pairs={{0,2},{2,0},{4,6},{6,4},{8,10},{10,8},{12,14},{14,12},{16,18},{18,... | collective-permute-start | bytes 1179656 | tf_op jit(solution)/shard_map/ppermute | solution.py:25
  66.7 2.3 %copy-start.26 = (f32[10,384]{1,0:T(8,128)}, f32[10,384]{1,0:T(8,128)S(1)}, u32[]{:S(2)}) copy-start(f32[10,384]{1,0:T(8,128)S(1)} %fusion.106) | copy-start | bytes 46084
  79.2 5.4 %copy-start.4 = (bf16[64,32,768]{2,1,0:T(8,128)(2,1)S(1)}, bf16[64,32,768]{2,1,0:T(8,128)(2,1)}, u32[]{:S(2)}) copy-start(bf16[64,32,768]{2,1,0:T(8,128)(2,1)} %param.10) | copy-start | bytes 9437188
  79.2 5.4 %copy-start.25 = (f32[64,512]{1,0:T(8,128)S(1)}, f32[64,512]{1,0:T(8,128)}, u32[]{:S(2)}) copy-start(f32[64,512]{1,0:T(8,128)} %get-tuple-element.28) | copy-start | bytes 393220
  80.9 2.5 %copy-start.13 = (f32[4,2,2,48,256]{4,3,2,1,0:T(8,128)}, f32[4,2,2,48,256]{4,3,2,1,0:T(8,128)S(1)}, u32[]{:S(2)}) copy-start(f32[4,2,2,48,256]{4,3,2,1,0:T(8,128)S(1)} %get-tuple-element.11) | copy-start | bytes 2359300
  81.8 58.1 %collective-permute-start.17 = (f32[4,2,48,256]{3,2,1,0:T(8,128)}, f32[4,2,48,256]{3,2,1,0:T(8,128)}, u32[]{:S(2)}, u32[]{:S(2)}) collective-permute-start(f32[4,2,48,256]{3,2,1,0:T(8,128)} %dynamic-slice_bitcast_fusion.6), channel_id=1, source_target_pairs={{0,2},{2,0},{4,6},{6,4},{8,10},{10,8},{12,14},{14,12},{16,18},{18,... | collective-permute-start | bytes 1179656 | tf_op jit(solution)/shard_map/ppermute | solution.py:25
  83.4 58.2 %collective-permute-start.19 = (f32[4,2,48,256]{3,2,1,0:T(8,128)}, f32[4,2,48,256]{3,2,1,0:T(8,128)}, u32[]{:S(2)}, u32[]{:S(2)}) collective-permute-start(f32[4,2,48,256]{3,2,1,0:T(8,128)} %dynamic-slice_bitcast_fusion.5), channel_id=1, source_target_pairs={{0,4},{2,6},{4,0},{6,2},{8,12},{10,14},{12,8},{14,10},{16,20},{18,... | collective-permute-start | bytes 1179656 | tf_op jit(solution)/shard_map/ppermute | solution.py:25
  96.4 4.8 %copy-start.24 = (f32[64,512]{1,0:T(8,128)S(1)}, f32[64,512]{1,0:T(8,128)}, u32[]{:S(2)}) copy-start(f32[64,512]{1,0:T(8,128)} %get-tuple-element.29) | copy-start | bytes 393220
  100.4 42.4 %collective-permute-start.31 = (f32[4,2,48,256]{3,2,1,0:T(8,128)}, f32[4,2,48,256]{3,2,1,0:T(8,128)}, u32[]{:S(2)}, u32[]{:S(2)}) collective-permute-start(f32[4,2,48,256]{3,2,1,0:T(8,128)} %dynamic-slice_bitcast_fusion.2), channel_id=1, source_target_pairs={{0,2},{2,0},{4,6},{6,4},{8,10},{10,8},{12,14},{14,12},{16,18},{18,... | collective-permute-start | bytes 1179656 | tf_op jit(solution)/shard_map/ppermute | solution.py:25
  111.5 2.1 %copy-start.27 = (f32[10,384]{1,0:T(8,128)S(1)}, f32[10,384]{1,0:T(8,128)}, u32[]{:S(2)}) copy-start(f32[10,384]{1,0:T(8,128)} %copy-done.26) | copy-start | bytes 46084
  111.6 3.1 %copy-start.29 = (s32[10,384]{1,0:T(8,128)S(1)}, s32[10,384]{1,0:T(8,128)}, u32[]{:S(2)}) copy-start(s32[10,384]{1,0:T(8,128)} %copy-done.28) | copy-start | bytes 46084
  111.6 7.4 %copy-start.15 = (bf16[384,768]{1,0:T(8,128)(2,1)S(1)}, bf16[384,768]{1,0:T(8,128)(2,1)}, u32[]{:S(2)}) copy-start(bf16[384,768]{1,0:T(8,128)(2,1)} %shard_map.127) | copy-start | bytes 1769476
  118.9 13.3 %copy-start.22 = (f32[4,2,1,32,384]{4,3,0,2,1:T(8,128)S(1)}, f32[4,2,1,32,384]{4,3,0,2,1:T(8,128)}, u32[]{:S(2)}) copy-start(f32[4,2,1,32,384]{4,3,0,2,1:T(8,128)} %get-tuple-element.36) | copy-start | bytes 1179652
  124.7 41.6 %all-to-all-start.1 = ((f32[16,48,96]{2,1,0:T(8,128)}), f32[16,48,96]{2,1,0:T(8,128)}, u32[]{:S(2)}, u32[]{:S(2)}) async-start(f32[16,48,96]{2,1,0:T(8,128)} %bitcast.73), calls=%async_computation.1 | async-start | bytes 786432 | tf_op jit(solution)/shard_map/all_to_all | solution.py:233
  129.2 16.2 %collective-permute-start.33 = (f32[4,2,48,256]{3,2,1,0:T(8,128)}, f32[4,2,48,256]{3,2,1,0:T(8,128)}, u32[]{:S(2)}, u32[]{:S(2)}) collective-permute-start(f32[4,2,48,256]{3,2,1,0:T(8,128)} %dynamic-slice_bitcast_fusion.1), channel_id=1, source_target_pairs={{0,4},{2,6},{4,0},{6,2},{8,12},{10,14},{12,8},{14,10},{16,20},{18,... | collective-permute-start | bytes 1179656 | tf_op jit(solution)/shard_map/ppermute | solution.py:25
  130.7 16.4 %collective-permute-start.24 = (f32[4,2,48,256]{3,2,1,0:T(8,128)}, f32[4,2,48,256]{3,2,1,0:T(8,128)}, u32[]{:S(2)}, u32[]{:S(2)}) collective-permute-start(f32[4,2,48,256]{3,2,1,0:T(8,128)} %dynamic-slice_bitcast_fusion.4), channel_id=1, source_target_pairs={{0,2},{2,0},{4,6},{6,4},{8,10},{10,8},{12,14},{14,12},{16,18},{18,... | collective-permute-start | bytes 1179656 | tf_op jit(solution)/shard_map/ppermute | solution.py:25
  134.8 6.9 %copy-start.8 = (f32[4,2,2,48,256]{4,3,2,1,0:T(8,128)S(1)}, f32[4,2,2,48,256]{4,3,2,1,0:T(8,128)}, u32[]{:S(2)}) copy-start(f32[4,2,2,48,256]{4,3,2,1,0:T(8,128)} %copy-done.7) | copy-start | bytes 2359300
  137.3 7.1 %copy-start.12 = (f32[4,2,2,48,256]{4,3,2,1,0:T(8,128)S(1)}, f32[4,2,2,48,256]{4,3,2,1,0:T(8,128)}, u32[]{:S(2)}) copy-start(f32[4,2,2,48,256]{4,3,2,1,0:T(8,128)} %copy-done.11) | copy-start | bytes 2359300
  139.0 7.1 %copy-start.6 = (f32[4,2,2,48,256]{4,3,2,1,0:T(8,128)S(1)}, f32[4,2,2,48,256]{4,3,2,1,0:T(8,128)}, u32[]{:S(2)}) copy-start(f32[4,2,2,48,256]{4,3,2,1,0:T(8,128)} %copy-done.5) | copy-start | bytes 2359300
  139.9 7.9 %copy-start.10 = (f32[4,2,2,48,256]{4,3,2,1,0:T(8,128)S(1)}, f32[4,2,2,48,256]{4,3,2,1,0:T(8,128)}, u32[]{:S(2)}) copy-start(f32[4,2,2,48,256]{4,3,2,1,0:T(8,128)} %copy-done.9) | copy-start | bytes 2359300
  139.9 10.6 %collective-permute-start.26 = (f32[4,2,48,256]{3,2,1,0:T(8,128)}, f32[4,2,48,256]{3,2,1,0:T(8,128)S(1)}, u32[]{:S(2)}, u32[]{:S(2)}) collective-permute-start(f32[4,2,48,256]{3,2,1,0:T(8,128)} %dynamic-slice_bitcast_fusion.3), channel_id=1, source_target_pairs={{0,4},{2,6},{4,0},{6,2},{8,12},{10,14},{12,8},{14,10},{16,20},{18,... | collective-permute-start | bytes 1179656 | tf_op jit(solution)/shard_map/ppermute | solution.py:25
  141.6 47.8 %collective-permute-start.16 = (f32[192,768]{1,0:T(8,128)}, f32[192,768]{1,0:T(8,128)}, u32[]{:S(2)}, u32[]{:S(2)}) collective-permute-start(f32[192,768]{1,0:T(8,128)} %dynamic-slice_bitcast_fusion), channel_id=1, source_target_pairs={{0,1},{1,0},{2,3},{3,2},{4,5},{5,4},{6,7},{7,6},{8,9},{9,8},{10,11... | collective-permute-start | bytes 1769480 | tf_op jit(solution)/shard_map/ppermute | solution.py:25
  142.8 11.9 %collective-permute-start.18 = (f32[4,48,256]{2,1,0:T(8,128)S(1)}, f32[4,48,256]{2,1,0:T(8,128)S(1)}, u32[]{:S(2)}, u32[]{:S(2)}) collective-permute-start(f32[4,48,256]{2,1,0:T(8,128)S(1)} %dynamic-slice_bitcast_fusion.12), channel_id=1, source_target_pairs={{0,4},{2,6},{4,0},{6,2},{8,12},{10,14},{12,8},{14,10},{16,20},{18,... | collective-permute-start | bytes 589832 | tf_op jit(solution)/shard_map/ppermute | solution.py:25
  145.4 9.5 %collective-permute-start.20 = (f32[4,48,256]{2,1,0:T(8,128)S(1)}, f32[4,48,256]{2,1,0:T(8,128)S(1)}, u32[]{:S(2)}, u32[]{:S(2)}) collective-permute-start(f32[4,48,256]{2,1,0:T(8,128)S(1)} %dynamic-slice_bitcast_fusion.11), channel_id=1, source_target_pairs={{0,2},{2,0},{4,6},{6,4},{8,10},{10,8},{12,14},{14,12},{16,18},{18,... | collective-permute-start | bytes 589832 | tf_op jit(solution)/shard_map/ppermute | solution.py:25
  147.2 11.6 %collective-permute-start.32 = (f32[4,48,256]{2,1,0:T(8,128)S(1)}, f32[4,48,256]{2,1,0:T(8,128)S(1)}, u32[]{:S(2)}, u32[]{:S(2)}) collective-permute-start(f32[4,48,256]{2,1,0:T(8,128)S(1)} %dynamic-slice_bitcast_fusion.8), channel_id=1, source_target_pairs={{0,4},{2,6},{4,0},{6,2},{8,12},{10,14},{12,8},{14,10},{16,20},{18,... | collective-permute-start | bytes 589832 | tf_op jit(solution)/shard_map/ppermute | solution.py:25
  150.5 9.4 %collective-permute-start.34 = (f32[4,48,256]{2,1,0:T(8,128)S(1)}, f32[4,48,256]{2,1,0:T(8,128)S(1)}, u32[]{:S(2)}, u32[]{:S(2)}) collective-permute-start(f32[4,48,256]{2,1,0:T(8,128)S(1)} %dynamic-slice_bitcast_fusion.7), channel_id=1, source_target_pairs={{0,2},{2,0},{4,6},{6,4},{8,10},{10,8},{12,14},{14,12},{16,18},{18,... | collective-permute-start | bytes 589832 | tf_op jit(solution)/shard_map/ppermute | solution.py:25
  154.7 8.5 %collective-permute-start.25 = (f32[4,48,256]{2,1,0:T(8,128)S(1)}, f32[4,48,256]{2,1,0:T(8,128)S(1)}, u32[]{:S(2)}, u32[]{:S(2)}) collective-permute-start(f32[4,48,256]{2,1,0:T(8,128)S(1)} %dynamic-slice_bitcast_fusion.10), channel_id=1, source_target_pairs={{0,4},{2,6},{4,0},{6,2},{8,12},{10,14},{12,8},{14,10},{16,20},{18,... | collective-permute-start | bytes 589832 | tf_op jit(solution)/shard_map/ppermute | solution.py:25
  155.0 3.8 %copy-start.17 = (f32[4,48,256]{2,1,0:T(8,128)}, f32[4,48,256]{2,1,0:T(8,128)S(1)}, u32[]{:S(2)}) copy-start(f32[4,48,256]{2,1,0:T(8,128)S(1)} %bitcast_add_fusion.12) | copy-start | bytes 589828
  155.0 9.2 %collective-permute-start.27 = (f32[4,48,256]{2,1,0:T(8,128)S(1)}, f32[4,48,256]{2,1,0:T(8,128)S(1)}, u32[]{:S(2)}, u32[]{:S(2)}) collective-permute-start(f32[4,48,256]{2,1,0:T(8,128)S(1)} %dynamic-slice_bitcast_fusion.9), channel_id=1, source_target_pairs={{0,2},{2,0},{4,6},{6,4},{8,10},{10,8},{12,14},{14,12},{16,18},{18,... | collective-permute-start | bytes 589832 | tf_op jit(solution)/shard_map/ppermute | solution.py:25
  157.5 2.5 %copy-start.20 = (f32[4,48,256]{2,1,0:T(8,128)}, f32[4,48,256]{2,1,0:T(8,128)S(1)}, u32[]{:S(2)}) copy-start(f32[4,48,256]{2,1,0:T(8,128)S(1)} %bitcast_add_fusion.11) | copy-start | bytes 589828
  158.8 11.4 %collective-permute-start.21 = (f32[48,512]{1,0:T(8,128)}, f32[48,512]{1,0:T(8,128)}, u32[]{:S(2)}, u32[]{:S(2)}) collective-permute-start(f32[48,512]{1,0:T(8,128)} %get-tuple-element.24), channel_id=1, source_target_pairs={{0,8},{2,10},{4,12},{6,14},{8,0},{10,2},{12,4},{14,6},{16,24},{18,... | collective-permute-start | bytes 294920 | tf_op jit(solution)/shard_map/ppermute | solution.py:25
  159.9 2.5 %copy-start.16 = (f32[4,48,256]{2,1,0:T(8,128)}, f32[4,48,256]{2,1,0:T(8,128)S(1)}, u32[]{:S(2)}) copy-start(f32[4,48,256]{2,1,0:T(8,128)S(1)} %bitcast_add_fusion.8) | copy-start | bytes 589828
  159.9 13.1 %collective-permute-start.22 = (f32[48,512]{1,0:T(8,128)}, f32[48,512]{1,0:T(8,128)}, u32[]{:S(2)}, u32[]{:S(2)}) collective-permute-start(f32[48,512]{1,0:T(8,128)} %get-tuple-element.25), channel_id=1, source_target_pairs={{0,16},{2,18},{4,20},{6,22},{8,24},{10,26},{12,28},{14,30},{16,0},... | collective-permute-start | bytes 294920 | tf_op jit(solution)/shard_map/ppermute | solution.py:25
  163.2 10.8 %collective-permute-start.23 = (f32[48,512]{1,0:T(8,128)}, f32[48,512]{1,0:T(8,128)}, u32[]{:S(2)}, u32[]{:S(2)}) collective-permute-start(f32[48,512]{1,0:T(8,128)} %get-tuple-element.26), channel_id=1, source_target_pairs={{0,24},{2,26},{4,28},{6,30},{8,16},{10,18},{12,20},{14,22},{16,8},... | collective-permute-start | bytes 294920 | tf_op jit(solution)/shard_map/ppermute | solution.py:25
  164.2 10.8 %collective-permute-start.35 = (f32[48,512]{1,0:T(8,128)}, f32[48,512]{1,0:T(8,128)}, u32[]{:S(2)}, u32[]{:S(2)}) collective-permute-start(f32[48,512]{1,0:T(8,128)} %get-tuple-element.33), channel_id=1, source_target_pairs={{0,8},{2,10},{4,12},{6,14},{8,0},{10,2},{12,4},{14,6},{16,24},{18,... | collective-permute-start | bytes 294920 | tf_op jit(solution)/shard_map/ppermute | solution.py:25
  165.5 25.9 %copy-start.1 = (bf16[768,1536]{1,0:T(8,128)(2,1)S(1)}, bf16[768,1536]{1,0:T(8,128)(2,1)}, u32[]{:S(2)}) copy-start(bf16[768,1536]{1,0:T(8,128)(2,1)} %param.12) | copy-start | bytes 7077892
  170.1 11.0 %collective-permute-start.36 = (f32[48,512]{1,0:T(8,128)}, f32[48,512]{1,0:T(8,128)S(1)}, u32[]{:S(2)}, u32[]{:S(2)}) collective-permute-start(f32[48,512]{1,0:T(8,128)} %get-tuple-element.34), channel_id=1, source_target_pairs={{0,16},{2,18},{4,20},{6,22},{8,24},{10,26},{12,28},{14,30},{16,0},... | collective-permute-start | bytes 294920 | tf_op jit(solution)/shard_map/ppermute | solution.py:25
  173.0 11.0 %collective-permute-start.37 = (f32[48,512]{1,0:T(8,128)}, f32[48,512]{1,0:T(8,128)S(1)}, u32[]{:S(2)}, u32[]{:S(2)}) collective-permute-start(f32[48,512]{1,0:T(8,128)} %get-tuple-element.35), channel_id=1, source_target_pairs={{0,24},{2,26},{4,28},{6,30},{8,16},{10,18},{12,20},{14,22},{16,8},... | collective-permute-start | bytes 294920 | tf_op jit(solution)/shard_map/ppermute | solution.py:25
  174.0 11.0 %collective-permute-start.28 = (f32[48,512]{1,0:T(8,128)}, f32[48,512]{1,0:T(8,128)S(1)}, u32[]{:S(2)}, u32[]{:S(2)}) collective-permute-start(f32[48,512]{1,0:T(8,128)} %get-tuple-element.30), channel_id=1, source_target_pairs={{0,8},{2,10},{4,12},{6,14},{8,0},{10,2},{12,4},{14,6},{16,24},{18,... | collective-permute-start | bytes 294920 | tf_op jit(solution)/shard_map/ppermute | solution.py:25
  175.0 11.3 %collective-permute-start.29 = (f32[48,512]{1,0:T(8,128)}, f32[48,512]{1,0:T(8,128)S(1)}, u32[]{:S(2)}, u32[]{:S(2)}) collective-permute-start(f32[48,512]{1,0:T(8,128)} %get-tuple-element.31), channel_id=1, source_target_pairs={{0,16},{2,18},{4,20},{6,22},{8,24},{10,26},{12,28},{14,30},{16,0},... | collective-permute-start | bytes 294920 | tf_op jit(solution)/shard_map/ppermute | solution.py:25
  181.1 6.7 %collective-permute-start.30 = (f32[48,512]{1,0:T(8,128)}, f32[48,512]{1,0:T(8,128)S(1)}, u32[]{:S(2)}, u32[]{:S(2)}) collective-permute-start(f32[48,512]{1,0:T(8,128)} %get-tuple-element.32), channel_id=1, source_target_pairs={{0,24},{2,26},{4,28},{6,30},{8,16},{10,18},{12,20},{14,22},{16,8},... | collective-permute-start | bytes 294920 | tf_op jit(solution)/shard_map/ppermute | solution.py:25
  (9 other events, 10.2 us)

commit v2 on v0

v2 whole, which is shorter than its diff:
```python
import functools
import math

import jax
import jax.numpy as jnp
from jax import lax
from jax.experimental import pallas as pl
from jax.experimental.pallas import tpu as pltpu
from jax.sharding import PartitionSpec as P

beta_one = 0.9
beta_two = 0.999
adam_eps = 1e-08
learn_rate = 0.05
first_fix = 1.0 - 0.9**10
second_fix = 1.0 - 0.999**10

PLANE = 4
THIRDS = 3
GELU_ONE = math.sqrt(2.0 / math.pi)
GELU_THREE = GELU_ONE * 0.044715
MIB = 2**20


def whole(shape):
    return pl.BlockSpec(shape, lambda *_: (0,) * len(shape))


def scalar_spec():
    return pl.BlockSpec(memory_space=pltpu.SMEM)


def params(mib):
    return pltpu.CompilerParams(vmem_limit_bytes=mib * MIB)


def f32(shape):
    return jax.ShapeDtypeStruct(shape, jnp.float32)


def bf16(shape):
    return jax.ShapeDtypeStruct(shape, jnp.bfloat16)


def pair_swap(values, axis, count, bits):
    return lax.ppermute(values, axis, [(s, s ^ bits) for s in range(count)])


def label_sum_parts(values, label_count):
    values = values + sum(pair_swap(values, "label", label_count, b) for b in range(1, PLANE))
    return [values] + [
        pair_swap(values, "label", label_count, b) for b in range(PLANE, label_count, PLANE)
    ]


def bit_order(label_count, part):
    bits = [1 << b for b in range(label_count.bit_length() - 1)]
    lead = ([1, 2, 4], [2, 1, 4], [4, 1, 2])[part]
    return [b for b in lead if b in bits] + [b for b in bits if b not in lead]


def relative_shards(label_count, order):
    count = len(order)
    return [
        sum(bit for place, bit in enumerate(order) if p >> (count - 1 - place) & 1)
        for p in range(label_count)
    ]


def scatter_sum(keep, give, label_count, order):
    parts = [keep]
    for bit in order:
        parts.append(pair_swap(give, "label", label_count, bit))
        size = parts[-1].shape[0]
        if size == 1:
            break
        give = sum(p[size // 2 : size] for p in parts)
    return sum(p[0] for p in parts)


def split_bf16(values):
    high = values.astype(jnp.bfloat16)
    low = (values - high.astype(jnp.float32)).astype(jnp.bfloat16)
    return high, low


def encode(text_rows, up_weight, down_weight, label_rows):
    tokens, model_width = text_rows.shape
    unit_cols = up_weight.shape[1]
    text_len = tokens // label_rows
    steps = 8
    rows = tokens // steps
    pools = label_rows // steps
    chunk = unit_cols // THIRDS

    def kernel(text_ref, up_ref, down_ref, pooled_ref, slope_ref, turned_ref, encoded_ref):
        step = pl.program_id(0)
        text = text_ref[...]
        turned_ref[...] = text.T
        for part in range(THIRDS):
            cols = slice(part * chunk, (part + 1) * chunk)
            x = jnp.dot(text, up_ref[:, cols], preferred_element_type=jnp.float32)
            square = x * x
            gate = 0.5 + 0.5 * jnp.tanh(x * (GELU_ONE + GELU_THREE * square))
            hidden = x * gate
            slope = gate + (hidden - hidden * gate) * (2 * GELU_ONE + 6 * GELU_THREE * square)
            slope_ref[:, cols] = slope.astype(jnp.bfloat16)
            pooled_ref[pl.ds(step * pools, pools), cols] = jnp.sum(
                hidden.reshape(pools, text_len, chunk), axis=1
            ) * (1.0 / text_len)

        @pl.when(step == steps - 1)
        def _():
            high, low = split_bf16(pooled_ref[...])
            both = lax.dot_general(
                jnp.concatenate((high, low)),
                down_ref[...],
                (((1,), (1,)), ((), ())),
                preferred_element_type=jnp.float32,
            )
            encoded_ref[...] = both[:label_rows] + both[label_rows:]

    return pl.pallas_call(
        kernel,
        grid=(steps,),
        in_specs=[
            pl.BlockSpec((rows, model_width), lambda i: (i, 0)),
            whole(up_weight.shape),
            whole(down_weight.shape),
        ],
        out_specs=[
            whole((label_rows, unit_cols)),
            pl.BlockSpec((rows, unit_cols), lambda i: (i, 0)),
            pl.BlockSpec((model_width, rows), lambda i: (0, i)),
            whole((label_rows, model_width)),
        ],
        out_shape=[
            f32((label_rows, unit_cols)),
            bf16((tokens, unit_cols)),
            bf16((model_width, tokens)),
            f32((label_rows, model_width)),
        ],
        compiler_params=params(28),
        name="encode",
    )(text_rows, up_weight, down_weight)


def score(place, encoded, pooled_text, free_vectors, query_pieces, ids, share):
    label_rows, model_width = free_vectors.shape
    choices, total = ids.shape
    terms = len(encoded)
    pieces = len(query_pieces)

    def kernel(place_ref, *refs):
        encoded_refs, refs = refs[:terms], refs[terms:]
        pooled_ref, free_ref, *refs = refs
        query_refs, refs = refs[:pieces], refs[pieces:]
        ids_ref, share_ref, every_ref, partial_ref, label_ref = refs
        label_vec = pooled_ref[...] + sum(r[...] for r in encoded_refs) + free_ref[...]
        label_bf = label_vec.astype(jnp.bfloat16)
        label_ref[...] = label_bf.astype(jnp.float32)
        share_ref[...] = label_ref[pl.ds(pl.multiple_of(place_ref[1], share), share), :]
        row = 0
        for ref in query_refs:
            every_ref[row : row + ref.shape[0], :] = ref[...].astype(jnp.bfloat16)
            row += ref.shape[0]
        similar = lax.dot_general(
            label_bf, every_ref[...], (((1,), (1,)), ((), ())), preferred_element_type=jnp.float32
        )
        label = lax.broadcasted_iota(jnp.int32, (label_rows, total), 0) + place_ref[0]
        for k in range(choices):
            partial_ref[k : k + 1, :] = jnp.sum(
                jnp.where(label == ids_ref[k : k + 1, :], similar, 0.0), axis=0, keepdims=True
            )

    return pl.pallas_call(
        kernel,
        in_specs=[scalar_spec()] + [pl.BlockSpec(memory_space=pltpu.VMEM)] * (terms + pieces + 3),
        out_shape=[
            f32((share, model_width)),
            bf16((total, model_width)),
            f32((choices, total)),
        ],
        scratch_shapes=[pltpu.VMEM((label_rows, model_width), jnp.float32)],
        compiler_params=params(24),
        name="score",
    )(place, *encoded, pooled_text, free_vectors, *query_pieces, ids)


def spread_of(ids_ref, coef, first, labels):
    choices, total = coef.shape
    label = lax.broadcasted_iota(jnp.int32, (labels, total), 0) + first
    spread = jnp.zeros((labels, total), jnp.float32)
    for k in range(choices):
        spread = jnp.where(label == ids_ref[k : k + 1, :total], coef[k : k + 1, :], spread)
    return spread.astype(jnp.bfloat16)


def label_gradient(place, score_terms, ids, every_query, down_weight, label_rows, text_len):
    choices, total = ids.shape
    model_width, unit_cols = down_weight.shape
    terms = len(score_terms)
    temper = 1.0 / math.sqrt(model_width)

    def kernel(place_ref, *refs):
        score_refs, refs = refs[:terms], refs[terms:]
        ids_ref, query_ref, down_ref, coef_ref, grad_ref, hidden_ref = refs
        scores = sum(r[...] for r in score_refs) * temper
        powers = jnp.exp(scores - jnp.max(scores, axis=0, keepdims=True))
        likely = powers / jnp.sum(powers, axis=0, keepdims=True)
        rank = lax.broadcasted_iota(jnp.int32, (choices, total), 0)
        coef = (likely - jnp.where(rank < 2, 0.5, 0.0)) * temper
        coef = coef.astype(jnp.bfloat16).astype(jnp.float32)
        coef_ref[...] = coef
        spread = spread_of(ids_ref, coef, place_ref[0], label_rows)
        grad = jnp.dot(spread, query_ref[...], preferred_element_type=jnp.float32)
        grad_ref[...] = grad
        hidden_ref[...] = jnp.dot(
            grad.astype(jnp.bfloat16), down_ref[...], preferred_element_type=jnp.float32
        ) * (1.0 / text_len)

    return pl.pallas_call(
        kernel,
        in_specs=[scalar_spec()] + [pl.BlockSpec(memory_space=pltpu.VMEM)] * (terms + 3),
        out_shape=[f32((choices, total)), f32((label_rows, model_width)), f32((label_rows, unit_cols))],
        compiler_params=params(24),
        name="label_gradient",
    )(place, *score_terms, ids, every_query, down_weight)


def up_gradient(place, turned, slope, hidden_grad, label_count, part):
    model_width, tokens = turned.shape
    label_rows, unit_cols = hidden_grad.shape
    text_len = tokens // label_rows
    cols = unit_cols // THIRDS
    own = model_width // label_count
    steps = 4
    depth = tokens // steps
    rows = label_rows // steps
    relative = relative_shards(label_count, bit_order(label_count, part))
    half = label_count // 2

    def kernel(place_ref, turned_ref, slope_ref, hidden_ref, keep_ref, give_ref, total_ref, blocks_ref):
        step = pl.program_id(0)
        slope = slope_ref[...].astype(jnp.float32).reshape(rows, text_len, cols)
        grad = slope * hidden_ref[...][:, None, :]
        grad = grad.reshape(depth, cols).astype(jnp.bfloat16)
        term = jnp.dot(turned_ref[...], grad, preferred_element_type=jnp.float32)

        @pl.when(step == 0)
        def _():
            total_ref[...] = term

        @pl.when(step > 0)
        def _():
            total_ref[...] += term

        @pl.when(step == steps - 1)
        def _():
            for block in range(label_count):
                blocks_ref[block] = total_ref[block * own : (block + 1) * own, :]
            for p in range(half):
                keep_ref[p] = blocks_ref[place_ref[0] ^ relative[p]]
                give_ref[p] = blocks_ref[place_ref[0] ^ relative[half + p]]

    return pl.pallas_call(
        kernel,
        grid=(steps,),
        in_specs=[
            scalar_spec(),
            pl.BlockSpec((model_width, depth), lambda i: (0, i)),
            pl.BlockSpec((depth, cols), lambda i: (i, part)),
            pl.BlockSpec((rows, cols), lambda i: (i, part)),
        ],
        out_specs=[whole((half, own, cols))] * 2,
        out_shape=[f32((half, own, cols))] * 2,
        scratch_shapes=[
            pltpu.VMEM((model_width, cols), jnp.float32),
            pltpu.VMEM((label_count, own, cols), jnp.float32),
        ],
        compiler_params=params(24),
        name="up_gradient",
    )(place, turned, slope, hidden_grad)


def query_gradient(coef, ids, label_all, first, count):
    labels, model_width = label_all.shape

    def kernel(coef_ref, ids_ref, label_ref, out_ref):
        spread = spread_of(ids_ref, coef_ref[...], 0, labels)
        out_ref[...] = lax.dot_general(
            spread,
            label_ref[...].astype(jnp.bfloat16),
            (((0,), (0,)), ((), ())),
            preferred_element_type=jnp.float32,
        )

    coef = lax.dynamic_slice_in_dim(coef, first, count, 1)
    ids = lax.dynamic_slice_in_dim(ids, first, count, 1)
    return pl.pallas_call(
        kernel,
        out_shape=f32((count, model_width)),
        compiler_params=params(32),
        name="query_gradient",
    )(coef, ids, label_all)


def down_gradient(coef, ids, every_query, pooled_all, label_count):
    labels, units = pooled_all.shape
    model_width = every_query.shape[1]
    own = model_width // label_count

    def kernel(coef_ref, ids_ref, query_ref, pooled_ref, out_ref):
        spread = spread_of(ids_ref, coef_ref[...], 0, labels)
        grad = jnp.dot(spread, query_ref[...], preferred_element_type=jnp.float32)
        grad = grad.astype(jnp.bfloat16)
        total = sum(
            lax.dot_general(grad, half, (((0,), (0,)), ((), ())), preferred_element_type=jnp.float32)
            for half in split_bf16(pooled_ref[...])
        )
        for block in range(label_count):
            out_ref[block] = total[block * own : (block + 1) * own, :]

    return pl.pallas_call(
        kernel,
        out_shape=f32((label_count, own, units)),
        compiler_params=params(32),
        name="down_gradient",
    )(coef, ids, every_query, pooled_all)


def body(
    label_count,
    query_count,
    queries,
    label_ids,
    label_text,
    up_weight,
    down_weight,
    free_vectors,
    moments,
    seconds,
):
    label_rows, text_len, model_width = label_text.shape
    query_rows = queries.shape[0]
    unit_cols = up_weight.shape[1]
    labels = label_count * label_rows
    shard = lax.axis_index("label")
    core = lax.axis_index("query")
    share = label_rows // query_count
    place = jnp.stack((shard * label_rows, core * share)).astype(jnp.int32)
    shard_place = shard.astype(jnp.int32).reshape(1)

    if query_count == 2:
        query_pieces = [queries, pair_swap(queries.astype(jnp.float32), "query", 2, 1)]
        ids = jnp.concatenate((label_ids.T, pair_swap(label_ids.T, "query", 2, 1)), axis=1)
        first_query = 0
    else:
        query_pieces = [lax.all_gather(queries.astype(jnp.float32), "query", tiled=True)]
        ids = lax.all_gather(label_ids, "query", tiled=True).T
        first_query = core * query_rows

    text_rows = label_text.reshape(label_rows * text_len, model_width)
    pooled_hidden, slope, turned, encoded_part = encode(
        text_rows, up_weight, down_weight, label_rows
    )
    pooled_text = jnp.mean(label_text, axis=1, dtype=jnp.float32)
    if query_count == 2:
        encoded = [encoded_part, pair_swap(encoded_part, "query", 2, 1)]
    else:
        encoded = [lax.psum(encoded_part, "query")]
    own_share, every_query, partial = score(
        place, encoded, pooled_text, free_vectors, query_pieces, ids, share
    )
    label_all = lax.all_gather(own_share, ("label", "query"), tiled=True)
    unit_share = unit_cols // label_count
    pooled_all = lax.all_to_all(
        pooled_hidden.reshape(label_rows, label_count, unit_share).swapaxes(0, 1), "label", 0, 0
    ).reshape(labels, unit_share)

    coef, label_grad, hidden_grad = label_gradient(
        place,
        label_sum_parts(partial, label_count),
        ids,
        every_query,
        down_weight,
        label_rows,
        text_len,
    )

    up_parts = []
    for part in range(THIRDS):
        keep, give = up_gradient(shard_place, turned, slope, hidden_grad, label_count, part)
        up_parts.append(scatter_sum(keep, give, label_count, bit_order(label_count, part)))
    up_grad = jnp.concatenate(up_parts, axis=1)

    down_cols = down_gradient(coef, ids, every_query, pooled_all, label_count)
    down_grad = lax.all_to_all(down_cols, "label", 0, 0)
    down_grad = down_grad.swapaxes(0, 1).reshape(model_width // label_count, unit_cols)

    query_grad = query_gradient(coef, ids, label_all, first_query, query_rows)

    touched = jnp.any(
        (ids - shard * label_rows)[:, None, :]
        == jnp.arange(label_rows, dtype=jnp.int32)[None, :, None],
        axis=(0, 2),
    )[:, None]
    moment_step = beta_one * moments + (1.0 - beta_one) * label_grad
    second_step = beta_two * seconds + (1.0 - beta_two) * label_grad * label_grad
    update = (
        learn_rate * (moment_step / first_fix) / (jnp.sqrt(second_step / second_fix) + adam_eps)
    )
    free_new = jnp.where(touched, free_vectors - update, free_vectors)
    moments_new = jnp.where(touched, moment_step, moments)
    seconds_new = jnp.where(touched, second_step, seconds)
    return (free_new, moments_new, seconds_new, query_grad, up_grad, down_grad)


def solution(mesh):
    placed = (
        P("query", None),
        P("query", None),
        P("label", None, None),
        P(None, "query"),
        P(None, "query"),
        P("label", None),
        P("label", None),
        P("label", None),
    )
    return jax.shard_map(
        functools.partial(body, mesh.shape["label"], mesh.shape["query"]),
        mesh=mesh,
        in_specs=placed,
        out_specs=(
            P("label", None),
            P("label", None),
            P("label", None),
            P("query", None),
            P("label", "query"),
            P("label", "query"),
        ),
        check_vma=False,
    )
```

time: 474 us -> 175 us (0.37)
  waiting for transfers between devices: 311 us -> 29.9 us
  blocking collectives: 79.5 us -> 0 us
  starting transfers between devices: 0.34 us -> 40.3 us
  Pallas kernels: 0 us -> 36.7 us
  matrix products: 29.3 us -> 0 us
  local copies, waits for them, and re-layouts: 15.3 us -> 34.6 us
  other arithmetic: 24 us -> 17.9 us
    unnamed x5 -> x1, waiting for transfers between devices: 167 us -> 0.02 us
    psum x3 -> x0, waiting for transfers between devices: 144 us -> none  [the longest x1 113 us: body(): query_grad = lax.psum(query_terms, 'label')]
    psum x2 -> x0, blocking collectives: 79.5 us -> none  [the longest x1 77 us: body(): scores = lax.psum(partial_value, 'label') * temper]
    pallas_call x0 -> x8, Pallas kernels: none -> 36.7 us  [the longest x3 13.2 us: up_gradient(): pl.pallas_call(kernel, grid=(steps,), in_specs=[scalar_spec(), pl.BlockSp...]
    ppermute x0 -> x21, waiting for transfers between devices: none -> 29.9 us  [pair_swap(): return lax.ppermute(values, axis, [(s, s ^ bits) for s in range(count)])]
    dot_general x8 -> x0, matrix products: 29.3 us -> none  [the longest x1 12.9 us: body(): preact = jnp.dot(text_rows, up_weight, preferred_element_type=jnp.float32)]
    ppermute x0 -> x21, starting transfers between devices: none -> 27.9 us  [pair_swap(): return lax.ppermute(values, axis, [(s, s ^ bits) for s in range(count)])]
    unnamed x26 -> x72, local copies, waits for them, and re-layouts: 13.3 us -> 28.6 us
  transfers between devices with their start and end apart: 4 -> 24, of which waited for: 4 -> 12; matrix products, arithmetic and copies ran while one was open for 2% -> 14% of each run, Pallas kernels for 0% -> 19%
where the time goes in v2:
time: 175 us; the launch traced here: 174 us
  starting transfers between devices  40.3 us (23%)
  Pallas kernels  36.7 us (21%)
  local copies, waits for them, and re-layouts  34.6 us (20%)
  waiting for transfers between devices  29.9 us (17%)
  other arithmetic  17.9 us (10%)
  between operations  14.2 us (8%)
    ppermute x21, waiting for transfers between devices, pair_swap(): return lax.ppermute(values, axis, [(s, s ^ bits) for s in range(count)])  29.9 us
    unnamed x72, local copies, waits for them, and re-layouts  28.6 us
    ppermute x21, starting transfers between devices, pair_swap(): return lax.ppermute(values, axis, [(s, s ^ bits) for s in range(count)])  27.9 us
    pallas_call x3, Pallas kernels, up_gradient(): pl.pallas_call(kernel, grid=(steps,), in_specs=[scalar_spec(), pl.BlockSp...  13.2 us
    pallas_call x1, Pallas kernels, encode(): pl.pallas_call(kernel, grid=(steps,), in_specs=[pl.BlockSpec((rows, model...  12.7 us
    add x9, other arithmetic, scatter_sum(): give = sum((p[size // 2:size] for p in parts))  8.84 us
    all_to_all x1, starting transfers between devices, body(): lax.all_to_all(pooled_hidden.reshape(label_rows, label_count, unit_share)...  7.98 us
    pallas_call x1, Pallas kernels, down_gradient(): pl.pallas_call(kernel, out_shape=f32((label_count, own, units)), compiler...  5.08 us
  transfers between devices with their start and end apart: 24, of which 12 were waited for; matrix products, arithmetic and copies ran while one was open for 14% of the time, Pallas kernels for 19%

profile of v2, /device:TPU:0, one launch (start us, length us, event | category | flops | bytes accessed | tf_op | source)
XLA Modules:
  0.0 173.7 jit_solution(17029354144965960628)
XLA Ops:
  7.7 1.9 %copy-done.3 = bf16[64,32,768]{2,1,0:T(8,128)(2,1)S(1)} copy-done((bf16[64,32,768]{2,1,0:T(8,128)(2,1)S(1)}, bf16[64,32,768]{2,1,0:T(8,128)(2,1)}, u32[]{:S(2)}) %copy-start.3) | copy-done | bytes 3145752
  9.6 1.7 copy-done.4
  11.3 1.7 copy-done.10
  13.0 12.7 %encode.1 = (f32[64,1536]{1,0:T(8,128)S(1)}, bf16[2048,1536]{1,0:T(8,128)(2,1)S(1)}, bf16[768,2048]{1,0:T(8,128)(2,1)S(1)}, f32[64,768]{1,0:T(8,128)}) custom-call(bf16[2048,768]{1,0:T(8,128)(2,1)S(1)} %bitcast.16, bf16[768,1536]{1,0:T(8,128)(2,1)S(1)} %copy-done.10, bf16[768,1536]{1,0:T(8,128)(2,1)S(1)} %copy-done.4), custom_call_target="tpu_custom_call" | custom-call | tf_op jit(solution)/shard_map/encode/pallas_call | solution.py:123
  25.7 2.6 %copy-done = bf16[2048,1536]{1,0:T(8,128)(2,1)} copy-done((bf16[2048,1536]{1,0:T(8,128)(2,1)}, bf16[2048,1536]{1,0:T(8,128)(2,1)S(1)}, u32[]{:S(2)}) %copy-start) | copy-done | bytes 6291480
  28.4 0.9 convert_element_type.7
  29.7 1.6 convert_reduce_fusion
  31.3 0.9 broadcast_multiply_fusion.refs_2_
  33.1 0.9 copy-done.13
  34.0 2.3 %score.1 = (f32[32,768]{1,0:T(8,128)}, bf16[384,768]{1,0:T(8,128)(2,1)S(1)}, f32[10,384]{1,0:T(8,128)S(1)}) custom-call(s32[2]{0:T(128)S(1)} %pad_add_fusion.1.place_ref, f32[64,768]{1,0:T(8,128)} %get-tuple-element.22.refs_0_, f32[64,768]{1,0:T(8,128)} %collective-permute-done.1.refs_1_, f32[64,768]{1,0:T(8,128)S(1)} %broadcast_multiply_fusion.refs_2_, ...), custom_call_target="tpu_custom_call" | custom-call | tf_op jit(solution)/shard_map/score/pallas_call | solution.py:176
  37.1 2.0 %reshape.57 = f32[64,16,96]{2,1,0:T(8,128)} reshape(f32[64,1536]{1,0:T(8,128)} %copy-done.24) | data formatting | bytes 786432 | tf_op jit(solution)/shard_map/reshape | solution.py:378
  39.1 2.0 %copy.20 = f32[64,16,96]{2,0,1:T(8,128)} copy(f32[64,16,96]{2,1,0:T(8,128)} %reshape.57) | data formatting | bytes 786432 | tf_op jit(solution)/shard_map/reshape | solution.py:378
  41.1 8.0 %all-to-all-start = ((f32[16,64,96]{2,1,0:T(8,128)}), f32[16,64,96]{2,1,0:T(8,128)}, u32[]{:S(2)}, u32[]{:S(2)}) async-start(f32[16,64,96]{2,1,0:T(8,128)} %bitcast.20), calls=%async_computation | async-start | bytes 1048576 | tf_op jit(solution)/shard_map/all_to_all | solution.py:377
  49.1 1.9 %collective-permute-start.3 = (f32[10,384]{1,0:T(8,128)S(1)}, f32[10,384]{1,0:T(8,128)S(1)}, u32[]{:S(2)}, u32[]{:S(2)}) collective-permute-start(f32[10,384]{1,0:T(8,128)S(1)} %get-tuple-element.23), channel_id=1, source_target_pairs={{0,2},{2,0},{4,6},{6,4},{8,10},{10,8},{12,14},{14,12},{16,18},{18,... | collective-permute-start | bytes 46088 | tf_op jit(solution)/shard_map/ppermute | solution.py:46
  51.0 1.4 collective-permute-start.4
  52.7 1.2 collective-permute-done.3
  53.9 1.8 %collective-permute-done.4 = f32[10,384]{1,0:T(8,128)S(1)} collective-permute-done((f32[10,384]{1,0:T(8,128)S(1)}, f32[10,384]{1,0:T(8,128)S(1)}, u32[]{:S(2)}, u32[]{:S(2)}) %collective-permute-start.4) | collective-permute-done | bytes 15392 | tf_op jit(solution)/shard_map/ppermute | solution.py:46
  55.7 1.6 collective-permute-done.5
  57.3 1.6 collective-permute-start.6
  58.9 2.3 %collective-permute-start.7 = (f32[10,384]{1,0:T(8,128)S(1)}, f32[10,384]{1,0:T(8,128)S(1)}, u32[]{:S(2)}, u32[]{:S(2)}) collective-permute-start(f32[10,384]{1,0:T(8,128)S(1)} %add_add_fusion.refs_0_), channel_id=1, source_target_pairs={{0,16},{2,18},{4,20},{6,22},{8,24},{10,26},{12,28},{14,30},{16,0},... | collective-permute-start | bytes 46088 | tf_op jit(solution)/shard_map/ppermute | solution.py:46
  61.7 5.9 %collective-permute-done.7.refs_2_ = f32[10,384]{1,0:T(8,128)S(1)} collective-permute-done((f32[10,384]{1,0:T(8,128)S(1)}, f32[10,384]{1,0:T(8,128)S(1)}, u32[]{:S(2)}, u32[]{:S(2)}) %collective-permute-start.7) | collective-permute-done | bytes 15392 | tf_op jit(solution)/shard_map/ppermute | solution.py:46
  67.7 1.7 copy-done.5
  69.3 1.1 copy-done.8
  71.8 1.3 label_gradient.1
  74.3 2.8 %copy-done.1 = bf16[2048,1536]{1,0:T(8,128)(2,1)S(1)} copy-done((bf16[2048,1536]{1,0:T(8,128)(2,1)S(1)}, bf16[2048,1536]{1,0:T(8,128)(2,1)}, u32[]{:S(2)}) %copy-start.1) | copy-done | bytes 6291480
  77.1 4.4 %up_gradient.3 = (f32[8,48,512]{2,1,0:T(8,128)S(1)}, f32[8,48,512]{2,1,0:T(8,128)}) custom-call(s32[1]{0:T(128)} %bitcast.4.place_ref, bf16[768,2048]{1,0:T(8,128)(2,1)S(1)} %get-tuple-element.28.turned_ref, bf16[2048,1536]{1,0:T(8,128)(2,1)S(1)} %copy-done.1, f32[64,1536]{1,0:T(8,128)S(1)} %get-tuple-element.30.hidden_ref), custom_call_target="tpu_custom_call" | custom-call | tf_op jit(solution)/shard_map/up_gradient/pallas_call | solution.py:266
  82.4 1.5 collective-permute-start.9
  83.9 1.1 copy-done.9
  86.4 5.1 %down_gradient.1 = f32[16,48,96]{2,1,0:T(8,128)S(1)} custom-call(f32[10,384]{1,0:T(8,128)S(1)} %copy-done.28, s32[10,384]{1,0:T(8,128)S(1)} %copy-done.23, bf16[384,768]{1,0:T(8,128)(2,1)S(1)} %copy-done.9, f32[1024,96]{1,0:T(8,128)} %bitcast.9.pooled_ref), custom_call_target="tpu_custom_call" | custom-call | tf_op jit(solution)/shard_map/down_gradient/pallas_call | solution.py:324
  92.3 4.4 %all-to-all-start.1 = ((f32[16,48,96]{2,1,0:T(8,128)}), f32[16,48,96]{2,1,0:T(8,128)}, u32[]{:S(2)}, u32[]{:S(2)}) async-start(f32[16,48,96]{2,1,0:T(8,128)} %copy-done.11), calls=%async_computation.1 | async-start | bytes 786432 | tf_op jit(solution)/shard_map/all_to_all | solution.py:398
  96.7 2.9 %copy-done.2 = bf16[2048,1536]{1,0:T(8,128)(2,1)S(1)} copy-done((bf16[2048,1536]{1,0:T(8,128)(2,1)S(1)}, bf16[2048,1536]{1,0:T(8,128)(2,1)}, u32[]{:S(2)}) %copy-start.2) | copy-done | bytes 6291480
  99.5 4.4 %up_gradient.4 = (f32[8,48,512]{2,1,0:T(8,128)S(1)}, f32[8,48,512]{2,1,0:T(8,128)}) custom-call(s32[1]{0:T(128)} %bitcast.4.place_ref, bf16[768,2048]{1,0:T(8,128)(2,1)S(1)} %get-tuple-element.28.turned_ref, bf16[2048,1536]{1,0:T(8,128)(2,1)S(1)} %copy-done.2, f32[64,1536]{1,0:T(8,128)S(1)} %get-tuple-element.30.hidden_ref), custom_call_target="tpu_custom_call" | custom-call | tf_op jit(solution)/shard_map/up_gradient/pallas_call | solution.py:266
  104.9 1.6 collective-permute-start.13
  106.5 4.4 %up_gradient.5 = (f32[8,48,512]{2,1,0:T(8,128)S(1)}, f32[8,48,512]{2,1,0:T(8,128)}) custom-call(s32[1]{0:T(128)} %bitcast.4.place_ref, bf16[768,2048]{1,0:T(8,128)(2,1)S(1)} %get-tuple-element.28.turned_ref, bf16[2048,1536]{1,0:T(8,128)(2,1)S(1)} %copy-done.2, f32[64,1536]{1,0:T(8,128)S(1)} %get-tuple-element.30.hidden_ref), custom_call_target="tpu_custom_call" | custom-call | tf_op jit(solution)/shard_map/up_gradient/pallas_call | solution.py:266
  110.9 0.9 copy-done.17
  111.9 1.5 collective-permute-start.17
  113.6 1.0 fusion.3
  114.6 1.1 copy.18
  116.7 1.1 slice_add_fusion.2
  118.3 8.5 %collective-permute-done.13 = f32[8,48,512]{2,1,0:T(8,128)} collective-permute-done((f32[8,48,512]{2,1,0:T(8,128)}, f32[8,48,512]{2,1,0:T(8,128)}, u32[]{:S(2)}, u32[]{:S(2)}) %collective-permute-start.13) | collective-permute-done | bytes 786464 | tf_op jit(solution)/shard_map/ppermute | solution.py:46
  126.8 1.1 slice_add_fusion.1
  127.9 1.5 collective-permute-start.14
  129.9 1.1 slice_add_fusion
  130.9 1.5 collective-permute-start.18
  133.3 1.0 slice_add_fusion.7
  134.3 1.7 collective-permute-start.11
  135.9 3.6 %collective-permute-done.14 = f32[4,48,512]{2,1,0:T(8,128)S(1)} collective-permute-done((f32[4,48,512]{2,1,0:T(8,128)S(1)}, f32[4,48,512]{2,1,0:T(8,128)S(1)}, u32[]{:S(2)}, u32[]{:S(2)}) %collective-permute-start.14) | collective-permute-done | bytes 393248 | tf_op jit(solution)/shard_map/ppermute | solution.py:46
  139.6 1.0 slice_add_fusion.5
  140.5 1.7 collective-permute-start.15
  142.2 1.6 collective-permute-done.18
  143.8 1.0 slice_add_fusion.3
  144.7 1.2 collective-permute-start.19
  146.0 0.9 slice_add_fusion.21
  146.9 3.1 %collective-permute-start.12 = (f32[1,48,512]{2,1,0:T(8,128)S(1)}, f32[1,48,512]{2,1,0:T(8,128)S(1)}, u32[]{:S(2)}, u32[]{:S(2)}) collective-permute-start(f32[1,48,512]{2,1,0:T(8,128)S(1)} %slice_add_fusion.21), channel_id=1, source_target_pairs={{0,16},{2,18},{4,20},{6,22},{8,24},{10,26},{12,28},{14,30},{16,0},... | collective-permute-start | bytes 294920 | tf_op jit(solution)/shard_map/ppermute | solution.py:46
  150.0 0.9 slice_add_fusion.15
  151.0 0.9 slice_add_fusion.9
  151.9 3.0 %collective-permute-start.20 = (f32[1,48,512]{2,1,0:T(8,128)S(1)}, f32[1,48,512]{2,1,0:T(8,128)S(1)}, u32[]{:S(2)}, u32[]{:S(2)}) collective-permute-start(f32[1,48,512]{2,1,0:T(8,128)S(1)} %slice_add_fusion.9), channel_id=1, source_target_pairs={{0,16},{2,18},{4,20},{6,22},{8,24},{10,26},{12,28},{14,30},{16,0},... | collective-permute-start | bytes 294920 | tf_op jit(solution)/shard_map/ppermute | solution.py:46
  154.9 2.3 %collective-permute-done.12 = f32[1,48,512]{2,1,0:T(8,128)S(1)} collective-permute-done((f32[1,48,512]{2,1,0:T(8,128)S(1)}, f32[1,48,512]{2,1,0:T(8,128)S(1)}, u32[]{:S(2)}, u32[]{:S(2)}) %collective-permute-start.12) | collective-permute-done | bytes 98336 | tf_op jit(solution)/shard_map/ppermute | solution.py:46
  157.2 0.9 fusion.9
  158.2 2.0 %collective-permute-done.16 = f32[1,48,512]{2,1,0:T(8,128)S(1)} collective-permute-done((f32[1,48,512]{2,1,0:T(8,128)S(1)}, f32[1,48,512]{2,1,0:T(8,128)S(1)}, u32[]{:S(2)}, u32[]{:S(2)}) %collective-permute-start.16) | collective-permute-done | bytes 98336 | tf_op jit(solution)/shard_map/ppermute | solution.py:46
  160.1 0.9 fusion.7
  161.2 0.9 fusion.5
  162.8 1.9 %copy-done.6 = f32[1024,768]{1,0:T(8,128)S(1)} copy-done((f32[1024,768]{1,0:T(8,128)S(1)}, f32[1024,768]{1,0:T(8,128)}, u32[]{:S(2)}) %copy-start.6) | copy-done | bytes 3145752
  164.7 2.1 %query_gradient.1 = f32[192,768]{1,0:T(8,128)} custom-call(f32[10,192]{1,0:T(8,128)S(1)} %dynamic_slice.3.coef_ref, s32[10,192]{1,0:T(8,128)S(1)} %bitcast.19, f32[1024,768]{1,0:T(8,128)S(1)} %copy-done.6), custom_call_target="tpu_custom_call" | custom-call | tf_op jit(solution)/shard_map/query_gradient/pallas_call | solution.py:300
  (91 shorter events, 14.1 us)
Async XLA Ops:
  7.2 155.7 %all-gather.2.cloned.1.call-start = ((), (), s32[]{:S(2)}) async-start(), calls=%async_computation.2 | async-start | bytes 3244032 | tf_op jit(solution)/shard_map/all_gather | solution.py:375
  7.2 25.2 %collective-permute-start = (s32[10,192]{1,0:T(8,128)}, s32[10,192]{1,0:T(8,128)S(1)}, u32[]{:S(2)}, u32[]{:S(2)}) collective-permute-start(s32[10,192]{1,0:T(8,128)} %bitcast.17), channel_id=1, source_target_pairs={{0,1},{1,0},{2,3},{3,2},{4,5},{5,4},{6,7},{7,6},{8,9},{9,8},{10,11... | collective-permute-start | bytes 23048 | tf_op jit(solution)/shard_map/ppermute | solution.py:46
  7.7 1.9 %copy-start.3 = (bf16[64,32,768]{2,1,0:T(8,128)(2,1)S(1)}, bf16[64,32,768]{2,1,0:T(8,128)(2,1)}, u32[]{:S(2)}) copy-start(bf16[64,32,768]{2,1,0:T(8,128)(2,1)} %param.10) | copy-start | bytes 9437188
  9.6 1.7 copy-start.4
  11.3 1.7 copy-start.10
  13.0 15.4 %copy-start.12 = (bf16[192,768]{1,0:T(8,128)(2,1)S(1)}, bf16[192,768]{1,0:T(8,128)(2,1)}, u32[]{:S(2)}) copy-start(bf16[192,768]{1,0:T(8,128)(2,1)} %refs_4_.1) | copy-start | bytes 884740
  25.7 2.6 %copy-start = (bf16[2048,1536]{1,0:T(8,128)(2,1)}, bf16[2048,1536]{1,0:T(8,128)(2,1)S(1)}, u32[]{:S(2)}) copy-start(bf16[2048,1536]{1,0:T(8,128)(2,1)S(1)} %get-tuple-element.29.slope_ref) | copy-start | bytes 18874372
  28.3 3.0 %copy-start.24 = (f32[64,1536]{1,0:T(8,128)}, f32[64,1536]{1,0:T(8,128)S(1)}, u32[]{:S(2)}) copy-start(f32[64,1536]{1,0:T(8,128)S(1)} %get-tuple-element.37) | copy-start | bytes 1179652
  28.3 4.0 %copy-start.30 = (s32[192,10]{0,1:T(8,128)S(1)}, s32[192,10]{0,1:T(8,128)}, u32[]{:S(2)}) copy-start(s32[192,10]{0,1:T(8,128)} %param.9) | copy-start | bytes 23044
  28.3 4.7 %collective-permute-start.1 = (f32[64,768]{1,0:T(8,128)}, f32[64,768]{1,0:T(8,128)}, u32[]{:S(2)}, u32[]{:S(2)}) collective-permute-start(f32[64,768]{1,0:T(8,128)} %get-tuple-element.22.refs_0_), channel_id=1, source_target_pairs={{0,1},{1,0},{2,3},{3,2},{4,5},{5,4},{6,7},{7,6},{8,9},{9,8},{10,11... | collective-permute-start | bytes 589832 | tf_op jit(solution)/shard_map/ppermute | solution.py:46
  29.3 3.8 %collective-permute-start.2 = (f32[192,768]{1,0:T(8,128)}, f32[192,768]{1,0:T(8,128)}, u32[]{:S(2)}, u32[]{:S(2)}) collective-permute-start(f32[192,768]{1,0:T(8,128)} %convert_element_type.7), channel_id=1, source_target_pairs={{0,1},{1,0},{2,3},{3,2},{4,5},{5,4},{6,7},{7,6},{8,9},{9,8},{10,11... | collective-permute-start | bytes 1769480 | tf_op jit(solution)/shard_map/ppermute | solution.py:46
  32.4 35.3 %copy-start.31 = (s32[2]{0:T(128)}, s32[2]{0:T(128)S(1)}, u32[]{:S(2)}) copy-start(s32[2]{0:T(128)S(1)} %pad_add_fusion.1.place_ref) | copy-start | bytes 28
  33.1 3.2 %copy-start.21 = (s32[10,384]{1,0:T(8,128)}, s32[10,384]{1,0:T(8,128)S(1)}, u32[]{:S(2)}) copy-start(s32[10,384]{1,0:T(8,128)S(1)} %get-tuple-element.39.refs_6_.refs_4_.ids_ref) | copy-start | bytes 46084
  33.1 0.9 copy-start.13
  36.3 0.8 copy-start.7
  41.1 42.7 %all-to-all-start = ((f32[16,64,96]{2,1,0:T(8,128)}), f32[16,64,96]{2,1,0:T(8,128)}, u32[]{:S(2)}, u32[]{:S(2)}) async-start(f32[16,64,96]{2,1,0:T(8,128)} %bitcast.20), calls=%async_computation | async-start | bytes 1048576 | tf_op jit(solution)/shard_map/all_to_all | solution.py:377
  49.1 4.7 %collective-permute-start.3 = (f32[10,384]{1,0:T(8,128)S(1)}, f32[10,384]{1,0:T(8,128)S(1)}, u32[]{:S(2)}, u32[]{:S(2)}) collective-permute-start(f32[10,384]{1,0:T(8,128)S(1)} %get-tuple-element.23), channel_id=1, source_target_pairs={{0,2},{2,0},{4,6},{6,4},{8,10},{10,8},{12,14},{14,12},{16,18},{18,... | collective-permute-start | bytes 46088 | tf_op jit(solution)/shard_map/ppermute | solution.py:46
  51.0 4.7 %collective-permute-start.4 = (f32[10,384]{1,0:T(8,128)S(1)}, f32[10,384]{1,0:T(8,128)S(1)}, u32[]{:S(2)}, u32[]{:S(2)}) collective-permute-start(f32[10,384]{1,0:T(8,128)S(1)} %get-tuple-element.23), channel_id=1, source_target_pairs={{0,4},{2,6},{4,0},{6,2},{8,12},{10,14},{12,8},{14,10},{16,20},{18,... | collective-permute-start | bytes 46088 | tf_op jit(solution)/shard_map/ppermute | solution.py:46
  52.5 4.8 %collective-permute-start.5 = (f32[10,384]{1,0:T(8,128)S(1)}, f32[10,384]{1,0:T(8,128)S(1)}, u32[]{:S(2)}, u32[]{:S(2)}) collective-permute-start(f32[10,384]{1,0:T(8,128)S(1)} %get-tuple-element.23), channel_id=1, source_target_pairs={{0,6},{2,4},{4,2},{6,0},{8,14},{10,12},{12,10},{14,8},{16,22},{18,... | collective-permute-start | bytes 46088 | tf_op jit(solution)/shard_map/ppermute | solution.py:46
  57.3 4.5 %collective-permute-start.6 = (f32[10,384]{1,0:T(8,128)S(1)}, f32[10,384]{1,0:T(8,128)S(1)}, u32[]{:S(2)}, u32[]{:S(2)}) collective-permute-start(f32[10,384]{1,0:T(8,128)S(1)} %add_add_fusion.refs_0_), channel_id=1, source_target_pairs={{0,8},{2,10},{4,12},{6,14},{8,0},{10,2},{12,4},{14,6},{16,24},{18,... | collective-permute-start | bytes 46088 | tf_op jit(solution)/shard_map/ppermute | solution.py:46
  58.9 8.8 %collective-permute-start.7 = (f32[10,384]{1,0:T(8,128)S(1)}, f32[10,384]{1,0:T(8,128)S(1)}, u32[]{:S(2)}, u32[]{:S(2)}) collective-permute-start(f32[10,384]{1,0:T(8,128)S(1)} %add_add_fusion.refs_0_), channel_id=1, source_target_pairs={{0,16},{2,18},{4,20},{6,22},{8,24},{10,26},{12,28},{14,30},{16,0},... | collective-permute-start | bytes 46088 | tf_op jit(solution)/shard_map/ppermute | solution.py:46
  61.2 6.5 %collective-permute-start.8 = (f32[10,384]{1,0:T(8,128)S(1)}, f32[10,384]{1,0:T(8,128)S(1)}, u32[]{:S(2)}, u32[]{:S(2)}) collective-permute-start(f32[10,384]{1,0:T(8,128)S(1)} %add_add_fusion.refs_0_), channel_id=1, source_target_pairs={{0,24},{2,26},{4,28},{6,30},{8,16},{10,18},{12,20},{14,22},{16,8},... | collective-permute-start | bytes 46088 | tf_op jit(solution)/shard_map/ppermute | solution.py:46
  67.7 1.7 copy-start.5
  69.3 1.1 copy-start.8
  70.4 0.7 copy-start.22
  71.1 0.6 copy-start.32
  73.0 0.7 copy-start.25
  73.7 0.6 copy-start.27
  74.3 2.8 %copy-start.1 = (bf16[2048,1536]{1,0:T(8,128)(2,1)S(1)}, bf16[2048,1536]{1,0:T(8,128)(2,1)}, u32[]{:S(2)}) copy-start(bf16[2048,1536]{1,0:T(8,128)(2,1)} %copy-done) | copy-start | bytes 18874372
  81.5 0.9 copy-start.15
  82.4 34.2 %collective-permute-start.9 = (f32[8,48,512]{2,1,0:T(8,128)}, f32[8,48,512]{2,1,0:T(8,128)}, u32[]{:S(2)}, u32[]{:S(2)}) collective-permute-start(f32[8,48,512]{2,1,0:T(8,128)} %get-tuple-element.32), channel_id=1, source_target_pairs={{0,2},{2,0},{4,6},{6,4},{8,10},{10,8},{12,14},{14,12},{16,18},{18,... | collective-permute-start | bytes 2359304 | tf_op jit(solution)/shard_map/ppermute | solution.py:46
  83.9 1.1 copy-start.9
  84.9 0.7 copy-start.23
  85.7 0.7 copy-start.28
  91.5 0.8 copy-start.11
  92.3 22.4 %all-to-all-start.1 = ((f32[16,48,96]{2,1,0:T(8,128)}), f32[16,48,96]{2,1,0:T(8,128)}, u32[]{:S(2)}, u32[]{:S(2)}) async-start(f32[16,48,96]{2,1,0:T(8,128)} %copy-done.11), calls=%async_computation.1 | async-start | bytes 786432 | tf_op jit(solution)/shard_map/all_to_all | solution.py:398
  96.7 2.9 %copy-start.2 = (bf16[2048,1536]{1,0:T(8,128)(2,1)S(1)}, bf16[2048,1536]{1,0:T(8,128)(2,1)}, u32[]{:S(2)}) copy-start(bf16[2048,1536]{1,0:T(8,128)(2,1)} %copy-done) | copy-start | bytes 18874372
  103.9 0.9 copy-start.19
  104.8 8.5 %copy-start.35 = (s32[10,384]{1,0:T(8,128)S(1)}, s32[10,384]{1,0:T(8,128)}, u32[]{:S(2)}) copy-start(s32[10,384]{1,0:T(8,128)} %get-tuple-element.38) | copy-start | bytes 46084
  104.8 8.7 %copy-start.29 = (f32[10,384]{1,0:T(8,128)S(1)}, f32[10,384]{1,0:T(8,128)}, u32[]{:S(2)}) copy-start(f32[10,384]{1,0:T(8,128)} %copy-done.27) | copy-start | bytes 46084
  104.8 8.7 %copy-start.14 = (f32[64,768]{1,0:T(8,128)S(1)}, f32[64,768]{1,0:T(8,128)}, u32[]{:S(2)}) copy-start(f32[64,768]{1,0:T(8,128)} %refs_3_.1) | copy-start | bytes 589828
  104.8 8.7 %copy-start.26 = (f32[64,768]{1,0:T(8,128)S(1)}, f32[64,768]{1,0:T(8,128)}, u32[]{:S(2)}) copy-start(f32[64,768]{1,0:T(8,128)} %copy-done.25) | copy-start | bytes 589828
  104.8 8.8 %copy-start.33 = (f32[64,768]{1,0:T(8,128)S(1)}, f32[64,768]{1,0:T(8,128)}, u32[]{:S(2)}) copy-start(f32[64,768]{1,0:T(8,128)} %param.15) | copy-start | bytes 589828
  104.9 8.8 %copy-start.34 = (f32[64,768]{1,0:T(8,128)S(1)}, f32[64,768]{1,0:T(8,128)}, u32[]{:S(2)}) copy-start(f32[64,768]{1,0:T(8,128)} %param.14) | copy-start | bytes 589828
  104.9 22.0 %collective-permute-start.13 = (f32[8,48,512]{2,1,0:T(8,128)}, f32[8,48,512]{2,1,0:T(8,128)}, u32[]{:S(2)}, u32[]{:S(2)}) collective-permute-start(f32[8,48,512]{2,1,0:T(8,128)} %get-tuple-element.34), channel_id=1, source_target_pairs={{0,4},{2,6},{4,0},{6,2},{8,12},{10,14},{12,8},{14,10},{16,20},{18,... | collective-permute-start | bytes 2359304 | tf_op jit(solution)/shard_map/ppermute | solution.py:46
  110.9 0.9 copy-start.17
  111.8 4.8 %copy-start.16 = (f32[8,48,512]{2,1,0:T(8,128)S(1)}, f32[8,48,512]{2,1,0:T(8,128)}, u32[]{:S(2)}) copy-start(f32[8,48,512]{2,1,0:T(8,128)} %copy-done.15) | copy-start | bytes 2359300
  111.8 15.0 %copy-start.20 = (f32[8,48,512]{2,1,0:T(8,128)S(1)}, f32[8,48,512]{2,1,0:T(8,128)}, u32[]{:S(2)}) copy-start(f32[8,48,512]{2,1,0:T(8,128)} %copy-done.19) | copy-start | bytes 2359300
  111.9 18.0 %copy-start.18 = (f32[8,48,512]{2,1,0:T(8,128)S(1)}, f32[8,48,512]{2,1,0:T(8,128)}, u32[]{:S(2)}) copy-start(f32[8,48,512]{2,1,0:T(8,128)} %copy-done.17) | copy-start | bytes 2359300
  111.9 18.0 %collective-permute-start.17 = (f32[8,48,512]{2,1,0:T(8,128)}, f32[8,48,512]{2,1,0:T(8,128)}, u32[]{:S(2)}, u32[]{:S(2)}) collective-permute-start(f32[8,48,512]{2,1,0:T(8,128)} %get-tuple-element.36), channel_id=1, source_target_pairs={{0,8},{2,10},{4,12},{6,14},{8,0},{10,2},{12,4},{14,6},{16,24},{18,... | collective-permute-start | bytes 2359304 | tf_op jit(solution)/shard_map/ppermute | solution.py:46
  117.7 15.6 %collective-permute-start.10 = (f32[4,48,512]{2,1,0:T(8,128)S(1)}, f32[4,48,512]{2,1,0:T(8,128)S(1)}, u32[]{:S(2)}, u32[]{:S(2)}) collective-permute-start(f32[4,48,512]{2,1,0:T(8,128)S(1)} %slice_add_fusion.2), channel_id=1, source_target_pairs={{0,4},{2,6},{4,0},{6,2},{8,12},{10,14},{12,8},{14,10},{16,20},{18,... | collective-permute-start | bytes 1179656 | tf_op jit(solution)/shard_map/ppermute | solution.py:46
  127.9 11.7 %collective-permute-start.14 = (f32[4,48,512]{2,1,0:T(8,128)S(1)}, f32[4,48,512]{2,1,0:T(8,128)S(1)}, u32[]{:S(2)}, u32[]{:S(2)}) collective-permute-start(f32[4,48,512]{2,1,0:T(8,128)S(1)} %slice_add_fusion.1), channel_id=1, source_target_pairs={{0,2},{2,0},{4,6},{6,4},{8,10},{10,8},{12,14},{14,12},{16,18},{18,... | collective-permute-start | bytes 1179656 | tf_op jit(solution)/shard_map/ppermute | solution.py:46
  130.9 12.9 %collective-permute-start.18 = (f32[4,48,512]{2,1,0:T(8,128)S(1)}, f32[4,48,512]{2,1,0:T(8,128)S(1)}, u32[]{:S(2)}, u32[]{:S(2)}) collective-permute-start(f32[4,48,512]{2,1,0:T(8,128)S(1)} %slice_add_fusion), channel_id=1, source_target_pairs={{0,2},{2,0},{4,6},{6,4},{8,10},{10,8},{12,14},{14,12},{16,18},{18,... | collective-permute-start | bytes 1179656 | tf_op jit(solution)/shard_map/ppermute | solution.py:46
  134.3 11.7 %collective-permute-start.11 = (f32[2,48,512]{2,1,0:T(8,128)S(1)}, f32[2,48,512]{2,1,0:T(8,128)S(1)}, u32[]{:S(2)}, u32[]{:S(2)}) collective-permute-start(f32[2,48,512]{2,1,0:T(8,128)S(1)} %slice_add_fusion.7), channel_id=1, source_target_pairs={{0,8},{2,10},{4,12},{6,14},{8,0},{10,2},{12,4},{14,6},{16,24},{18,... | collective-permute-start | bytes 589832 | tf_op jit(solution)/shard_map/ppermute | solution.py:46
  140.5 9.5 %collective-permute-start.15 = (f32[2,48,512]{2,1,0:T(8,128)S(1)}, f32[2,48,512]{2,1,0:T(8,128)S(1)}, u32[]{:S(2)}, u32[]{:S(2)}) collective-permute-start(f32[2,48,512]{2,1,0:T(8,128)S(1)} %slice_add_fusion.5), channel_id=1, source_target_pairs={{0,8},{2,10},{4,12},{6,14},{8,0},{10,2},{12,4},{14,6},{16,24},{18,... | collective-permute-start | bytes 589832 | tf_op jit(solution)/shard_map/ppermute | solution.py:46
  144.7 6.3 %collective-permute-start.19 = (f32[2,48,512]{2,1,0:T(8,128)S(1)}, f32[2,48,512]{2,1,0:T(8,128)S(1)}, u32[]{:S(2)}, u32[]{:S(2)}) collective-permute-start(f32[2,48,512]{2,1,0:T(8,128)S(1)} %slice_add_fusion.3), channel_id=1, source_target_pairs={{0,4},{2,6},{4,0},{6,2},{8,12},{10,14},{12,8},{14,10},{16,20},{18,... | collective-permute-start | bytes 589832 | tf_op jit(solution)/shard_map/ppermute | solution.py:46
  146.9 10.3 %collective-permute-start.12 = (f32[1,48,512]{2,1,0:T(8,128)S(1)}, f32[1,48,512]{2,1,0:T(8,128)S(1)}, u32[]{:S(2)}, u32[]{:S(2)}) collective-permute-start(f32[1,48,512]{2,1,0:T(8,128)S(1)} %slice_add_fusion.21), channel_id=1, source_target_pairs={{0,16},{2,18},{4,20},{6,22},{8,24},{10,26},{12,28},{14,30},{16,0},... | collective-permute-start | bytes 294920 | tf_op jit(solution)/shard_map/ppermute | solution.py:46
  150.9 9.2 %collective-permute-start.16 = (f32[1,48,512]{2,1,0:T(8,128)S(1)}, f32[1,48,512]{2,1,0:T(8,128)S(1)}, u32[]{:S(2)}, u32[]{:S(2)}) collective-permute-start(f32[1,48,512]{2,1,0:T(8,128)S(1)} %slice_add_fusion.15), channel_id=1, source_target_pairs={{0,16},{2,18},{4,20},{6,22},{8,24},{10,26},{12,28},{14,30},{16,0},... | collective-permute-start | bytes 294920 | tf_op jit(solution)/shard_map/ppermute | solution.py:46
  151.9 9.2 %collective-permute-start.20 = (f32[1,48,512]{2,1,0:T(8,128)S(1)}, f32[1,48,512]{2,1,0:T(8,128)S(1)}, u32[]{:S(2)}, u32[]{:S(2)}) collective-permute-start(f32[1,48,512]{2,1,0:T(8,128)S(1)} %slice_add_fusion.9), channel_id=1, source_target_pairs={{0,16},{2,18},{4,20},{6,22},{8,24},{10,26},{12,28},{14,30},{16,0},... | collective-permute-start | bytes 294920 | tf_op jit(solution)/shard_map/ppermute | solution.py:46
  162.8 1.9 %copy-start.6 = (f32[1024,768]{1,0:T(8,128)S(1)}, f32[1024,768]{1,0:T(8,128)}, u32[]{:S(2)}) copy-start(f32[1024,768]{1,0:T(8,128)} %all-gather.2.cloned.1.call-done.label_ref) | copy-start | bytes 9437188
Sparse Core Ops, SparseCore 0:
  37.2 71.9 all-gather.1

commit v3 on v2

v3 whole, which is shorter than its diff:
```python
import functools
import math

import jax
import jax.numpy as jnp
from jax import lax
from jax.experimental import pallas as pl
from jax.experimental.pallas import tpu as pltpu
from jax.sharding import PartitionSpec as P

beta_one = 0.9
beta_two = 0.999
adam_eps = 1e-08
learn_rate = 0.05
first_fix = 1.0 - 0.9**10
second_fix = 1.0 - 0.999**10

PLANE = 4
THIRDS = 3
GELU_ONE = math.sqrt(2.0 / math.pi)
GELU_THREE = GELU_ONE * 0.044715
MIB = 2**20
ENCODE = 28
SCORE = 24
BACKWARD = 32
REST = 24


def whole(shape):
    return pl.BlockSpec(shape, lambda *_: (0,) * len(shape))


def params(mib):
    return pltpu.CompilerParams(vmem_limit_bytes=mib * MIB)


def f32(shape):
    return jax.ShapeDtypeStruct(shape, jnp.float32)


def bf16(shape):
    return jax.ShapeDtypeStruct(shape, jnp.bfloat16)


def pair_swap(values, axis, count, bits):
    return lax.ppermute(values, axis, [(s, s ^ bits) for s in range(count)])


def parity_swap(values, counts, bits):
    label_count, query_count = counts
    return lax.ppermute(
        values,
        ("label", "query"),
        [
            (s * query_count + q, (s ^ bits[q % 2]) * query_count + q)
            for s in range(label_count)
            for q in range(query_count)
        ],
    )


def plane_sum(values, label_count):
    return values + sum(pair_swap(values, "label", label_count, b) for b in range(1, PLANE))


def plane_terms(values, label_count):
    return [values] + [
        pair_swap(values, "label", label_count, b) for b in range(PLANE, label_count, PLANE)
    ]


def bit_orders(label_count):
    bits = [1 << b for b in range(label_count.bit_length() - 1)]
    return [lead + bits[3:] for lead in ([1, 4, 2], [2, 1, 4], [4, 2, 1])]


def relative_shards(label_count, order):
    count = len(order)
    return [
        sum(bit for place, bit in enumerate(order) if p >> (count - 1 - place) & 1)
        for p in range(label_count)
    ]


def upper(parts):
    size = parts[-1].shape[0]
    return sum(p[size // 2 : size] for p in parts)


def scatter_sum(keeps, gives, label_count, before):
    orders = bit_orders(label_count)

    def swap(values, bit):
        return pair_swap(values, "label", label_count, bit)

    thirds = [[keep, swap(give, order[0])] for keep, give, order in zip(keeps, gives, orders)]
    for step in range(1, 3):
        gives = before[step - 1]([upper(parts) for parts in thirds])
        for parts, give, order in zip(thirds, gives, orders):
            parts.append(swap(give, order[step]))
    size = thirds[0][-1].shape[0]
    parts = [jnp.concatenate([sum(p[:size] for p in third) for third in thirds], axis=2)]
    for step in range(3, len(orders[0])):
        give = upper(parts)
        if step == 3:
            (give,) = before[2]([give])
        parts.append(swap(give, orders[0][step]))
    return sum(p[0] for p in parts)


def after(values, *gates):
    return lax.optimization_barrier((values, gates))[0]


def gather_planes(values, label_count):
    return jnp.stack(
        [values]
        + [pair_swap(values, "label", label_count, b) for b in range(PLANE, label_count, PLANE)]
    )


def gather_near(whole_planes, counts):
    return jnp.stack((whole_planes, parity_swap(whole_planes, counts, (1, 2))))


def gather_far(near, counts):
    return jnp.concatenate((near, parity_swap(near, counts, (2, 1))))


def split_bf16(values):
    high = values.astype(jnp.bfloat16)
    low = (values - high.astype(jnp.float32)).astype(jnp.bfloat16)
    return high, low


def gate_of(x):
    square = x * x
    inner = x * (jnp.bfloat16(GELU_ONE) + jnp.bfloat16(GELU_THREE) * square)
    return jnp.bfloat16(0.5) + jnp.bfloat16(0.5) * jnp.tanh(inner), square


def column_steps(cols):
    return 6 if cols % (6 * 128) == 0 else 3


def encode(text_rows, up_weight, down_weight, label_rows, label_count):
    tokens, model_width = text_rows.shape
    unit_cols = up_weight.shape[1]
    text_len = tokens // label_rows
    steps = column_steps(unit_cols)
    chunk = unit_cols // steps
    width = model_width // steps
    share = unit_cols // label_count

    def pool(values):
        values = values.astype(jnp.float32).reshape(label_rows, text_len, values.shape[1])
        return jnp.sum(values, axis=1) * (1.0 / text_len)

    def kernel(
        text_ref,
        up_ref,
        down_ref,
        shares_ref,
        slope_ref,
        turned_ref,
        mean_ref,
        encoded_ref,
        pooled_ref,
    ):
        step = pl.program_id(0)
        x = jnp.dot(text_ref[...], up_ref[...], preferred_element_type=jnp.float32)
        x = x.astype(jnp.bfloat16)
        gate, square = gate_of(x)
        hidden = x * gate
        inner = jnp.bfloat16(2 * GELU_ONE) + jnp.bfloat16(6 * GELU_THREE) * square
        slope_ref[...] = gate + (hidden - hidden * gate) * inner
        pooled_ref[:, pl.ds(pl.multiple_of(step * chunk, chunk), chunk)] = pool(hidden)
        some = text_ref[:, pl.ds(pl.multiple_of(step * width, width), width)]
        turned_ref[...] = some.T
        mean_ref[...] = pool(some)

        @pl.when(step == steps - 1)
        def _():
            pooled = pooled_ref[...]
            for place in range(label_count):
                shares_ref[place] = pooled[:, place * share : (place + 1) * share]
            both = lax.dot_general(
                jnp.concatenate(split_bf16(pooled)),
                down_ref[...],
                (((1,), (1,)), ((), ())),
                preferred_element_type=jnp.float32,
            )
            encoded_ref[...] = both[:label_rows] + both[label_rows:]

    return pl.pallas_call(
        kernel,
        grid=(steps,),
        in_specs=[
            whole(text_rows.shape),
            pl.BlockSpec((model_width, chunk), lambda i: (0, i)),
            whole(down_weight.shape),
        ],
        out_specs=[
            whole((label_count, label_rows, share)),
            pl.BlockSpec((tokens, chunk), lambda i: (0, i)),
            pl.BlockSpec((width, tokens), lambda i: (i, 0)),
            pl.BlockSpec((label_rows, width), lambda i: (0, i)),
            whole((label_rows, model_width)),
        ],
        out_shape=[
            f32((label_count, label_rows, share)),
            bf16((tokens, unit_cols)),
            bf16((model_width, tokens)),
            f32((label_rows, model_width)),
            f32((label_rows, model_width)),
        ],
        scratch_shapes=[pltpu.VMEM((label_rows, unit_cols), jnp.float32)],
        compiler_params=params(ENCODE),
        name="encode",
    )(text_rows, up_weight, down_weight)


def score(encoded, pooled_text, free_vectors, query_pieces, id_pieces, share):
    label_rows, model_width = free_vectors.shape
    choices = id_pieces[0].shape[0]
    total = sum(p.shape[1] for p in id_pieces)
    terms = len(encoded)
    pieces = len(query_pieces)

    def kernel(*refs):
        encoded_refs, refs = refs[:terms], refs[terms:]
        pooled_ref, free_ref, *refs = refs
        query_refs, refs = refs[:pieces], refs[pieces:]
        id_refs, refs = refs[:pieces], refs[pieces:]
        share_ref, every_ref, ids_ref, partial_ref, label_ref = refs
        core = lax.axis_index("query")
        label_vec = pooled_ref[...] + sum(r[...] for r in encoded_refs) + free_ref[...]
        label_bf = label_vec.astype(jnp.bfloat16)
        label_ref[...] = label_bf.astype(jnp.float32)
        share_ref[...] = label_ref[pl.ds(pl.multiple_of(core * share, share), share), :]
        if pieces == 1:
            every_ref[...] = query_refs[0][...].astype(jnp.bfloat16)
            ids_ref[...] = id_refs[0][...]
        else:
            rows = total // 2
            for place, ref in enumerate(query_refs):
                first = pl.multiple_of((core ^ place) * rows, rows)
                every_ref[pl.ds(first, rows), :] = ref[...].astype(jnp.bfloat16)
            own, other = (r[...] for r in id_refs)
            own_first = core == 0
            ids_ref[...] = jnp.concatenate(
                (jnp.where(own_first, own, other), jnp.where(own_first, other, own)), axis=1
            )
        similar = lax.dot_general(
            label_bf, every_ref[...], (((1,), (1,)), ((), ())), preferred_element_type=jnp.float32
        )
        label = lax.broadcasted_iota(jnp.int32, (label_rows, total), 0)
        label = label + lax.axis_index("label") * label_rows
        for k in range(choices):
            partial_ref[k : k + 1, :] = jnp.sum(
                jnp.where(label == ids_ref[k : k + 1, :], similar, 0.0), axis=0, keepdims=True
            )

    return pl.pallas_call(
        kernel,
        out_shape=[
            f32((share, model_width)),
            bf16((total, model_width)),
            jax.ShapeDtypeStruct((choices, total), jnp.int32),
            f32((choices, total)),
        ],
        scratch_shapes=[pltpu.VMEM((label_rows, model_width), jnp.float32)],
        compiler_params=params(SCORE),
        name="score",
    )(*encoded, pooled_text, free_vectors, *query_pieces, *id_pieces)


def spread_of(ids_ref, coef, first, labels):
    choices, total = coef.shape
    label = lax.broadcasted_iota(jnp.int32, (labels, total), 0) + first
    spread = jnp.zeros((labels, total), jnp.float32)
    for k in range(choices):
        spread = jnp.where(label == ids_ref[k : k + 1, :], coef[k : k + 1, :], spread)
    return spread.astype(jnp.bfloat16)


def backward(score_terms, ids, every_query, down_weight, turned, slope, label_rows, label_count):
    choices, total = ids.shape
    model_width, unit_cols = down_weight.shape
    tokens = turned.shape[1]
    text_len = tokens // label_rows
    cols = unit_cols // THIRDS
    own = model_width // label_count
    half = label_count // 2
    terms = len(score_terms)
    temper = 1.0 / math.sqrt(model_width)
    relative = [relative_shards(label_count, order) for order in bit_orders(label_count)]

    def kernel(*refs):
        score_refs, refs = refs[:terms], refs[terms:]
        shard = lax.axis_index("label")
        ids_ref, query_ref, down_ref, *refs = refs
        turned_ref, slope_ref, coef_ref, grad_ref, *refs = refs
        outs, refs = refs[: 2 * THIRDS], refs[2 * THIRDS :]
        blocks_ref, kept_ref, given_ref, out_sem = refs

        scores = sum(r[...] for r in score_refs) * temper
        powers = jnp.exp(scores - jnp.max(scores, axis=0, keepdims=True))
        likely = powers / jnp.sum(powers, axis=0, keepdims=True)
        rank = lax.broadcasted_iota(jnp.int32, (choices, total), 0)
        coef = (likely - jnp.where(rank < 2, 0.5, 0.0)) * temper
        coef = coef.astype(jnp.bfloat16).astype(jnp.float32)
        coef_ref[...] = coef
        spread = spread_of(ids_ref, coef, shard * label_rows, label_rows)
        grad = jnp.dot(spread, query_ref[...], preferred_element_type=jnp.float32)
        grad_ref[...] = grad
        out_grad = grad.astype(jnp.bfloat16)

        flights = []
        for third in range(THIRDS):
            span = slice(third * cols, (third + 1) * cols)
            hidden_grad = jnp.dot(
                out_grad, down_ref[:, span], preferred_element_type=jnp.float32
            ) * (1.0 / text_len)
            preact_grad = (
                slope_ref[:, span].astype(jnp.float32).reshape(label_rows, text_len, cols)
                * hidden_grad[:, None, :]
            )
            up_term = jnp.dot(
                turned_ref[...],
                preact_grad.reshape(tokens, cols).astype(jnp.bfloat16),
                preferred_element_type=jnp.float32,
            )
            for block in range(label_count):
                blocks_ref[block] = up_term[block * own : (block + 1) * own, :]
            for p in range(half):
                given_ref[third, p] = blocks_ref[shard ^ relative[third][half + p]]
                kept_ref[third, p] = blocks_ref[shard ^ relative[third][p]]
            for side, buffer in enumerate((kept_ref, given_ref)):
                place = 2 * third + side
                flight = pltpu.make_async_copy(buffer.at[third], outs[place], out_sem.at[place])
                flight.start()
                flights.append(flight)
        for flight in flights:
            flight.wait()

    outs = pl.pallas_call(
        kernel,
        in_specs=[pl.BlockSpec(memory_space=pltpu.VMEM)] * (terms + 5),
        out_specs=[pl.BlockSpec(memory_space=pltpu.VMEM)] * 2
        + [pl.BlockSpec(memory_space=pl.ANY)] * (2 * THIRDS),
        out_shape=[f32((choices, total)), f32((label_rows, model_width))]
        + [f32((half, own, cols))] * (2 * THIRDS),
        scratch_shapes=[pltpu.VMEM((label_count, own, cols), jnp.float32)]
        + [pltpu.VMEM((THIRDS, half, own, cols), jnp.float32)] * 2
        + [pltpu.SemaphoreType.DMA((2 * THIRDS,))],
        compiler_params=params(BACKWARD),
        cost_estimate=pl.CostEstimate(
            flops=2 * tokens * model_width * unit_cols,
            bytes_accessed=16 * MIB,
            transcendentals=choices * total,
        ),
        name="backward",
    )(*score_terms, ids, every_query, down_weight, turned, slope)
    return outs[0], outs[1], outs[2::2], outs[3::2]


def query_gradient(coef, ids, vectors, label_rows):
    choices, total = ids.shape
    near, planes, share, model_width = vectors.shape
    rows = near * planes * share

    def kernel(coef_ref, ids_ref, vector_ref, out_ref):
        core = lax.axis_index("query")
        row = lax.broadcasted_iota(jnp.int32, (rows, total), 0)
        block = row // share
        plane, place = block % planes, block // planes
        turned = place // 2 + place % 2 * 2
        place = jnp.where(lax.rem(core, 2) == 0, place, turned)
        owner = lax.axis_index("label") ^ (plane * PLANE + place)
        label = owner * label_rows + core * share + row % share
        spread = jnp.zeros((rows, total), jnp.float32)
        for k in range(choices):
            spread = jnp.where(label == ids_ref[k : k + 1, :], coef_ref[k : k + 1, :], spread)
        out_ref[...] = lax.dot_general(
            spread.astype(jnp.bfloat16),
            vector_ref[...].reshape(rows, model_width).astype(jnp.bfloat16),
            (((0,), (0,)), ((), ())),
            preferred_element_type=jnp.float32,
        )

    return pl.pallas_call(
        kernel,
        out_shape=f32((total, model_width)),
        compiler_params=params(REST),
        name="query_gradient",
    )(coef, ids, vectors)


def down_gradient_and_adam(
    coef, ids, every_query, pooled_all, label_grad, free_vectors, moments, seconds, label_count
):
    labels, units = pooled_all.shape
    model_width = every_query.shape[1]
    label_rows = free_vectors.shape[0]
    own = model_width // label_count
    choices, total = ids.shape

    def product(left, right):
        both = lax.dot_general(
            left,
            jnp.concatenate(split_bf16(right), axis=1),
            (((0,), (0,)), ((), ())),
            preferred_element_type=jnp.float32,
        )
        return both[:, :units] + both[:, units:]

    def kernel(
        coef_ref,
        ids_ref,
        query_ref,
        pooled_ref,
        grad_ref,
        free_ref,
        moment_ref,
        second_ref,
        out_ref,
        free_out,
        moment_out,
        second_out,
    ):
        spread = spread_of(ids_ref, coef_ref[...], 0, labels)
        result = product(query_ref[...], product(spread, pooled_ref[...]))
        for block in range(label_count):
            out_ref[block] = result[block * own : (block + 1) * own, :]

        label = lax.broadcasted_iota(jnp.int32, (label_rows, total), 0)
        label = label + lax.axis_index("label") * label_rows
        hits = jnp.zeros((label_rows, total), jnp.float32)
        for k in range(choices):
            hits = jnp.where(label == ids_ref[k : k + 1, :], 1.0, hits)
        touched = jnp.max(hits, axis=1, keepdims=True) > 0.5
        grad, free, moment, second = (r[...] for r in (grad_ref, free_ref, moment_ref, second_ref))
        moment_step = beta_one * moment + (1.0 - beta_one) * grad
        second_step = beta_two * second + (1.0 - beta_two) * grad * grad
        update = (
            learn_rate
            * (moment_step / first_fix)
            / (jnp.sqrt(second_step / second_fix) + adam_eps)
        )
        free_out[...] = jnp.where(touched, free - update, free)
        moment_out[...] = jnp.where(touched, moment_step, moment)
        second_out[...] = jnp.where(touched, second_step, second)

    return pl.pallas_call(
        kernel,
        out_shape=[f32((label_count, own, units))] + [f32(free_vectors.shape)] * 3,
        compiler_params=params(REST),
        name="down_gradient_and_adam",
    )(coef, ids, every_query, pooled_all, label_grad, free_vectors, moments, seconds)


def body(
    label_count,
    query_count,
    queries,
    label_ids,
    label_text,
    up_weight,
    down_weight,
    free_vectors,
    moments,
    seconds,
):
    label_rows, text_len, model_width = label_text.shape
    query_rows = queries.shape[0]
    unit_cols = up_weight.shape[1]
    labels = label_count * label_rows
    share = label_rows // query_count

    text_rows = label_text.reshape(label_rows * text_len, model_width)
    ids = label_ids.T
    wide_queries = queries.astype(jnp.float32)
    pooled_shares, slope, turned, pooled_text, encoded_part = encode(
        text_rows, up_weight, down_weight, label_rows, label_count
    )
    if query_count == 2:
        encoded = [encoded_part, pair_swap(encoded_part, "query", 2, 1)]
        query_pieces = [queries, pair_swap(wide_queries, "query", 2, 1)]
        id_pieces = [ids, pair_swap(ids, "query", 2, 1)]
    else:
        encoded = [lax.psum(encoded_part, "query")]
        query_pieces = [lax.all_gather(wide_queries, "query", tiled=True)]
        id_pieces = [lax.all_gather(ids, "query", axis=1, tiled=True)]

    own_share, every_query, ids, partial = score(
        encoded, pooled_text, free_vectors, query_pieces, id_pieces, share
    )

    counts = (label_count, query_count)
    tied = lax.optimization_barrier
    score_terms = plane_terms(plane_sum(partial, label_count), label_count)
    vectors = gather_planes(own_share, label_count)
    score_terms, vectors = tied((score_terms, vectors))
    vectors = gather_near(vectors, counts)

    coef, label_grad, keeps, gives = backward(
        score_terms, ids, every_query, down_weight, turned, slope, label_rows, label_count
    )

    gives, vectors = tied((gives, vectors))
    pooled_all = lax.all_to_all(after(pooled_shares, gives), "label", 0, 0)
    given = [gives]
    late = [pooled_all]

    def second_step(gives):
        *gives, late[0] = tied((*gives, late[0]))
        given.append(gives)
        return gives

    def third_step(gives):
        given.append(gives)
        return gives

    def fourth_step(gives):
        given.append(gives)
        return gives

    up_grad = scatter_sum(keeps, gives, label_count, (second_step, third_step, fourth_step))

    vectors = gather_far(after(vectors, given[2]), counts)
    down_cols, free_new, moments_new, seconds_new = down_gradient_and_adam(
        coef,
        ids,
        every_query,
        after(late[0], given[1]).reshape(labels, unit_cols // label_count),
        label_grad,
        free_vectors,
        moments,
        seconds,
        label_count,
    )
    down_rows = lax.all_to_all(after(down_cols, given[1]), "label", 0, 0)
    query_terms = query_gradient(coef, ids, vectors, label_rows)
    down_grad = down_rows.swapaxes(0, 1).reshape(model_width // label_count, unit_cols)
    core = lax.axis_index("query")
    if query_count == 2:
        query_terms = query_terms.reshape(2, query_rows, model_width)
        query_grad = lax.dynamic_index_in_dim(query_terms, core, keepdims=False) + pair_swap(
            lax.dynamic_index_in_dim(query_terms, 1 - core, keepdims=False), "query", 2, 1
        )
    else:
        query_grad = lax.dynamic_slice_in_dim(
            lax.psum(query_terms, "query"), core * query_rows, query_rows
        )
    return (free_new, moments_new, seconds_new, query_grad, up_grad, down_grad)


def solution(mesh):
    placed = (
        P("query", None),
        P("query", None),
        P("label", None, None),
        P(None, "query"),
        P(None, "query"),
        P("label", None),
        P("label", None),
        P("label", None),
    )
    return jax.shard_map(
        functools.partial(body, mesh.shape["label"], mesh.shape["query"]),
        mesh=mesh,
        in_specs=placed,
        out_specs=(
            P("label", None),
            P("label", None),
            P("label", None),
            P("query", None),
            P("label", "query"),
            P("label", "query"),
        ),
        check_vma=False,
    )
```

time: 175 us -> 120 us (0.69)
  local copies, waits for them, and re-layouts: 34.6 us -> 10.7 us
  between operations: 14.2 us -> 0.87 us
  Pallas kernels: 36.7 us -> 23.6 us
  waiting for transfers between devices: 29.9 us -> 25.3 us
    unnamed x72 -> x30, local copies, waits for them, and re-layouts: 28.6 us -> 7.92 us
    pallas_call x8 -> x5, Pallas kernels: 36.7 us -> 23.6 us  [the longest x1 11 us: encode(): pl.pallas_call(kernel, grid=(steps,), in_specs=[whole(text_rows.shape), p...]
    ppermute x21 -> x23, waiting for transfers between devices: 29.9 us -> 19.5 us  [pair_swap(): return lax.ppermute(values, axis, [(s, s ^ bits) for s in range(count)])]
    reshape x3 -> x1, local copies, waits for them, and re-layouts: 4.93 us -> 0.89 us  [body(): down_rows.swapaxes(0, 1).reshape(model_width // label_count, unit_cols)]
    add x10 -> x11, other arithmetic: 8.85 us -> 12.8 us  [the longest x6 8.67 us: upper(): return sum((p[size // 2:size] for p in parts))]
    ppermute x0 -> x2, waiting for transfers between devices: none -> 3.52 us  [parity_swap(): lax.ppermute(values, ('label', 'query'), [(s * query_count + q, (s ^ bits...]
    all_to_all x2, starting transfers between devices: 12.4 us -> 10.1 us  [the longest x1 5.21 us: body(): pooled_all = lax.all_to_all(after(pooled_shares, gives), 'label', 0, 0)]
    all_to_all x2, waiting for transfers between devices: 0.01 us -> 2.24 us  [the longest x1 2.23 us: body(): pooled_all = lax.all_to_all(after(pooled_shares, gives), 'label', 0, 0)]
  transfers between devices with their start and end apart: 24 -> 27, of which waited for: 12 -> 10; matrix products, arithmetic and copies ran while one was open for 14% -> 14% of each run, Pallas kernels for 19% -> 19%
where the time goes in v3:
time: 120 us; the launch traced here: 119 us
  starting transfers between devices  42 us (35%)
  waiting for transfers between devices  25.3 us (21%)
  Pallas kernels  23.6 us (20%)
  other arithmetic  16.7 us (14%)
  local copies, waits for them, and re-layouts  10.7 us (9%)
    ppermute x23, starting transfers between devices, pair_swap(): return lax.ppermute(values, axis, [(s, s ^ bits) for s in range(count)])  29.8 us
    ppermute x23, waiting for transfers between devices, pair_swap(): return lax.ppermute(values, axis, [(s, s ^ bits) for s in range(count)])  19.5 us
    pallas_call x1, Pallas kernels, encode(): pl.pallas_call(kernel, grid=(steps,), in_specs=[whole(text_rows.shape), p...  11 us
    add x6, other arithmetic, upper(): return sum((p[size // 2:size] for p in parts))  8.67 us
    pallas_call x1, Pallas kernels, backward(): pl.pallas_call(kernel, in_specs=[pl.BlockSpec(memory_space=pltpu.VMEM)] *...  7.93 us
    unnamed x30, local copies, waits for them, and re-layouts  7.92 us
    all_to_all x1, starting transfers between devices, body(): pooled_all = lax.all_to_all(after(pooled_shares, gives), 'label', 0, 0)  5.21 us
    all_to_all x1, starting transfers between devices, body(): down_rows = lax.all_to_all(after(down_cols, given[1]), 'label', 0, 0)  4.89 us
  transfers between devices with their start and end apart: 27, of which 10 were waited for; matrix products, arithmetic and copies ran while one was open for 14% of the time, Pallas kernels for 19%

profile of v3, /device:TPU:0, one launch (start us, length us, event | category | flops | bytes accessed | tf_op | source)
XLA Modules:
  0.0 119.2 jit_solution(12352063714333462211)
XLA Ops:
  0.6 1.0 convert_element_type.3
  1.6 0.5 collective-permute-start.1
  2.2 1.9 %copy-done = bf16[64,32,768]{2,1,0:T(8,128)(2,1)S(1)} copy-done((bf16[64,32,768]{2,1,0:T(8,128)(2,1)S(1)}, bf16[64,32,768]{2,1,0:T(8,128)(2,1)}, u32[]{:S(2)}) %copy-start) | copy-done | bytes 3145752
  4.0 1.7 %copy-done.1 = bf16[768,1536]{1,0:T(8,128)(2,1)S(1)} copy-done((bf16[768,1536]{1,0:T(8,128)(2,1)S(1)}, bf16[768,1536]{1,0:T(8,128)(2,1)}, u32[]{:S(2)}) %copy-start.1) | copy-done | bytes 2359320
  5.7 1.7 %copy-done.2 = bf16[768,1536]{1,0:T(8,128)(2,1)S(1)} copy-done((bf16[768,1536]{1,0:T(8,128)(2,1)S(1)}, bf16[768,1536]{1,0:T(8,128)(2,1)}, u32[]{:S(2)}) %copy-start.2) | copy-done | bytes 2359320
  7.4 11.0 %encode.1 = (f32[16,64,96]{2,1,0:T(8,128)S(1)}, bf16[2048,1536]{1,0:T(8,128)(2,1)S(1)}, bf16[768,2048]{1,0:T(8,128)(2,1)S(1)}, f32[64,768]{1,0:T(8,128)S(1)}, f32[64,768]{1,0:T(8,128)S(1)}) custom-call(bf16[2048,768]{1,0:T(8,128)(2,1)S(1)} %bitcast.19, bf16[768,1536]{1,0:T(8,128)(2,1)S(1)} %copy-done.1, bf16[768,1536]{1,0:T(8,128)(2,1)S(1)} %copy-done.2), custom_call_target="tpu_custom_call" | custom-call | tf_op jit(solution)/shard_map/encode/pallas_call | solution.py:195
  18.4 0.0 copy-start.3
  18.4 0.1 collective-permute-start
  18.5 0.5 collective-permute-start.2
  19.0 1.0 collective-permute-done.2.refs_7_
  20.0 0.4 score.1
  20.4 3.7 %collective-permute-start.5 = (f32[10,384]{1,0:T(8,128)S(1)}, f32[10,384]{1,0:T(8,128)S(1)}, u32[]{:S(2)}, u32[]{:S(2)}) collective-permute-start(f32[10,384]{1,0:T(8,128)S(1)} %get-tuple-element.46), channel_id=1, source_target_pairs={{0,6},{2,4},{4,2},{6,0},{8,14},{10,12},{12,10},{14,8},{16,22},{18,... | collective-permute-start | bytes 46088 | tf_op jit(solution)/shard_map/ppermute | solution.py:46
  24.2 0.5 collective-permute-start.3
  24.7 0.1 collective-permute-start.4
  24.8 4.0 %collective-permute-start.11 = (f32[32,768]{1,0:T(8,128)S(1)}, f32[32,768]{1,0:T(8,128)S(1)}, u32[]{:S(2)}, u32[]{:S(2)}) collective-permute-start(f32[32,768]{1,0:T(8,128)S(1)} %get-tuple-element.47), channel_id=1, source_target_pairs={{0,24},{2,26},{4,28},{6,30},{8,16},{10,18},{12,20},{14,22},{16,8},... | collective-permute-start | bytes 294920 | tf_op jit(solution)/shard_map/ppermute | solution.py:46
  28.8 0.6 collective-permute-start.9
  29.4 1.5 %collective-permute-start.6 = (f32[10,384]{1,0:T(8,128)S(1)}, f32[10,384]{1,0:T(8,128)S(1)}, u32[]{:S(2)}, u32[]{:S(2)}) collective-permute-start(f32[10,384]{1,0:T(8,128)S(1)} %add_add_fusion.refs_0_), channel_id=1, source_target_pairs={{0,8},{2,10},{4,12},{6,14},{8,0},{10,2},{12,4},{14,6},{16,24},{18,... | collective-permute-start | bytes 46088 | tf_op jit(solution)/shard_map/ppermute | solution.py:46
  30.9 2.9 %collective-permute-start.7 = (f32[10,384]{1,0:T(8,128)S(1)}, f32[10,384]{1,0:T(8,128)S(1)}, u32[]{:S(2)}, u32[]{:S(2)}) collective-permute-start(f32[10,384]{1,0:T(8,128)S(1)} %add_add_fusion.refs_0_), channel_id=1, source_target_pairs={{0,16},{2,18},{4,20},{6,22},{8,24},{10,26},{12,28},{14,30},{16,0},... | collective-permute-start | bytes 46088 | tf_op jit(solution)/shard_map/ppermute | solution.py:46
  33.8 2.5 %collective-permute-start.8 = (f32[10,384]{1,0:T(8,128)S(1)}, f32[10,384]{1,0:T(8,128)S(1)}, u32[]{:S(2)}, u32[]{:S(2)}) collective-permute-start(f32[10,384]{1,0:T(8,128)S(1)} %add_add_fusion.refs_0_), channel_id=1, source_target_pairs={{0,24},{2,26},{4,28},{6,30},{8,16},{10,18},{12,20},{14,22},{16,8},... | collective-permute-start | bytes 46088 | tf_op jit(solution)/shard_map/ppermute | solution.py:46
  36.3 1.7 %collective-permute-done.10 = f32[32,768]{1,0:T(8,128)S(1)} collective-permute-done((f32[32,768]{1,0:T(8,128)S(1)}, f32[32,768]{1,0:T(8,128)S(1)}, u32[]{:S(2)}, u32[]{:S(2)}) %collective-permute-start.10) | collective-permute-done | bytes 98336 | tf_op jit(solution)/shard_map/ppermute | solution.py:46
  38.0 0.2 collective-permute-done.7.refs_2_
  38.3 1.2 %collective-permute-done.8.refs_3_ = f32[10,384]{1,0:T(8,128)S(1)} collective-permute-done((f32[10,384]{1,0:T(8,128)S(1)}, f32[10,384]{1,0:T(8,128)S(1)}, u32[]{:S(2)}, u32[]{:S(2)}) %collective-permute-start.8) | collective-permute-done | bytes 15392 | tf_op jit(solution)/shard_map/ppermute | solution.py:46
  39.5 1.5 %collective-permute-start.12 = (f32[4,32,768]{2,1,0:T(8,128)S(1)}, f32[4,32,768]{2,1,0:T(8,128)S(1)}, u32[]{:S(2)}, u32[]{:S(2)}) collective-permute-start(f32[4,32,768]{2,1,0:T(8,128)S(1)} %pad_maximum_fusion.3), channel_id=1, source_target_pairs={{0,2},{1,5},{2,0},{3,7},{4,6},{5,1},{6,4},{7,3},{8,10},{9,13},{10,... | collective-permute-start | bytes 1179656 | tf_op jit(solution)/shard_map/ppermute | solution.py:51
  41.0 7.9 %backward.1 = (f32[10,384]{1,0:T(8,128)S(1)}, f32[64,768]{1,0:T(8,128)S(1)}, f32[8,48,512]{2,1,0:T(8,128)S(1)}, f32[8,48,512]{2,1,0:T(8,128)}, f32[8,48,512]{2,1...) custom-call(f32[10,384]{1,0:T(8,128)S(1)} %add_add_fusion.refs_0_, ...), custom_call_target="tpu_custom_call" | custom-call | flops 4831838208 | bytes 16777216 | tf_op jit(solution)/shard_map/backward/pallas_call | solution.py:347
  48.9 0.7 copy-done.11
  49.6 1.0 pad_maximum_fusion.1
  50.6 0.5 collective-permute-start.13
  51.1 1.5 %collective-permute-start.14 = (f32[8,48,512]{2,1,0:T(8,128)}, f32[8,48,512]{2,1,0:T(8,128)}, u32[]{:S(2)}, u32[]{:S(2)}) collective-permute-start(f32[8,48,512]{2,1,0:T(8,128)} %get-tuple-element.64), channel_id=1, source_target_pairs={{0,4},{2,6},{4,0},{6,2},{8,12},{10,14},{12,8},{14,10},{16,20},{18,... | collective-permute-start | bytes 2359304 | tf_op jit(solution)/shard_map/ppermute | solution.py:46
  52.6 1.1 collective-permute-start.15
  53.8 5.2 %all-to-all-start = ((f32[16,64,96]{2,1,0:T(8,128)}), f32[16,64,96]{2,1,0:T(8,128)S(1)}, u32[]{:S(2)}, u32[]{:S(2)}) async-start(f32[16,64,96]{2,1,0:T(8,128)} %copy-done.8), calls=%async_computation | async-start | bytes 1048576 | tf_op jit(solution)/shard_map/all_to_all | solution.py:512
  59.0 12.0 %collective-permute-done.13 = f32[8,48,512]{2,1,0:T(8,128)} collective-permute-done((f32[8,48,512]{2,1,0:T(8,128)}, f32[8,48,512]{2,1,0:T(8,128)}, u32[]{:S(2)}, u32[]{:S(2)}) %collective-permute-start.13) | collective-permute-done | bytes 786464 | tf_op jit(solution)/shard_map/ppermute | solution.py:46
  71.0 1.9 %slice_add_fusion.2 = f32[4,48,512]{2,1,0:T(8,128)} fusion(f32[8,48,512]{2,1,0:T(8,128)} %collective-permute-done.13, f32[8,48,512]{2,1,0:T(8,128)S(1)} %get-tuple-element.57), kind=kLoop, calls=%fused_computation.7 | loop fusion | flops 98304 | bytes 1179648 | tf_op jit(solution)/shard_map/add | solution.py:87
  72.8 1.8 %slice_add_fusion.1 = f32[4,48,512]{2,1,0:T(8,128)} fusion(f32[8,48,512]{2,1,0:T(8,128)} %collective-permute-done.14, f32[8,48,512]{2,1,0:T(8,128)S(1)} %get-tuple-element.63), kind=kLoop, calls=%fused_computation.6 | loop fusion | flops 98304 | bytes 1179648 | tf_op jit(solution)/shard_map/add | solution.py:87
  74.6 0.6 collective-permute-done.15
  75.2 1.8 %slice_add_fusion = f32[4,48,512]{2,1,0:T(8,128)} fusion(f32[8,48,512]{2,1,0:T(8,128)} %collective-permute-done.15, f32[8,48,512]{2,1,0:T(8,128)S(1)} %get-tuple-element.65), kind=kLoop, calls=%fused_computation.5 | loop fusion | flops 98304 | bytes 1179648 | tf_op jit(solution)/shard_map/add | solution.py:87
  77.0 2.2 %all-to-all-done = f32[16,64,96]{2,1,0:T(8,128)S(1)} async-done(((f32[16,64,96]{2,1,0:T(8,128)}), f32[16,64,96]{2,1,0:T(8,128)S(1)}, u32[]{:S(2)}, u32[]{:S(2)}) %all-to-all-start) | async-done | bytes 393248 | tf_op jit(solution)/shard_map/all_to_all | solution.py:512
  79.2 1.0 collective-permute-start.17
  80.3 0.7 collective-permute-start.16
  81.0 1.1 copy-done.7
  82.1 0.9 copy-done.12
  83.0 3.1 %down_gradient_and_adam.1 = (f32[16,48,96]{2,1,0:T(8,128)}, f32[64,768]{1,0:T(8,128)}, f32[64,768]{1,0:T(8,128)}, f32[64,768]{1,0:T(8,128)}) custom-call(f32[10,384]{1,0:T(8,128)S(1)} %get-tuple-element.56.coef_ref, s32[10,384]{1,0:T(8,128)S(1)} %get-tuple-element.52.refs_4_.ids_ref, bf16[384,768]{1,0:T(8,128)(2,1)S(1)} %copy-done.7, ...), custom_call_target="tpu_custom_call" | custom-call | tf_op jit(solution)/shard_map/down_gradient_and_adam/pallas_call | solution.py:455
  86.1 4.9 %all-to-all-start.1 = ((f32[16,48,96]{2,1,0:T(8,128)}), f32[16,48,96]{2,1,0:T(8,128)}, u32[]{:S(2)}, u32[]{:S(2)}) async-start(f32[16,48,96]{2,1,0:T(8,128)} %get-tuple-element.81), calls=%async_computation.1 | async-start | bytes 786432 | tf_op jit(solution)/shard_map/all_to_all | solution.py:543
  91.0 1.1 slice_add_fusion.10
  92.0 1.9 %collective-permute-start.23 = (f32[2,48,512]{2,1,0:T(8,128)S(1)}, f32[2,48,512]{2,1,0:T(8,128)S(1)}, u32[]{:S(2)}, u32[]{:S(2)}) collective-permute-start(f32[2,48,512]{2,1,0:T(8,128)S(1)} %slice_add_fusion.10), channel_id=1, source_target_pairs={{0,2},{2,0},{4,6},{6,4},{8,10},{10,8},{12,14},{14,12},{16,18},{18,... | collective-permute-start | bytes 589832 | tf_op jit(solution)/shard_map/ppermute | solution.py:46
  94.0 1.1 slice_add_fusion.12
  95.0 1.5 %collective-permute-start.22 = (f32[2,48,512]{2,1,0:T(8,128)S(1)}, f32[2,48,512]{2,1,0:T(8,128)S(1)}, u32[]{:S(2)}, u32[]{:S(2)}) collective-permute-start(f32[2,48,512]{2,1,0:T(8,128)S(1)} %slice_add_fusion.12), channel_id=1, source_target_pairs={{0,8},{2,10},{4,12},{6,14},{8,0},{10,2},{12,4},{14,6},{16,24},{18,... | collective-permute-start | bytes 589832 | tf_op jit(solution)/shard_map/ppermute | solution.py:46
  96.6 1.1 slice_add_fusion.14
  97.6 1.5 %collective-permute-start.21 = (f32[2,48,512]{2,1,0:T(8,128)S(1)}, f32[2,48,512]{2,1,0:T(8,128)S(1)}, u32[]{:S(2)}, u32[]{:S(2)}) collective-permute-start(f32[2,48,512]{2,1,0:T(8,128)S(1)} %slice_add_fusion.14), channel_id=1, source_target_pairs={{0,4},{2,6},{4,0},{6,2},{8,12},{10,14},{12,8},{14,10},{16,20},{18,... | collective-permute-start | bytes 589832 | tf_op jit(solution)/shard_map/ppermute | solution.py:46
  99.2 0.6 collective-permute-start.19
  99.7 1.6 %collective-permute-done.23 = f32[2,48,512]{2,1,0:T(8,128)S(1)} collective-permute-done((f32[2,48,512]{2,1,0:T(8,128)S(1)}, f32[2,48,512]{2,1,0:T(8,128)S(1)}, u32[]{:S(2)}, u32[]{:S(2)}) %collective-permute-start.23) | collective-permute-done | bytes 196640 | tf_op jit(solution)/shard_map/ppermute | solution.py:46
  101.4 1.1 fusion.1
  102.5 1.1 fusion.2
  103.6 1.1 fusion.3
  104.7 0.7 slice.120
  105.5 2.8 %collective-permute-start.24 = (f32[1,48,1536]{2,1,0:T(8,128)}, f32[1,48,1536]{2,1,0:T(8,128)}, u32[]{:S(2)}, u32[]{:S(2)}) collective-permute-start(f32[1,48,1536]{2,1,0:T(8,128)} %slice.120), channel_id=1, source_target_pairs={{0,16},{2,18},{4,20},{6,22},{8,24},{10,26},{12,28},{14,30},{16,0},... | collective-permute-start | bytes 884744 | tf_op jit(solution)/shard_map/ppermute | solution.py:46
  108.3 3.5 %collective-permute-done.19 = f32[2,4,32,768]{3,2,1,0:T(8,128)S(1)} collective-permute-done((f32[2,4,32,768]{3,2,1,0:T(8,128)S(1)}, f32[2,4,32,768]{3,2,1,0:T(8,128)S(1)}, u32[]{:S(2)}, u32[]{:S(2)}) %collective-permute-start.19) | collective-permute-done | bytes 786464 | tf_op jit(solution)/shard_map/ppermute | solution.py:51
  111.8 0.1 pad_maximum_fusion.vector_ref
  111.9 1.2 query_gradient.1
  113.2 0.1 collective-permute-start.20
  113.3 1.1 copy.14
  114.4 0.9 reshape.28
  115.3 1.3 %collective-permute-done.24 = f32[1,48,1536]{2,1,0:T(8,128)} collective-permute-done((f32[1,48,1536]{2,1,0:T(8,128)}, f32[1,48,1536]{2,1,0:T(8,128)}, u32[]{:S(2)}, u32[]{:S(2)}) %collective-permute-start.24) | collective-permute-done | bytes 294944 | tf_op jit(solution)/shard_map/ppermute | solution.py:46
  116.6 1.7 %fusion = f32[48,1536]{1,0:T(8,128)} fusion(f32[1,48,1536]{2,1,0:T(8,128)} %collective-permute-done.24, f32[2,48,1536]{2,1,0:T(8,128)S(1)} %pad_maximum_fusion.2), kind=kLoop, calls=%fused_computation.10 | loop fusion | flops 73728 | bytes 884736 | tf_op jit(solution)/shard_map/add | solution.py:108
  118.3 0.9 bitcast_add_fusion
  (46 shorter events, 0.2 us)
Async XLA Ops:
  1.6 18.3 %collective-permute-start.1 = (f32[192,768]{1,0:T(8,128)S(1)}, f32[192,768]{1,0:T(8,128)S(1)}, u32[]{:S(2)}, u32[]{:S(2)}) collective-permute-start(f32[192,768]{1,0:T(8,128)S(1)} %convert_element_type.3), channel_id=1, source_target_pairs={{0,1},{1,0},{2,3},{3,2},{4,5},{5,4},{6,7},{7,6},{8,9},{9,8},{10,11... | collective-permute-start | bytes 1769480 | tf_op jit(solution)/shard_map/ppermute | solution.py:46
  2.2 1.9 %copy-start = (bf16[64,32,768]{2,1,0:T(8,128)(2,1)S(1)}, bf16[64,32,768]{2,1,0:T(8,128)(2,1)}, u32[]{:S(2)}) copy-start(bf16[64,32,768]{2,1,0:T(8,128)(2,1)} %param.10) | copy-start | bytes 9437188
  4.0 1.7 %copy-start.1 = (bf16[768,1536]{1,0:T(8,128)(2,1)S(1)}, bf16[768,1536]{1,0:T(8,128)(2,1)}, u32[]{:S(2)}) copy-start(bf16[768,1536]{1,0:T(8,128)(2,1)} %up_ref.1) | copy-start | bytes 7077892
  5.7 1.7 %copy-start.2 = (bf16[768,1536]{1,0:T(8,128)(2,1)S(1)}, bf16[768,1536]{1,0:T(8,128)(2,1)}, u32[]{:S(2)}) copy-start(bf16[768,1536]{1,0:T(8,128)(2,1)} %refs_6_.1) | copy-start | bytes 7077892
  7.4 11.1 %copy-start.13 = (s32[192,10]{0,1:T(8,128)S(1)}, s32[192,10]{0,1:T(8,128)}, u32[]{:S(2)}) copy-start(s32[192,10]{0,1:T(8,128)} %param.9) | copy-start | bytes 23044
  7.4 12.6 %copy-start.4 = (bf16[192,768]{1,0:T(8,128)(2,1)S(1)}, bf16[192,768]{1,0:T(8,128)(2,1)}, u32[]{:S(2)}) copy-start(bf16[192,768]{1,0:T(8,128)(2,1)} %refs_4_.1) | copy-start | bytes 884740
  7.4 12.6 %copy-start.5 = (f32[64,768]{1,0:T(8,128)S(1)}, f32[64,768]{1,0:T(8,128)}, u32[]{:S(2)}) copy-start(f32[64,768]{1,0:T(8,128)} %free_ref.1) | copy-start | bytes 589828
  18.4 22.6 %copy-start.8 = (f32[16,64,96]{2,1,0:T(8,128)}, f32[16,64,96]{2,1,0:T(8,128)S(1)}, u32[]{:S(2)}) copy-start(f32[16,64,96]{2,1,0:T(8,128)S(1)} %get-tuple-element.68) | copy-start | bytes 1179652
  18.4 22.6 %copy-start.3 = (bf16[768,1536]{1,0:T(8,128)(2,1)S(1)}, bf16[768,1536]{1,0:T(8,128)(2,1)}, u32[]{:S(2)}) copy-start(bf16[768,1536]{1,0:T(8,128)(2,1)} %refs_6_.1) | copy-start | bytes 7077892
  18.4 1.5 %collective-permute-start = (f32[64,768]{1,0:T(8,128)S(1)}, f32[64,768]{1,0:T(8,128)S(1)}, u32[]{:S(2)}, u32[]{:S(2)}) collective-permute-start(f32[64,768]{1,0:T(8,128)S(1)} %get-tuple-element.44.refs_0_), channel_id=1, source_target_pairs={{0,1},{1,0},{2,3},{3,2},{4,5},{5,4},{6,7},{7,6},{8,9},{9,8},{10,11... | collective-permute-start | bytes 589832 | tf_op jit(solution)/shard_map/ppermute | solution.py:46
  18.5 1.4 %collective-permute-start.2 = (s32[10,192]{1,0:T(8,128)S(1)}, s32[10,192]{1,0:T(8,128)S(1)}, u32[]{:S(2)}, u32[]{:S(2)}) collective-permute-start(s32[10,192]{1,0:T(8,128)S(1)} %bitcast.22), channel_id=1, source_target_pairs={{0,1},{1,0},{2,3},{3,2},{4,5},{5,4},{6,7},{7,6},{8,9},{9,8},{10,11... | collective-permute-start | bytes 23048 | tf_op jit(solution)/shard_map/ppermute | solution.py:46
  20.4 28.5 %copy-start.6 = (bf16[384,768]{1,0:T(8,128)(2,1)}, bf16[384,768]{1,0:T(8,128)(2,1)S(1)}, u32[]{:S(2)}) copy-start(bf16[384,768]{1,0:T(8,128)(2,1)S(1)} %get-tuple-element.53.refs_5_.query_ref) | copy-start | bytes 1769476
  20.4 8.4 %collective-permute-start.5 = (f32[10,384]{1,0:T(8,128)S(1)}, f32[10,384]{1,0:T(8,128)S(1)}, u32[]{:S(2)}, u32[]{:S(2)}) collective-permute-start(f32[10,384]{1,0:T(8,128)S(1)} %get-tuple-element.46), channel_id=1, source_target_pairs={{0,6},{2,4},{4,2},{6,0},{8,14},{10,12},{12,10},{14,8},{16,22},{18,... | collective-permute-start | bytes 46088 | tf_op jit(solution)/shard_map/ppermute | solution.py:46
  24.2 5.2 %collective-permute-start.3 = (f32[10,384]{1,0:T(8,128)S(1)}, f32[10,384]{1,0:T(8,128)S(1)}, u32[]{:S(2)}, u32[]{:S(2)}) collective-permute-start(f32[10,384]{1,0:T(8,128)S(1)} %get-tuple-element.46), channel_id=1, source_target_pairs={{0,2},{2,0},{4,6},{6,4},{8,10},{10,8},{12,14},{14,12},{16,18},{18,... | collective-permute-start | bytes 46088 | tf_op jit(solution)/shard_map/ppermute | solution.py:46
  24.7 4.7 %collective-permute-start.4 = (f32[10,384]{1,0:T(8,128)S(1)}, f32[10,384]{1,0:T(8,128)S(1)}, u32[]{:S(2)}, u32[]{:S(2)}) collective-permute-start(f32[10,384]{1,0:T(8,128)S(1)} %get-tuple-element.46), channel_id=1, source_target_pairs={{0,4},{2,6},{4,0},{6,2},{8,12},{10,14},{12,8},{14,10},{16,20},{18,... | collective-permute-start | bytes 46088 | tf_op jit(solution)/shard_map/ppermute | solution.py:46
  24.8 9.1 %collective-permute-start.11 = (f32[32,768]{1,0:T(8,128)S(1)}, f32[32,768]{1,0:T(8,128)S(1)}, u32[]{:S(2)}, u32[]{:S(2)}) collective-permute-start(f32[32,768]{1,0:T(8,128)S(1)} %get-tuple-element.47), channel_id=1, source_target_pairs={{0,24},{2,26},{4,28},{6,30},{8,16},{10,18},{12,20},{14,22},{16,8},... | collective-permute-start | bytes 294920 | tf_op jit(solution)/shard_map/ppermute | solution.py:46
  28.8 9.2 %collective-permute-start.10 = (f32[32,768]{1,0:T(8,128)S(1)}, f32[32,768]{1,0:T(8,128)S(1)}, u32[]{:S(2)}, u32[]{:S(2)}) collective-permute-start(f32[32,768]{1,0:T(8,128)S(1)} %get-tuple-element.47), channel_id=1, source_target_pairs={{0,16},{2,18},{4,20},{6,22},{8,24},{10,26},{12,28},{14,30},{16,0},... | collective-permute-start | bytes 294920 | tf_op jit(solution)/shard_map/ppermute | solution.py:46
  28.8 9.2 %collective-permute-start.9 = (f32[32,768]{1,0:T(8,128)S(1)}, f32[32,768]{1,0:T(8,128)S(1)}, u32[]{:S(2)}, u32[]{:S(2)}) collective-permute-start(f32[32,768]{1,0:T(8,128)S(1)} %get-tuple-element.47), channel_id=1, source_target_pairs={{0,8},{2,10},{4,12},{6,14},{8,0},{10,2},{12,4},{14,6},{16,24},{18,... | collective-permute-start | bytes 294920 | tf_op jit(solution)/shard_map/ppermute | solution.py:46
  29.4 8.6 %collective-permute-start.6 = (f32[10,384]{1,0:T(8,128)S(1)}, f32[10,384]{1,0:T(8,128)S(1)}, u32[]{:S(2)}, u32[]{:S(2)}) collective-permute-start(f32[10,384]{1,0:T(8,128)S(1)} %add_add_fusion.refs_0_), channel_id=1, source_target_pairs={{0,8},{2,10},{4,12},{6,14},{8,0},{10,2},{12,4},{14,6},{16,24},{18,... | collective-permute-start | bytes 46088 | tf_op jit(solution)/shard_map/ppermute | solution.py:46
  30.9 7.3 %collective-permute-start.7 = (f32[10,384]{1,0:T(8,128)S(1)}, f32[10,384]{1,0:T(8,128)S(1)}, u32[]{:S(2)}, u32[]{:S(2)}) collective-permute-start(f32[10,384]{1,0:T(8,128)S(1)} %add_add_fusion.refs_0_), channel_id=1, source_target_pairs={{0,16},{2,18},{4,20},{6,22},{8,24},{10,26},{12,28},{14,30},{16,0},... | collective-permute-start | bytes 46088 | tf_op jit(solution)/shard_map/ppermute | solution.py:46
  33.8 5.6 %collective-permute-start.8 = (f32[10,384]{1,0:T(8,128)S(1)}, f32[10,384]{1,0:T(8,128)S(1)}, u32[]{:S(2)}, u32[]{:S(2)}) collective-permute-start(f32[10,384]{1,0:T(8,128)S(1)} %add_add_fusion.refs_0_), channel_id=1, source_target_pairs={{0,24},{2,26},{4,28},{6,30},{8,16},{10,18},{12,20},{14,22},{16,8},... | collective-permute-start | bytes 46088 | tf_op jit(solution)/shard_map/ppermute | solution.py:46
  39.5 10.1 %collective-permute-start.12 = (f32[4,32,768]{2,1,0:T(8,128)S(1)}, f32[4,32,768]{2,1,0:T(8,128)S(1)}, u32[]{:S(2)}, u32[]{:S(2)}) collective-permute-start(f32[4,32,768]{2,1,0:T(8,128)S(1)} %pad_maximum_fusion.3), channel_id=1, source_target_pairs={{0,2},{1,5},{2,0},{3,7},{4,6},{5,1},{6,4},{7,3},{8,10},{9,13},{10,... | collective-permute-start | bytes 1179656 | tf_op jit(solution)/shard_map/ppermute | solution.py:51
  48.9 0.7 copy-start.11
  50.6 20.4 %collective-permute-start.13 = (f32[8,48,512]{2,1,0:T(8,128)}, f32[8,48,512]{2,1,0:T(8,128)}, u32[]{:S(2)}, u32[]{:S(2)}) collective-permute-start(f32[8,48,512]{2,1,0:T(8,128)} %get-tuple-element.62), channel_id=1, source_target_pairs={{0,2},{2,0},{4,6},{6,4},{8,10},{10,8},{12,14},{14,12},{16,18},{18,... | collective-permute-start | bytes 2359304 | tf_op jit(solution)/shard_map/ppermute | solution.py:46
  51.1 21.7 %collective-permute-start.14 = (f32[8,48,512]{2,1,0:T(8,128)}, f32[8,48,512]{2,1,0:T(8,128)}, u32[]{:S(2)}, u32[]{:S(2)}) collective-permute-start(f32[8,48,512]{2,1,0:T(8,128)} %get-tuple-element.64), channel_id=1, source_target_pairs={{0,4},{2,6},{4,0},{6,2},{8,12},{10,14},{12,8},{14,10},{16,20},{18,... | collective-permute-start | bytes 2359304 | tf_op jit(solution)/shard_map/ppermute | solution.py:46
  52.6 22.6 %collective-permute-start.15 = (f32[8,48,512]{2,1,0:T(8,128)}, f32[8,48,512]{2,1,0:T(8,128)}, u32[]{:S(2)}, u32[]{:S(2)}) collective-permute-start(f32[8,48,512]{2,1,0:T(8,128)} %get-tuple-element.66), channel_id=1, source_target_pairs={{0,8},{2,10},{4,12},{6,14},{8,0},{10,2},{12,4},{14,6},{16,24},{18,... | collective-permute-start | bytes 2359304 | tf_op jit(solution)/shard_map/ppermute | solution.py:46
  53.8 25.5 %all-to-all-start = ((f32[16,64,96]{2,1,0:T(8,128)}), f32[16,64,96]{2,1,0:T(8,128)S(1)}, u32[]{:S(2)}, u32[]{:S(2)}) async-start(f32[16,64,96]{2,1,0:T(8,128)} %copy-done.8), calls=%async_computation | async-start | bytes 1048576 | tf_op jit(solution)/shard_map/all_to_all | solution.py:512
  71.0 10.0 %copy-start.9 = (f32[64,768]{1,0:T(8,128)S(1)}, f32[64,768]{1,0:T(8,128)}, u32[]{:S(2)}) copy-start(f32[64,768]{1,0:T(8,128)} %moment_ref.1) | copy-start | bytes 589828
  71.0 10.0 %copy-start.10 = (f32[64,768]{1,0:T(8,128)S(1)}, f32[64,768]{1,0:T(8,128)}, u32[]{:S(2)}) copy-start(f32[64,768]{1,0:T(8,128)} %second_ref.1) | copy-start | bytes 589828
  79.2 11.7 %collective-permute-start.18 = (f32[4,48,512]{2,1,0:T(8,128)}, f32[4,48,512]{2,1,0:T(8,128)}, u32[]{:S(2)}, u32[]{:S(2)}) collective-permute-start(f32[4,48,512]{2,1,0:T(8,128)} %slice_add_fusion), channel_id=1, source_target_pairs={{0,4},{2,6},{4,0},{6,2},{8,12},{10,14},{12,8},{14,10},{16,20},{18,... | collective-permute-start | bytes 1179656 | tf_op jit(solution)/shard_map/ppermute | solution.py:46
  79.2 14.7 %collective-permute-start.17 = (f32[4,48,512]{2,1,0:T(8,128)}, f32[4,48,512]{2,1,0:T(8,128)}, u32[]{:S(2)}, u32[]{:S(2)}) collective-permute-start(f32[4,48,512]{2,1,0:T(8,128)} %slice_add_fusion.1), channel_id=1, source_target_pairs={{0,2},{2,0},{4,6},{6,4},{8,10},{10,8},{12,14},{14,12},{16,18},{18,... | collective-permute-start | bytes 1179656 | tf_op jit(solution)/shard_map/ppermute | solution.py:46
  80.3 16.3 %collective-permute-start.16 = (f32[4,48,512]{2,1,0:T(8,128)}, f32[4,48,512]{2,1,0:T(8,128)}, u32[]{:S(2)}, u32[]{:S(2)}) collective-permute-start(f32[4,48,512]{2,1,0:T(8,128)} %slice_add_fusion.2), channel_id=1, source_target_pairs={{0,8},{2,10},{4,12},{6,14},{8,0},{10,2},{12,4},{14,6},{16,24},{18,... | collective-permute-start | bytes 1179656 | tf_op jit(solution)/shard_map/ppermute | solution.py:46
  81.0 1.1 copy-start.7
  82.1 0.9 copy-start.12
  86.1 13.1 %copy-start.14 = (f32[2,4,32,768]{3,2,1,0:T(8,128)S(1)}, f32[2,4,32,768]{3,2,1,0:T(8,128)}, u32[]{:S(2)}) copy-start(f32[2,4,32,768]{3,2,1,0:T(8,128)} %pad_maximum_fusion.1) | copy-start | bytes 2359300
  86.1 27.2 %all-to-all-start.1 = ((f32[16,48,96]{2,1,0:T(8,128)}), f32[16,48,96]{2,1,0:T(8,128)}, u32[]{:S(2)}, u32[]{:S(2)}) async-start(f32[16,48,96]{2,1,0:T(8,128)} %get-tuple-element.81), calls=%async_computation.1 | async-start | bytes 786432 | tf_op jit(solution)/shard_map/all_to_all | solution.py:543
  92.0 9.3 %collective-permute-start.23 = (f32[2,48,512]{2,1,0:T(8,128)S(1)}, f32[2,48,512]{2,1,0:T(8,128)S(1)}, u32[]{:S(2)}, u32[]{:S(2)}) collective-permute-start(f32[2,48,512]{2,1,0:T(8,128)S(1)} %slice_add_fusion.10), channel_id=1, source_target_pairs={{0,2},{2,0},{4,6},{6,4},{8,10},{10,8},{12,14},{14,12},{16,18},{18,... | collective-permute-start | bytes 589832 | tf_op jit(solution)/shard_map/ppermute | solution.py:46
  95.0 7.4 %collective-permute-start.22 = (f32[2,48,512]{2,1,0:T(8,128)S(1)}, f32[2,48,512]{2,1,0:T(8,128)S(1)}, u32[]{:S(2)}, u32[]{:S(2)}) collective-permute-start(f32[2,48,512]{2,1,0:T(8,128)S(1)} %slice_add_fusion.12), channel_id=1, source_target_pairs={{0,8},{2,10},{4,12},{6,14},{8,0},{10,2},{12,4},{14,6},{16,24},{18,... | collective-permute-start | bytes 589832 | tf_op jit(solution)/shard_map/ppermute | solution.py:46
  97.6 5.9 %collective-permute-start.21 = (f32[2,48,512]{2,1,0:T(8,128)S(1)}, f32[2,48,512]{2,1,0:T(8,128)S(1)}, u32[]{:S(2)}, u32[]{:S(2)}) collective-permute-start(f32[2,48,512]{2,1,0:T(8,128)S(1)} %slice_add_fusion.14), channel_id=1, source_target_pairs={{0,4},{2,6},{4,0},{6,2},{8,12},{10,14},{12,8},{14,10},{16,20},{18,... | collective-permute-start | bytes 589832 | tf_op jit(solution)/shard_map/ppermute | solution.py:46
  99.2 12.6 %collective-permute-start.19 = (f32[2,4,32,768]{3,2,1,0:T(8,128)S(1)}, f32[2,4,32,768]{3,2,1,0:T(8,128)S(1)}, u32[]{:S(2)}, u32[]{:S(2)}) collective-permute-start(f32[2,4,32,768]{3,2,1,0:T(8,128)S(1)} %copy-done.14), channel_id=1, source_target_pairs={{0,4},{1,3},{2,6},{3,1},{4,0},{5,7},{6,2},{7,5},{8,12},{9,11},{10,... | collective-permute-start | bytes 2359304 | tf_op jit(solution)/shard_map/ppermute | solution.py:51
  105.5 11.1 %collective-permute-start.24 = (f32[1,48,1536]{2,1,0:T(8,128)}, f32[1,48,1536]{2,1,0:T(8,128)}, u32[]{:S(2)}, u32[]{:S(2)}) collective-permute-start(f32[1,48,1536]{2,1,0:T(8,128)} %slice.120), channel_id=1, source_target_pairs={{0,16},{2,18},{4,20},{6,22},{8,24},{10,26},{12,28},{14,30},{16,0},... | collective-permute-start | bytes 884744 | tf_op jit(solution)/shard_map/ppermute | solution.py:46
  113.2 5.1 %collective-permute-start.20 = (f32[192,768]{1,0:T(8,128)S(1)}, f32[192,768]{1,0:T(8,128)S(1)}, u32[]{:S(2)}, u32[]{:S(2)}) collective-permute-start(f32[192,768]{1,0:T(8,128)S(1)} %dynamic-slice_bitcast_fusion), channel_id=1, source_target_pairs={{0,1},{1,0},{2,3},{3,2},{4,5},{5,4},{6,7},{7,6},{8,9},{9,8},{10,11... | collective-permute-start | bytes 1769480 | tf_op jit(solution)/shard_map/ppermute | solution.py:46

commit v4 on v3

--- a/solution.py
+++ b/solution.py
@@ -24,6 +24,8 @@
 SCORE = 24
 BACKWARD = 32
 REST = 24
+DOWN = 60
+SUMS = 16
 
 
 def whole(shape):
@@ -95,7 +97,8 @@
 
     thirds = [[keep, swap(give, order[0])] for keep, give, order in zip(keeps, gives, orders)]
     for step in range(1, 3):
-        gives = before[step - 1]([upper(parts) for parts in thirds])
+        given = upper_sums(thirds) if step == 1 else [upper(parts) for parts in thirds]
+        gives = before[step - 1](given)
         for parts, give, order in zip(thirds, gives, orders):
             parts.append(swap(give, order[step]))
     size = thirds[0][-1].shape[0]
@@ -143,6 +146,29 @@
     return 6 if cols % (6 * 128) == 0 else 3
 
 
+def packs(rows, cols):
+    return cols == 96 and rows % 64 == 0
+
+
+def pack(block):
+    rows, cols = block.shape
+    if not packs(rows, cols):
+        return block
+    most, third = rows * 3 // 4, cols // 3
+    rest = block[most:]
+    beside = [rest[:, p * third : (p + 1) * third] for p in range(3)]
+    return jnp.concatenate((block[:most], jnp.concatenate(beside)), axis=1)
+
+
+def unpack(block, rows, cols):
+    if not packs(rows, cols):
+        return block
+    most = rows * 3 // 4
+    few = rows - most
+    beside = [block[p * few : (p + 1) * few, cols:] for p in range(3)]
+    return jnp.concatenate((block[:, :cols], jnp.concatenate(beside, axis=1)))
+
+
 def encode(text_rows, up_weight, down_weight, label_rows, label_count):
     tokens, model_width = text_rows.shape
     unit_cols = up_weight.shape[1]
@@ -151,6 +177,7 @@
     chunk = unit_cols // steps
     width = model_width // steps
     share = unit_cols // label_count
+    packed = (label_rows * 3 // 4, 128) if packs(label_rows, share) else (label_rows, share)
 
     def pool(values):
         values = values.astype(jnp.float32).reshape(label_rows, text_len, values.shape[1])
@@ -183,7 +210,7 @@
         def _():
             pooled = pooled_ref[...]
             for place in range(label_count):
-                shares_ref[place] = pooled[:, place * share : (place + 1) * share]
+                shares_ref[place] = pack(pooled[:, place * share : (place + 1) * share])
             both = lax.dot_general(
                 jnp.concatenate(split_bf16(pooled)),
                 down_ref[...],
@@ -201,14 +228,14 @@
             whole(down_weight.shape),
         ],
         out_specs=[
-            whole((label_count, label_rows, share)),
+            whole((label_count, *packed)),
             pl.BlockSpec((tokens, chunk), lambda i: (0, i)),
             pl.BlockSpec((width, tokens), lambda i: (i, 0)),
             pl.BlockSpec((label_rows, width), lambda i: (0, i)),
             whole((label_rows, model_width)),
         ],
         out_shape=[
-            f32((label_count, label_rows, share)),
+            f32((label_count, *packed)),
             bf16((tokens, unit_cols)),
             bf16((model_width, tokens)),
             f32((label_rows, model_width)),
@@ -397,14 +424,9 @@
     )(coef, ids, vectors)
 
 
-def down_gradient_and_adam(
-    coef, ids, every_query, pooled_all, label_grad, free_vectors, moments, seconds, label_count
-):
-    labels, units = pooled_all.shape
+def down_gradient(coef, ids, every_query, pooled_all, label_count, units, label_rows):
     model_width = every_query.shape[1]
-    label_rows = free_vectors.shape[0]
     own = model_width // label_count
-    choices, total = ids.shape
 
     def product(left, right):
         both = lax.dot_general(
@@ -415,25 +437,29 @@
         )
         return both[:, :units] + both[:, units:]
 
-    def kernel(
-        coef_ref,
-        ids_ref,
-        query_ref,
-        pooled_ref,
-        grad_ref,
-        free_ref,
-        moment_ref,
-        second_ref,
-        out_ref,
-        free_out,
-        moment_out,
-        second_out,
-    ):
-        spread = spread_of(ids_ref, coef_ref[...], 0, labels)
-        result = product(query_ref[...], product(spread, pooled_ref[...]))
+    def kernel(coef_ref, ids_ref, query_ref, pooled_ref, out_ref):
+        spread = spread_of(ids_ref, coef_ref[...], 0, label_count * label_rows)
+        pooled = jnp.concatenate(
+            [unpack(pooled_ref[place], label_rows, units) for place in range(label_count)]
+        )
+        result = product(query_ref[...], product(spread, pooled))
         for block in range(label_count):
             out_ref[block] = result[block * own : (block + 1) * own, :]
 
+    return pl.pallas_call(
+        kernel,
+        out_shape=f32((label_count, own, units)),
+        compiler_params=params(DOWN),
+        name="down_gradient",
+    )(coef, ids, every_query, pooled_all)
+
+
+def adam(ids, label_grad, free_vectors, moments, seconds):
+    choices, total = ids.shape
+    label_rows = free_vectors.shape[0]
+
+    def kernel(ids_ref, grad_ref, free_ref, moment_ref, second_ref, *outs):
+        free_out, moment_out, second_out = outs
         label = lax.broadcasted_iota(jnp.int32, (label_rows, total), 0)
         label = label + lax.axis_index("label") * label_rows
         hits = jnp.zeros((label_rows, total), jnp.float32)
@@ -454,10 +480,57 @@
 
     return pl.pallas_call(
         kernel,
-        out_shape=[f32((label_count, own, units))] + [f32(free_vectors.shape)] * 3,
+        out_shape=[f32(free_vectors.shape)] * 3,
         compiler_params=params(REST),
-        name="down_gradient_and_adam",
-    )(coef, ids, every_query, pooled_all, label_grad, free_vectors, moments, seconds)
+        name="adam",
+    )(ids, label_grad, free_vectors, moments, seconds)
+
+
+def upper_sums(held):
+    size, own, cols = held[0][-1].shape
+    half = size // 2
+    steps = 2 if half % 2 == 0 else 1
+    block = half // steps
+    count = len(held[0])
+
+    def kernel(*refs):
+        ins, outs = refs[: THIRDS * count], refs[THIRDS * count :]
+        for third, out in enumerate(outs):
+            out[...] = sum(r[...] for r in ins[third * count : (third + 1) * count])
+
+    return pl.pallas_call(
+        kernel,
+        grid=(steps,),
+        in_specs=[pl.BlockSpec((block, own, cols), lambda i: (steps + i, 0, 0))] * (THIRDS * count),
+        out_specs=[pl.BlockSpec((block, own, cols), lambda i: (i, 0, 0))] * THIRDS,
+        out_shape=[f32((half, own, cols))] * THIRDS,
+        compiler_params=params(SUMS),
+        name="upper_sums",
+    )(*[part for parts in held for part in parts])
+
+
+def joined_sums(held):
+    size, own, cols = held[0][-1].shape
+    half = size // 2
+    count = len(held[0])
+
+    def kernel(*refs):
+        ins, (keep_ref, give_ref) = refs[:-2], refs[-2:]
+        for third in range(THIRDS):
+            span = slice(third * cols, (third + 1) * cols)
+            some = ins[third * count : (third + 1) * count]
+            keep_ref[:, :, span] = sum(r[:half] for r in some)
+            give_ref[:, :, span] = sum(r[half:] for r in some)
+
+    return pl.pallas_call(
+        kernel,
+        grid=(1,),
+        in_specs=[pl.BlockSpec((size, own, cols), lambda i: (0, 0, 0))] * (THIRDS * count),
+        out_specs=[whole((half, own, THIRDS * cols))] * 2,
+        out_shape=[f32((half, own, THIRDS * cols))] * 2,
+        compiler_params=params(SUMS),
+        name="joined_sums",
+    )(*[part for parts in held for part in parts])
 
 
 def body(
@@ -529,16 +602,17 @@
     up_grad = scatter_sum(keeps, gives, label_count, (second_step, third_step, fourth_step))
 
     vectors = gather_far(after(vectors, given[2]), counts)
-    down_cols, free_new, moments_new, seconds_new = down_gradient_and_adam(
+    down_cols = down_gradient(
         coef,
         ids,
         every_query,
-        after(late[0], given[1]).reshape(labels, unit_cols // label_count),
-        label_grad,
-        free_vectors,
-        moments,
-        seconds,
+        after(late[0], given[1]),
         label_count,
+        unit_cols // label_count,
+        label_rows,
+    )
+    free_new, moments_new, seconds_new = adam(
+        ids, after(label_grad, given[3]), free_vectors, moments, seconds
     )
     down_rows = lax.all_to_all(after(down_cols, given[1]), "label", 0, 0)
     query_terms = query_gradient(coef, ids, vectors, label_rows)

time: 120 us -> 117 us (0.975)
  other arithmetic: 16.7 us -> 11.2 us
  Pallas kernels: 23.6 us -> 27.2 us
  waiting for transfers between devices: 25.3 us -> 24 us
    add x6 -> x3, other arithmetic: 8.67 us -> 3.16 us  [upper(): return sum((p[size // 2:size] for p in parts))]
    pallas_call x1 -> x3, Pallas kernels: 3.08 us -> 6.68 us  [the longest x1 4.26 us: down_gradient(): pl.pallas_call(kernel, out_shape=f32((label_count, own, units)), compiler...]
    all_to_all x1, waiting for transfers between devices: 2.23 us -> 0.54 us  [body(): pooled_all = lax.all_to_all(after(pooled_shares, gives), 'label', 0, 0)]
    unnamed x30 -> x42, local copies, waits for them, and re-layouts: 7.92 us -> 7.57 us
  transfers between devices with their start and end apart: 27 -> 27, of which waited for: 10 -> 10; matrix products, arithmetic and copies ran while one was open for 14% -> 9% of each run, Pallas kernels for 19% -> 23%
where the time goes in v4:
time: 117 us; the launch traced here: 116 us
  starting transfers between devices  41.9 us (36%)
  Pallas kernels  27.2 us (23%)
  waiting for transfers between devices  24 us (21%)
  other arithmetic  11.2 us (10%)
  local copies, waits for them, and re-layouts  11.2 us (10%)
    ppermute x23, starting transfers between devices, pair_swap(): return lax.ppermute(values, axis, [(s, s ^ bits) for s in range(count)])  29.8 us
    ppermute x23, waiting for transfers between devices, pair_swap(): return lax.ppermute(values, axis, [(s, s ^ bits) for s in range(count)])  20 us
    pallas_call x1, Pallas kernels, encode(): pl.pallas_call(kernel, grid=(steps,), in_specs=[whole(text_rows.shape), p...  11 us
    pallas_call x1, Pallas kernels, backward(): pl.pallas_call(kernel, in_specs=[pl.BlockSpec(memory_space=pltpu.VMEM)] *...  7.9 us
    unnamed x42, local copies, waits for them, and re-layouts  7.57 us
    all_to_all x1, starting transfers between devices, body(): pooled_all = lax.all_to_all(after(pooled_shares, gives), 'label', 0, 0)  5.27 us
    all_to_all x1, starting transfers between devices, body(): down_rows = lax.all_to_all(after(down_cols, given[1]), 'label', 0, 0)  4.76 us
    pallas_call x1, Pallas kernels, down_gradient(): pl.pallas_call(kernel, out_shape=f32((label_count, own, units)), compiler...  4.26 us
  transfers between devices with their start and end apart: 27, of which 10 were waited for; matrix products, arithmetic and copies ran while one was open for 9% of the time, Pallas kernels for 23%

profile of v4, /device:TPU:0, one launch (start us, length us, event | category | flops | bytes accessed | tf_op | source)
XLA Modules:
  0.0 116.4 jit_solution(7742375758627453542)
XLA Ops:
  0.6 1.0 convert_element_type.3
  1.6 0.5 collective-permute-start.1
  2.2 1.9 %copy-done = bf16[64,32,768]{2,1,0:T(8,128)(2,1)S(1)} copy-done((bf16[64,32,768]{2,1,0:T(8,128)(2,1)S(1)}, bf16[64,32,768]{2,1,0:T(8,128)(2,1)}, u32[]{:S(2)}) %copy-start) | copy-done | bytes 3145752
  4.0 1.7 %copy-done.1 = bf16[768,1536]{1,0:T(8,128)(2,1)S(1)} copy-done((bf16[768,1536]{1,0:T(8,128)(2,1)S(1)}, bf16[768,1536]{1,0:T(8,128)(2,1)}, u32[]{:S(2)}) %copy-start.1) | copy-done | bytes 2359320
  5.7 1.7 %copy-done.2 = bf16[768,1536]{1,0:T(8,128)(2,1)S(1)} copy-done((bf16[768,1536]{1,0:T(8,128)(2,1)S(1)}, bf16[768,1536]{1,0:T(8,128)(2,1)}, u32[]{:S(2)}) %copy-start.2) | copy-done | bytes 2359320
  7.4 11.0 %encode.1 = (f32[16,48,128]{2,1,0:T(8,128)S(1)}, bf16[2048,1536]{1,0:T(8,128)(2,1)S(1)}, bf16[768,2048]{1,0:T(8,128)(2,1)S(1)}, f32[64,768]{1,0:T(8,128)S(1)}, f32[64,768]{1,0:T(8,128)S(1)}) custom-call(bf16[2048,768]{1,0:T(8,128)(2,1)S(1)} %bitcast.18, bf16[768,1536]{1,0:T(8,128)(2,1)S(1)} %copy-done.1, bf16[768,1536]{1,0:T(8,128)(2,1)S(1)} %copy-done.2), custom_call_target="tpu_custom_call" | custom-call | tf_op jit(solution)/shard_map/encode/pallas_call | solution.py:222
  18.4 0.0 copy-start.3
  18.4 0.1 collective-permute-start
  18.5 0.4 collective-permute-start.2
  19.0 1.0 collective-permute-done.2.refs_7_
  19.9 0.5 score.1
  20.4 3.7 %collective-permute-start.5 = (f32[10,384]{1,0:T(8,128)S(1)}, f32[10,384]{1,0:T(8,128)S(1)}, u32[]{:S(2)}, u32[]{:S(2)}) collective-permute-start(f32[10,384]{1,0:T(8,128)S(1)} %get-tuple-element.50), channel_id=1, source_target_pairs={{0,6},{2,4},{4,2},{6,0},{8,14},{10,12},{12,10},{14,8},{16,22},{18,... | collective-permute-start | bytes 46088 | tf_op jit(solution)/shard_map/ppermute | solution.py:48
  24.2 0.5 collective-permute-start.3
  24.7 0.1 collective-permute-start.4
  24.8 4.0 %collective-permute-start.11 = (f32[32,768]{1,0:T(8,128)S(1)}, f32[32,768]{1,0:T(8,128)S(1)}, u32[]{:S(2)}, u32[]{:S(2)}) collective-permute-start(f32[32,768]{1,0:T(8,128)S(1)} %get-tuple-element.51), channel_id=1, source_target_pairs={{0,24},{2,26},{4,28},{6,30},{8,16},{10,18},{12,20},{14,22},{16,8},... | collective-permute-start | bytes 294920 | tf_op jit(solution)/shard_map/ppermute | solution.py:48
  28.8 0.6 collective-permute-start.9
  29.4 1.5 %collective-permute-start.6 = (f32[10,384]{1,0:T(8,128)S(1)}, f32[10,384]{1,0:T(8,128)S(1)}, u32[]{:S(2)}, u32[]{:S(2)}) collective-permute-start(f32[10,384]{1,0:T(8,128)S(1)} %add_add_fusion.refs_0_), channel_id=1, source_target_pairs={{0,8},{2,10},{4,12},{6,14},{8,0},{10,2},{12,4},{14,6},{16,24},{18,... | collective-permute-start | bytes 46088 | tf_op jit(solution)/shard_map/ppermute | solution.py:48
  30.9 2.9 %collective-permute-start.7 = (f32[10,384]{1,0:T(8,128)S(1)}, f32[10,384]{1,0:T(8,128)S(1)}, u32[]{:S(2)}, u32[]{:S(2)}) collective-permute-start(f32[10,384]{1,0:T(8,128)S(1)} %add_add_fusion.refs_0_), channel_id=1, source_target_pairs={{0,16},{2,18},{4,20},{6,22},{8,24},{10,26},{12,28},{14,30},{16,0},... | collective-permute-start | bytes 46088 | tf_op jit(solution)/shard_map/ppermute | solution.py:48
  33.9 2.5 %collective-permute-start.8 = (f32[10,384]{1,0:T(8,128)S(1)}, f32[10,384]{1,0:T(8,128)S(1)}, u32[]{:S(2)}, u32[]{:S(2)}) collective-permute-start(f32[10,384]{1,0:T(8,128)S(1)} %add_add_fusion.refs_0_), channel_id=1, source_target_pairs={{0,24},{2,26},{4,28},{6,30},{8,16},{10,18},{12,20},{14,22},{16,8},... | collective-permute-start | bytes 46088 | tf_op jit(solution)/shard_map/ppermute | solution.py:48
  36.4 1.7 %collective-permute-done.10 = f32[32,768]{1,0:T(8,128)S(1)} collective-permute-done((f32[32,768]{1,0:T(8,128)S(1)}, f32[32,768]{1,0:T(8,128)S(1)}, u32[]{:S(2)}, u32[]{:S(2)}) %collective-permute-start.10) | collective-permute-done | bytes 98336 | tf_op jit(solution)/shard_map/ppermute | solution.py:48
  38.1 0.2 collective-permute-done.7.refs_2_
  38.3 1.2 %collective-permute-done.8.refs_3_ = f32[10,384]{1,0:T(8,128)S(1)} collective-permute-done((f32[10,384]{1,0:T(8,128)S(1)}, f32[10,384]{1,0:T(8,128)S(1)}, u32[]{:S(2)}, u32[]{:S(2)}) %collective-permute-start.8) | collective-permute-done | bytes 15392 | tf_op jit(solution)/shard_map/ppermute | solution.py:48
  39.5 1.5 %collective-permute-start.12 = (f32[4,32,768]{2,1,0:T(8,128)S(1)}, f32[4,32,768]{2,1,0:T(8,128)S(1)}, u32[]{:S(2)}, u32[]{:S(2)}) collective-permute-start(f32[4,32,768]{2,1,0:T(8,128)S(1)} %pad_maximum_fusion.3), channel_id=1, source_target_pairs={{0,2},{1,5},{2,0},{3,7},{4,6},{5,1},{6,4},{7,3},{8,10},{9,13},{10,... | collective-permute-start | bytes 1179656 | tf_op jit(solution)/shard_map/ppermute | solution.py:53
  41.0 7.9 %backward.1 = (f32[10,384]{1,0:T(8,128)S(1)}, f32[64,768]{1,0:T(8,128)S(1)}, f32[8,48,512]{2,1,0:T(8,128)S(1)}, f32[8,48,512]{2,1,0:T(8,128)}, f32[8,48,512]{2,1...) custom-call(f32[10,384]{1,0:T(8,128)S(1)} %add_add_fusion.refs_0_, ...), custom_call_target="tpu_custom_call" | custom-call | flops 4831838208 | bytes 16777216 | tf_op jit(solution)/shard_map/backward/pallas_call | solution.py:374
  49.0 1.0 pad_maximum_fusion.1
  49.9 0.5 collective-permute-start.13
  50.4 1.5 %collective-permute-start.14 = (f32[8,48,512]{2,1,0:T(8,128)}, f32[8,48,512]{2,1,0:T(8,128)}, u32[]{:S(2)}, u32[]{:S(2)}) collective-permute-start(f32[8,48,512]{2,1,0:T(8,128)} %get-tuple-element.67), channel_id=1, source_target_pairs={{0,4},{2,6},{4,0},{6,2},{8,12},{10,14},{12,8},{14,10},{16,20},{18,... | collective-permute-start | bytes 2359304 | tf_op jit(solution)/shard_map/ppermute | solution.py:48
  52.0 1.1 collective-permute-start.15
  53.1 5.3 %all-to-all-start = ((f32[16,48,128]{2,1,0:T(8,128)}), f32[16,48,128]{2,1,0:T(8,128)}, u32[]{:S(2)}, u32[]{:S(2)}) async-start(f32[16,48,128]{2,1,0:T(8,128)} %copy-done.7), calls=%async_computation | async-start | bytes 786432 | tf_op jit(solution)/shard_map/all_to_all | solution.py:585
  58.4 10.9 %collective-permute-done.13.refs_1_ = f32[8,48,512]{2,1,0:T(8,128)S(1)} collective-permute-done((f32[8,48,512]{2,1,0:T(8,128)}, f32[8,48,512]{2,1,0:T(8,128)S(1)}, u32[]{:S(2)}, u32[]{:S(2)}) %collective-permute-start.13) | collective-permute-done | bytes 786464 | tf_op jit(solution)/shard_map/ppermute | solution.py:48
  69.3 1.3 %collective-permute-done.14.refs_3_ = f32[8,48,512]{2,1,0:T(8,128)} collective-permute-done((f32[8,48,512]{2,1,0:T(8,128)}, f32[8,48,512]{2,1,0:T(8,128)}, u32[]{:S(2)}, u32[]{:S(2)}) %collective-permute-start.14) | collective-permute-done | bytes 786464 | tf_op jit(solution)/shard_map/ppermute | solution.py:48
  70.6 1.8 %collective-permute-done.15.refs_5_ = f32[8,48,512]{2,1,0:T(8,128)} collective-permute-done((f32[8,48,512]{2,1,0:T(8,128)}, f32[8,48,512]{2,1,0:T(8,128)}, u32[]{:S(2)}, u32[]{:S(2)}) %collective-permute-start.15) | collective-permute-done | bytes 786464 | tf_op jit(solution)/shard_map/ppermute | solution.py:48
  72.5 1.3 %upper_sums.1 = (f32[4,48,512]{2,1,0:T(8,128)S(1)}, f32[4,48,512]{2,1,0:T(8,128)S(1)}, f32[4,48,512]{2,1,0:T(8,128)S(1)}) custom-call(f32[8,48,512]{2,1,0:T(8,128)S(1)} %get-tuple-element.60.refs_0_, f32[8,48,512]{2,1,0:T(8,128)S(1)} %collective-permute-done.13.refs_1_, f32[8,48,512]{2,1,0:T(8,128)S(1)} %get-tuple-element.66.refs_2_, ...), custom_call_target="tpu_custom_call" | custom-call | tf_op jit(solution)/shard_map/upper_sums/pallas_call | solution.py:501
  73.8 0.8 copy-done.17
  74.5 0.8 copy-done.18
  75.3 0.7 copy-done.19
  76.0 0.5 all-to-all-done.pooled_ref
  76.6 1.0 collective-permute-start.20
  77.6 0.5 collective-permute-start.18
  78.1 0.4 collective-permute-start.16
  78.5 4.3 %down_gradient.1 = f32[16,48,96]{2,1,0:T(8,128)} custom-call(f32[10,384]{1,0:T(8,128)} %copy-done.14, s32[10,384]{1,0:T(8,128)} %copy-done.8, bf16[384,768]{1,0:T(8,128)(2,1)} %copy-done.6, f32[16,48,128]{2,1,0:T(8,128)} %all-to-all-done.pooled_ref), custom_call_target="tpu_custom_call" | custom-call | tf_op jit(solution)/shard_map/down_gradient/pallas_call | solution.py:449
  82.8 4.8 %all-to-all-start.1 = ((f32[16,48,96]{2,1,0:T(8,128)}), f32[16,48,96]{2,1,0:T(8,128)}, u32[]{:S(2)}, u32[]{:S(2)}) async-start(f32[16,48,96]{2,1,0:T(8,128)} %down_gradient.1), calls=%async_computation.1 | async-start | bytes 786432 | tf_op jit(solution)/shard_map/all_to_all | solution.py:617
  87.5 1.1 slice_add_fusion.1
  88.7 1.9 %collective-permute-start.21 = (f32[2,48,512]{2,1,0:T(8,128)S(1)}, f32[2,48,512]{2,1,0:T(8,128)S(1)}, u32[]{:S(2)}, u32[]{:S(2)}) collective-permute-start(f32[2,48,512]{2,1,0:T(8,128)S(1)} %slice_add_fusion.1), channel_id=1, source_target_pairs={{0,2},{2,0},{4,6},{6,4},{8,10},{10,8},{12,14},{14,12},{16,18},{18,... | collective-permute-start | bytes 589832 | tf_op jit(solution)/shard_map/ppermute | solution.py:48
  90.6 1.1 slice_add_fusion.5
  91.7 1.5 %collective-permute-start.19 = (f32[2,48,512]{2,1,0:T(8,128)S(1)}, f32[2,48,512]{2,1,0:T(8,128)S(1)}, u32[]{:S(2)}, u32[]{:S(2)}) collective-permute-start(f32[2,48,512]{2,1,0:T(8,128)S(1)} %slice_add_fusion.5), channel_id=1, source_target_pairs={{0,8},{2,10},{4,12},{6,14},{8,0},{10,2},{12,4},{14,6},{16,24},{18,... | collective-permute-start | bytes 589832 | tf_op jit(solution)/shard_map/ppermute | solution.py:48
  93.2 1.0 slice_add_fusion.9
  94.2 1.5 %collective-permute-start.17 = (f32[2,48,512]{2,1,0:T(8,128)S(1)}, f32[2,48,512]{2,1,0:T(8,128)S(1)}, u32[]{:S(2)}, u32[]{:S(2)}) collective-permute-start(f32[2,48,512]{2,1,0:T(8,128)S(1)} %slice_add_fusion.9), channel_id=1, source_target_pairs={{0,4},{2,6},{4,0},{6,2},{8,12},{10,14},{12,8},{14,10},{16,20},{18,... | collective-permute-start | bytes 589832 | tf_op jit(solution)/shard_map/ppermute | solution.py:48
  95.7 0.6 collective-permute-start.22
  96.3 1.8 %collective-permute-done.21 = f32[2,48,512]{2,1,0:T(8,128)S(1)} collective-permute-done((f32[2,48,512]{2,1,0:T(8,128)S(1)}, f32[2,48,512]{2,1,0:T(8,128)S(1)}, u32[]{:S(2)}, u32[]{:S(2)}) %collective-permute-start.21) | collective-permute-done | bytes 196640 | tf_op jit(solution)/shard_map/ppermute | solution.py:48
  98.1 1.1 fusion.1
  99.2 1.1 fusion.2
  100.3 1.0 fusion.3
  101.3 0.7 slice.92
  102.1 2.7 %collective-permute-start.24 = (f32[1,48,1536]{2,1,0:T(8,128)}, f32[1,48,1536]{2,1,0:T(8,128)S(1)}, u32[]{:S(2)}, u32[]{:S(2)}) collective-permute-start(f32[1,48,1536]{2,1,0:T(8,128)} %slice.92), channel_id=1, source_target_pairs={{0,16},{2,18},{4,20},{6,22},{8,24},{10,26},{12,28},{14,30},{16,0},... | collective-permute-start | bytes 884744 | tf_op jit(solution)/shard_map/ppermute | solution.py:48
  104.8 3.5 %collective-permute-done.22 = f32[2,4,32,768]{3,2,1,0:T(8,128)S(1)} collective-permute-done((f32[2,4,32,768]{3,2,1,0:T(8,128)S(1)}, f32[2,4,32,768]{3,2,1,0:T(8,128)S(1)}, u32[]{:S(2)}, u32[]{:S(2)}) %collective-permute-start.22) | collective-permute-done | bytes 786464 | tf_op jit(solution)/shard_map/ppermute | solution.py:53
  108.3 0.1 pad_maximum_fusion.vector_ref
  108.5 1.2 %query_gradient.1 = f32[384,768]{1,0:T(8,128)S(1)} custom-call(f32[10,384]{1,0:T(8,128)S(1)} %copy-done.15, s32[10,384]{1,0:T(8,128)S(1)} %copy-done.9, f32[4,4,32,768]{3,2,1,0:T(8,128)S(1)} %pad_maximum_fusion.vector_ref), custom_call_target="tpu_custom_call" | custom-call | tf_op jit(solution)/shard_map/query_gradient/pallas_call | solution.py:419
  109.7 0.9 dynamic-slice_bitcast_fusion
  110.6 1.1 copy.14
  111.7 0.9 reshape.24
  112.6 1.1 adam.1
  113.7 0.7 fusion
  114.5 1.9 %bitcast_add_fusion = f32[192,768]{1,0:T(8,128)} fusion(f32[192,768]{1,0:T(8,128)} %collective-permute-done.23, f32[2,192,768]{2,1,0:T(8,128)S(1)} %bitcast.17, s32[]{:T(128)S(6)} %select_n.7), kind=kLoop, calls=%fused_computation.3 | loop fusion | flops 147456 | bytes 1769476 | tf_op jit(solution)/shard_map/add | solution.py:623
  (57 shorter events, 0.2 us)
Async XLA Ops:
  1.6 18.3 %collective-permute-start.1 = (f32[192,768]{1,0:T(8,128)S(1)}, f32[192,768]{1,0:T(8,128)S(1)}, u32[]{:S(2)}, u32[]{:S(2)}) collective-permute-start(f32[192,768]{1,0:T(8,128)S(1)} %convert_element_type.3), channel_id=1, source_target_pairs={{0,1},{1,0},{2,3},{3,2},{4,5},{5,4},{6,7},{7,6},{8,9},{9,8},{10,11... | collective-permute-start | bytes 1769480 | tf_op jit(solution)/shard_map/ppermute | solution.py:48
  2.2 1.9 %copy-start = (bf16[64,32,768]{2,1,0:T(8,128)(2,1)S(1)}, bf16[64,32,768]{2,1,0:T(8,128)(2,1)}, u32[]{:S(2)}) copy-start(bf16[64,32,768]{2,1,0:T(8,128)(2,1)} %param.10) | copy-start | bytes 9437188
  4.0 1.7 %copy-start.1 = (bf16[768,1536]{1,0:T(8,128)(2,1)S(1)}, bf16[768,1536]{1,0:T(8,128)(2,1)}, u32[]{:S(2)}) copy-start(bf16[768,1536]{1,0:T(8,128)(2,1)} %up_ref.1) | copy-start | bytes 7077892
  5.7 1.7 %copy-start.2 = (bf16[768,1536]{1,0:T(8,128)(2,1)S(1)}, bf16[768,1536]{1,0:T(8,128)(2,1)}, u32[]{:S(2)}) copy-start(bf16[768,1536]{1,0:T(8,128)(2,1)} %refs_6_.1) | copy-start | bytes 7077892
  7.4 11.2 %copy-start.16 = (s32[192,10]{0,1:T(8,128)S(1)}, s32[192,10]{0,1:T(8,128)}, u32[]{:S(2)}) copy-start(s32[192,10]{0,1:T(8,128)} %param.9) | copy-start | bytes 23044
  7.4 12.6 %copy-start.4 = (bf16[192,768]{1,0:T(8,128)(2,1)S(1)}, bf16[192,768]{1,0:T(8,128)(2,1)}, u32[]{:S(2)}) copy-start(bf16[192,768]{1,0:T(8,128)(2,1)} %refs_4_.1) | copy-start | bytes 884740
  7.4 12.6 %copy-start.5 = (f32[64,768]{1,0:T(8,128)S(1)}, f32[64,768]{1,0:T(8,128)}, u32[]{:S(2)}) copy-start(f32[64,768]{1,0:T(8,128)} %free_ref.1) | copy-start | bytes 589828
  18.4 22.6 %copy-start.7 = (f32[16,48,128]{2,1,0:T(8,128)}, f32[16,48,128]{2,1,0:T(8,128)S(1)}, u32[]{:S(2)}) copy-start(f32[16,48,128]{2,1,0:T(8,128)S(1)} %get-tuple-element.74) | copy-start | bytes 1179652
  18.4 22.6 %copy-start.3 = (bf16[768,1536]{1,0:T(8,128)(2,1)S(1)}, bf16[768,1536]{1,0:T(8,128)(2,1)}, u32[]{:S(2)}) copy-start(bf16[768,1536]{1,0:T(8,128)(2,1)} %refs_6_.1) | copy-start | bytes 7077892
  18.4 1.5 %collective-permute-start = (f32[64,768]{1,0:T(8,128)S(1)}, f32[64,768]{1,0:T(8,128)S(1)}, u32[]{:S(2)}, u32[]{:S(2)}) collective-permute-start(f32[64,768]{1,0:T(8,128)S(1)} %get-tuple-element.47.refs_0_), channel_id=1, source_target_pairs={{0,1},{1,0},{2,3},{3,2},{4,5},{5,4},{6,7},{7,6},{8,9},{9,8},{10,11... | collective-permute-start | bytes 589832 | tf_op jit(solution)/shard_map/ppermute | solution.py:48
  18.5 1.4 %collective-permute-start.2 = (s32[10,192]{1,0:T(8,128)S(1)}, s32[10,192]{1,0:T(8,128)S(1)}, u32[]{:S(2)}, u32[]{:S(2)}) collective-permute-start(s32[10,192]{1,0:T(8,128)S(1)} %bitcast.20), channel_id=1, source_target_pairs={{0,1},{1,0},{2,3},{3,2},{4,5},{5,4},{6,7},{7,6},{8,9},{9,8},{10,11... | collective-permute-start | bytes 23048 | tf_op jit(solution)/shard_map/ppermute | solution.py:48
  20.4 28.5 %copy-start.6 = (bf16[384,768]{1,0:T(8,128)(2,1)}, bf16[384,768]{1,0:T(8,128)(2,1)S(1)}, u32[]{:S(2)}) copy-start(bf16[384,768]{1,0:T(8,128)(2,1)S(1)} %get-tuple-element.56.refs_5_.query_ref) | copy-start | bytes 1769476
  20.4 28.5 %copy-start.8 = (s32[10,384]{1,0:T(8,128)}, s32[10,384]{1,0:T(8,128)S(1)}, u32[]{:S(2)}) copy-start(s32[10,384]{1,0:T(8,128)S(1)} %get-tuple-element.49.refs_4_.ids_ref) | copy-start | bytes 46084
  20.4 8.4 %collective-permute-start.5 = (f32[10,384]{1,0:T(8,128)S(1)}, f32[10,384]{1,0:T(8,128)S(1)}, u32[]{:S(2)}, u32[]{:S(2)}) collective-permute-start(f32[10,384]{1,0:T(8,128)S(1)} %get-tuple-element.50), channel_id=1, source_target_pairs={{0,6},{2,4},{4,2},{6,0},{8,14},{10,12},{12,10},{14,8},{16,22},{18,... | collective-permute-start | bytes 46088 | tf_op jit(solution)/shard_map/ppermute | solution.py:48
  24.2 5.2 %collective-permute-start.3 = (f32[10,384]{1,0:T(8,128)S(1)}, f32[10,384]{1,0:T(8,128)S(1)}, u32[]{:S(2)}, u32[]{:S(2)}) collective-permute-start(f32[10,384]{1,0:T(8,128)S(1)} %get-tuple-element.50), channel_id=1, source_target_pairs={{0,2},{2,0},{4,6},{6,4},{8,10},{10,8},{12,14},{14,12},{16,18},{18,... | collective-permute-start | bytes 46088 | tf_op jit(solution)/shard_map/ppermute | solution.py:48
  24.7 4.7 %collective-permute-start.4 = (f32[10,384]{1,0:T(8,128)S(1)}, f32[10,384]{1,0:T(8,128)S(1)}, u32[]{:S(2)}, u32[]{:S(2)}) collective-permute-start(f32[10,384]{1,0:T(8,128)S(1)} %get-tuple-element.50), channel_id=1, source_target_pairs={{0,4},{2,6},{4,0},{6,2},{8,12},{10,14},{12,8},{14,10},{16,20},{18,... | collective-permute-start | bytes 46088 | tf_op jit(solution)/shard_map/ppermute | solution.py:48
  24.8 9.1 %collective-permute-start.11 = (f32[32,768]{1,0:T(8,128)S(1)}, f32[32,768]{1,0:T(8,128)S(1)}, u32[]{:S(2)}, u32[]{:S(2)}) collective-permute-start(f32[32,768]{1,0:T(8,128)S(1)} %get-tuple-element.51), channel_id=1, source_target_pairs={{0,24},{2,26},{4,28},{6,30},{8,16},{10,18},{12,20},{14,22},{16,8},... | collective-permute-start | bytes 294920 | tf_op jit(solution)/shard_map/ppermute | solution.py:48
  28.8 9.2 %collective-permute-start.10 = (f32[32,768]{1,0:T(8,128)S(1)}, f32[32,768]{1,0:T(8,128)S(1)}, u32[]{:S(2)}, u32[]{:S(2)}) collective-permute-start(f32[32,768]{1,0:T(8,128)S(1)} %get-tuple-element.51), channel_id=1, source_target_pairs={{0,16},{2,18},{4,20},{6,22},{8,24},{10,26},{12,28},{14,30},{16,0},... | collective-permute-start | bytes 294920 | tf_op jit(solution)/shard_map/ppermute | solution.py:48
  28.8 9.2 %collective-permute-start.9 = (f32[32,768]{1,0:T(8,128)S(1)}, f32[32,768]{1,0:T(8,128)S(1)}, u32[]{:S(2)}, u32[]{:S(2)}) collective-permute-start(f32[32,768]{1,0:T(8,128)S(1)} %get-tuple-element.51), channel_id=1, source_target_pairs={{0,8},{2,10},{4,12},{6,14},{8,0},{10,2},{12,4},{14,6},{16,24},{18,... | collective-permute-start | bytes 294920 | tf_op jit(solution)/shard_map/ppermute | solution.py:48
  29.4 8.6 %collective-permute-start.6 = (f32[10,384]{1,0:T(8,128)S(1)}, f32[10,384]{1,0:T(8,128)S(1)}, u32[]{:S(2)}, u32[]{:S(2)}) collective-permute-start(f32[10,384]{1,0:T(8,128)S(1)} %add_add_fusion.refs_0_), channel_id=1, source_target_pairs={{0,8},{2,10},{4,12},{6,14},{8,0},{10,2},{12,4},{14,6},{16,24},{18,... | collective-permute-start | bytes 46088 | tf_op jit(solution)/shard_map/ppermute | solution.py:48
  30.9 7.3 %collective-permute-start.7 = (f32[10,384]{1,0:T(8,128)S(1)}, f32[10,384]{1,0:T(8,128)S(1)}, u32[]{:S(2)}, u32[]{:S(2)}) collective-permute-start(f32[10,384]{1,0:T(8,128)S(1)} %add_add_fusion.refs_0_), channel_id=1, source_target_pairs={{0,16},{2,18},{4,20},{6,22},{8,24},{10,26},{12,28},{14,30},{16,0},... | collective-permute-start | bytes 46088 | tf_op jit(solution)/shard_map/ppermute | solution.py:48
  33.9 5.6 %collective-permute-start.8 = (f32[10,384]{1,0:T(8,128)S(1)}, f32[10,384]{1,0:T(8,128)S(1)}, u32[]{:S(2)}, u32[]{:S(2)}) collective-permute-start(f32[10,384]{1,0:T(8,128)S(1)} %add_add_fusion.refs_0_), channel_id=1, source_target_pairs={{0,24},{2,26},{4,28},{6,30},{8,16},{10,18},{12,20},{14,22},{16,8},... | collective-permute-start | bytes 46088 | tf_op jit(solution)/shard_map/ppermute | solution.py:48
  39.5 9.4 %collective-permute-start.12 = (f32[4,32,768]{2,1,0:T(8,128)S(1)}, f32[4,32,768]{2,1,0:T(8,128)S(1)}, u32[]{:S(2)}, u32[]{:S(2)}) collective-permute-start(f32[4,32,768]{2,1,0:T(8,128)S(1)} %pad_maximum_fusion.3), channel_id=1, source_target_pairs={{0,2},{1,5},{2,0},{3,7},{4,6},{5,1},{6,4},{7,3},{8,10},{9,13},{10,... | collective-permute-start | bytes 1179656 | tf_op jit(solution)/shard_map/ppermute | solution.py:53
  48.9 1.0 copy-start.12
  48.9 1.0 copy-start.14
  49.9 19.4 %collective-permute-start.13 = (f32[8,48,512]{2,1,0:T(8,128)}, f32[8,48,512]{2,1,0:T(8,128)S(1)}, u32[]{:S(2)}, u32[]{:S(2)}) collective-permute-start(f32[8,48,512]{2,1,0:T(8,128)} %get-tuple-element.65), channel_id=1, source_target_pairs={{0,2},{2,0},{4,6},{6,4},{8,10},{10,8},{12,14},{14,12},{16,18},{18,... | collective-permute-start | bytes 2359304 | tf_op jit(solution)/shard_map/ppermute | solution.py:48
  50.4 20.2 %collective-permute-start.14 = (f32[8,48,512]{2,1,0:T(8,128)}, f32[8,48,512]{2,1,0:T(8,128)}, u32[]{:S(2)}, u32[]{:S(2)}) collective-permute-start(f32[8,48,512]{2,1,0:T(8,128)} %get-tuple-element.67), channel_id=1, source_target_pairs={{0,4},{2,6},{4,0},{6,2},{8,12},{10,14},{12,8},{14,10},{16,20},{18,... | collective-permute-start | bytes 2359304 | tf_op jit(solution)/shard_map/ppermute | solution.py:48
  52.0 20.5 %collective-permute-start.15 = (f32[8,48,512]{2,1,0:T(8,128)}, f32[8,48,512]{2,1,0:T(8,128)}, u32[]{:S(2)}, u32[]{:S(2)}) collective-permute-start(f32[8,48,512]{2,1,0:T(8,128)} %get-tuple-element.69), channel_id=1, source_target_pairs={{0,8},{2,10},{4,12},{6,14},{8,0},{10,2},{12,4},{14,6},{16,24},{18,... | collective-permute-start | bytes 2359304 | tf_op jit(solution)/shard_map/ppermute | solution.py:48
  53.1 23.5 %all-to-all-start = ((f32[16,48,128]{2,1,0:T(8,128)}), f32[16,48,128]{2,1,0:T(8,128)}, u32[]{:S(2)}, u32[]{:S(2)}) async-start(f32[16,48,128]{2,1,0:T(8,128)} %copy-done.7), calls=%async_computation | async-start | bytes 786432 | tf_op jit(solution)/shard_map/all_to_all | solution.py:585
  73.8 0.8 copy-start.17
  74.5 0.8 copy-start.18
  75.3 0.7 copy-start.19
  76.6 10.9 %collective-permute-start.20 = (f32[4,48,512]{2,1,0:T(8,128)}, f32[4,48,512]{2,1,0:T(8,128)}, u32[]{:S(2)}, u32[]{:S(2)}) collective-permute-start(f32[4,48,512]{2,1,0:T(8,128)} %copy-done.19), channel_id=1, source_target_pairs={{0,4},{2,6},{4,0},{6,2},{8,12},{10,14},{12,8},{14,10},{16,20},{18,... | collective-permute-start | bytes 1179656 | tf_op jit(solution)/shard_map/ppermute | solution.py:48
  77.6 13.1 %collective-permute-start.18 = (f32[4,48,512]{2,1,0:T(8,128)}, f32[4,48,512]{2,1,0:T(8,128)}, u32[]{:S(2)}, u32[]{:S(2)}) collective-permute-start(f32[4,48,512]{2,1,0:T(8,128)} %copy-done.18), channel_id=1, source_target_pairs={{0,2},{2,0},{4,6},{6,4},{8,10},{10,8},{12,14},{14,12},{16,18},{18,... | collective-permute-start | bytes 1179656 | tf_op jit(solution)/shard_map/ppermute | solution.py:48
  78.1 15.1 %collective-permute-start.16 = (f32[4,48,512]{2,1,0:T(8,128)}, f32[4,48,512]{2,1,0:T(8,128)}, u32[]{:S(2)}, u32[]{:S(2)}) collective-permute-start(f32[4,48,512]{2,1,0:T(8,128)} %copy-done.17), channel_id=1, source_target_pairs={{0,8},{2,10},{4,12},{6,14},{8,0},{10,2},{12,4},{14,6},{16,24},{18,... | collective-permute-start | bytes 1179656 | tf_op jit(solution)/shard_map/ppermute | solution.py:48
  82.8 27.8 %all-to-all-start.1 = ((f32[16,48,96]{2,1,0:T(8,128)}), f32[16,48,96]{2,1,0:T(8,128)}, u32[]{:S(2)}, u32[]{:S(2)}) async-start(f32[16,48,96]{2,1,0:T(8,128)} %down_gradient.1), calls=%async_computation.1 | async-start | bytes 786432 | tf_op jit(solution)/shard_map/all_to_all | solution.py:617
  87.5 8.2 %copy-start.20 = (f32[2,4,32,768]{3,2,1,0:T(8,128)S(1)}, f32[2,4,32,768]{3,2,1,0:T(8,128)}, u32[]{:S(2)}) copy-start(f32[2,4,32,768]{3,2,1,0:T(8,128)} %pad_maximum_fusion.1) | copy-start | bytes 2359300
  88.7 9.4 %collective-permute-start.21 = (f32[2,48,512]{2,1,0:T(8,128)S(1)}, f32[2,48,512]{2,1,0:T(8,128)S(1)}, u32[]{:S(2)}, u32[]{:S(2)}) collective-permute-start(f32[2,48,512]{2,1,0:T(8,128)S(1)} %slice_add_fusion.1), channel_id=1, source_target_pairs={{0,2},{2,0},{4,6},{6,4},{8,10},{10,8},{12,14},{14,12},{16,18},{18,... | collective-permute-start | bytes 589832 | tf_op jit(solution)/shard_map/ppermute | solution.py:48
  91.7 7.5 %collective-permute-start.19 = (f32[2,48,512]{2,1,0:T(8,128)S(1)}, f32[2,48,512]{2,1,0:T(8,128)S(1)}, u32[]{:S(2)}, u32[]{:S(2)}) collective-permute-start(f32[2,48,512]{2,1,0:T(8,128)S(1)} %slice_add_fusion.5), channel_id=1, source_target_pairs={{0,8},{2,10},{4,12},{6,14},{8,0},{10,2},{12,4},{14,6},{16,24},{18,... | collective-permute-start | bytes 589832 | tf_op jit(solution)/shard_map/ppermute | solution.py:48
  94.2 6.1 %collective-permute-start.17 = (f32[2,48,512]{2,1,0:T(8,128)S(1)}, f32[2,48,512]{2,1,0:T(8,128)S(1)}, u32[]{:S(2)}, u32[]{:S(2)}) collective-permute-start(f32[2,48,512]{2,1,0:T(8,128)S(1)} %slice_add_fusion.9), channel_id=1, source_target_pairs={{0,4},{2,6},{4,0},{6,2},{8,12},{10,14},{12,8},{14,10},{16,20},{18,... | collective-permute-start | bytes 589832 | tf_op jit(solution)/shard_map/ppermute | solution.py:48
  95.7 12.6 %collective-permute-start.22 = (f32[2,4,32,768]{3,2,1,0:T(8,128)S(1)}, f32[2,4,32,768]{3,2,1,0:T(8,128)S(1)}, u32[]{:S(2)}, u32[]{:S(2)}) collective-permute-start(f32[2,4,32,768]{3,2,1,0:T(8,128)S(1)} %copy-done.20), channel_id=1, source_target_pairs={{0,4},{1,3},{2,6},{3,1},{4,0},{5,7},{6,2},{7,5},{8,12},{9,11},{10,... | collective-permute-start | bytes 2359304 | tf_op jit(solution)/shard_map/ppermute | solution.py:53
  102.1 6.4 %copy-start.9 = (s32[10,384]{1,0:T(8,128)S(1)}, s32[10,384]{1,0:T(8,128)}, u32[]{:S(2)}) copy-start(s32[10,384]{1,0:T(8,128)} %copy-done.8) | copy-start | bytes 46084
  102.1 6.4 %copy-start.15 = (f32[10,384]{1,0:T(8,128)S(1)}, f32[10,384]{1,0:T(8,128)}, u32[]{:S(2)}) copy-start(f32[10,384]{1,0:T(8,128)} %copy-done.14) | copy-start | bytes 46084
  102.1 11.6 %collective-permute-start.24 = (f32[1,48,1536]{2,1,0:T(8,128)}, f32[1,48,1536]{2,1,0:T(8,128)S(1)}, u32[]{:S(2)}, u32[]{:S(2)}) collective-permute-start(f32[1,48,1536]{2,1,0:T(8,128)} %slice.92), channel_id=1, source_target_pairs={{0,16},{2,18},{4,20},{6,22},{8,24},{10,26},{12,28},{14,30},{16,0},... | collective-permute-start | bytes 884744 | tf_op jit(solution)/shard_map/ppermute | solution.py:48
  109.7 2.9 %copy-start.10 = (f32[64,768]{1,0:T(8,128)S(1)}, f32[64,768]{1,0:T(8,128)}, u32[]{:S(2)}) copy-start(f32[64,768]{1,0:T(8,128)} %moment_ref.1) | copy-start | bytes 589828
  109.7 2.9 %copy-start.11 = (f32[64,768]{1,0:T(8,128)S(1)}, f32[64,768]{1,0:T(8,128)}, u32[]{:S(2)}) copy-start(f32[64,768]{1,0:T(8,128)} %second_ref.1) | copy-start | bytes 589828
  109.7 2.9 %copy-start.13 = (f32[64,768]{1,0:T(8,128)S(1)}, f32[64,768]{1,0:T(8,128)}, u32[]{:S(2)}) copy-start(f32[64,768]{1,0:T(8,128)} %copy-done.12) | copy-start | bytes 589828
  110.6 3.9 %collective-permute-start.23 = (f32[192,768]{1,0:T(8,128)}, f32[192,768]{1,0:T(8,128)}, u32[]{:S(2)}, u32[]{:S(2)}) collective-permute-start(f32[192,768]{1,0:T(8,128)} %dynamic-slice_bitcast_fusion), channel_id=1, source_target_pairs={{0,1},{1,0},{2,3},{3,2},{4,5},{5,4},{6,7},{7,6},{8,9},{9,8},{10,11... | collective-permute-start | bytes 1769480 | tf_op jit(solution)/shard_map/ppermute | solution.py:48
